TPU v7x, 128 devices: a whole 4x4x4 slice. The times are simulated.
128 devices in a mesh: dp: 8 (over z_hi, x), ctx: 16 (over y, z_lo, core).
Axes of the slice: x: 4, y: 4, z: 4 (z_hi: 2, z_lo: 2; z = z_hi * 2 + z_lo), core: 2. Of those that a mesh axis runs over, the one named last changes fastest.
Arguments:
- loaded_x: bfloat16 [16384, 5120], P(('dp', 'ctx')), may hold values from -6 to 6
- dest_dp: int32 [16384], P(('dp', 'ctx')), may hold values from 0 to 7, as said below
- dest_pos: int32 [16384], P(('dp', 'ctx')), may hold values from 0 to 127, as said below
- queries: bfloat16 [16384, 2560], P(('dp', 'ctx')), may hold values from -500 to 500
- grad_out: bfloat16 [16384, 2560], P(('dp', 'ctx')), may hold values from -6 to 6
- kv_weight: bfloat16 [5120, 1024], replicated, may hold values from -0.078125 to 0.078125
- kv_bias: bfloat16 [1024], replicated, may hold values from -3 to 3
- lengths: int32 [8, 4], replicated, may hold values from 1 to 1536, 2048 in all within a row
Outputs:
- attention_out: bfloat16 [16384, 2560], P(('dp', 'ctx'))
- query_grad: bfloat16 [16384, 2560], P(('dp', 'ctx'))
- kv_weight_grad: float32 [5120, 1024], P(('dp', 'ctx'))
Inputs may be any that keep to these rules, and one draw needn't show every extreme that they name: `dest_dp`: each loader device sends exactly 16 of its rows to each dp index, always to the device with its own ctx index. `dest_pos`: the rows that reach one device take each of its 128 rows exactly once. `lengths`: each row sums to 2048; its largest entry is 1536.
All inputs are finite; a program needn't handle non-finite values.
Results may differ from a plain program's by a relative error of at most 0.034.
The roundings to bfloat16 on the way count: a program that leaves them out, or rounds other values in their place, can miss the bound.
Values may be sent and summed in bfloat16 or wider, within the bound.
No kernel may reach another device: no remote copies, remote signals or barrier semaphores. Data moves between devices by JAX's collectives and lax.ppermute only.
A program may use at most 128 MiB of HBM per device.

v0:
```python
import math

import jax
import jax.numpy as jnp
from jax import lax
from jax.sharding import PartitionSpec as P

HD = 128


masked_score = -1e30
rotary_base = 1000000.0


def rotary(flat_rows, position, head_count, direction):
    row_count = flat_rows.shape[0]
    head_width = flat_rows.shape[1] // head_count
    half_width = head_width // 2
    frequency = jnp.power(
        jnp.float32(rotary_base), -jnp.arange(half_width, dtype=jnp.float32) * (2.0 / head_width)
    )
    angles = position.astype(jnp.float32)[:, None] * frequency[None, :]
    cosine = jnp.cos(angles)[:, None, :]
    sine_part = direction * jnp.sin(angles)[:, None, :]
    shaped = flat_rows.reshape(row_count, head_count, head_width)
    first_half = shaped[..., :half_width]
    second_half = shaped[..., half_width:]
    turned = jnp.concatenate(
        [
            first_half * cosine - second_half * sine_part,
            second_half * cosine + first_half * sine_part,
        ],
        axis=-1,
    )
    return turned.reshape(row_count, head_count * head_width)


def query_heads(flat_rows, head_count, repeat):
    row_count = flat_rows.shape[0]
    head_width = flat_rows.shape[1] // (head_count * repeat)
    shaped = flat_rows.reshape(row_count, head_count, repeat, head_width)
    return shaped.transpose(1, 2, 0, 3).reshape(head_count, repeat * row_count, head_width)


def query_rows(stacked, repeat):
    head_count, stacked_rows, head_width = stacked.shape
    row_count = stacked_rows // repeat
    shaped = stacked.reshape(head_count, repeat, row_count, head_width)
    return shaped.transpose(2, 0, 1, 3).reshape(row_count, head_count * repeat * head_width)


def key_heads(flat_rows, head_count):
    row_count = flat_rows.shape[0]
    return flat_rows.reshape(row_count, head_count, flat_rows.shape[1] // head_count).transpose(
        1, 0, 2
    )


def key_rows(stacked):
    head_count, row_count, head_width = stacked.shape
    return stacked.transpose(1, 0, 2).reshape(row_count, head_count * head_width)


def shards(loaded_x, dest_dp, dest_pos, queries, grad_out, kv_weight, kv_bias, lengths):
    dp_count = lax.axis_size("dp")
    ctx_count = lax.axis_size("ctx")
    local_rows = loaded_x.shape[0]
    kv_width = kv_weight.shape[1] // 2
    head_count = kv_width // HD
    repeat = queries.shape[1] // kv_width
    capacity = local_rows // dp_count
    score_scale = HD ** (-0.5)
    buckets = jnp.arange(dp_count, dtype=jnp.int32)
    one_hot = (dest_dp[:, None] == buckets[None, :]).astype(jnp.int32)
    earlier = jnp.cumsum(one_hot, axis=0) - one_hot
    slot_rank = jnp.sum(earlier * one_hot, axis=1)
    send_order = dest_dp * capacity + slot_rank
    send_rows = jnp.zeros_like(loaded_x).at[send_order].set(loaded_x)
    send_places = jnp.zeros((local_rows,), jnp.int32).at[send_order].set(dest_pos)
    got_rows, got_places = (
        lax.all_to_all(send_rows, "dp", split_axis=0, concat_axis=0, tiled=True),
        lax.all_to_all(send_places, "dp", split_axis=0, concat_axis=0, tiled=True),
    )
    packed = jnp.zeros_like(got_rows).at[got_places].set(got_rows)
    group_rows = local_rows * ctx_count
    my_places = lax.axis_index("ctx") * local_rows + jnp.arange(local_rows, dtype=jnp.int32)
    my_lengths = lax.dynamic_index_in_dim(lengths, lax.axis_index("dp"), 0, keepdims=False)
    seq_ends = jnp.cumsum(my_lengths)
    my_starts = jnp.max(
        jnp.where(seq_ends[None, :] <= my_places[:, None], seq_ends[None, :], 0), axis=1
    )
    position = my_places - my_starts
    projected = jnp.dot(packed, kv_weight, preferred_element_type=jnp.float32) + kv_bias.astype(
        jnp.float32
    )
    rotated_keys = rotary(projected[:, :kv_width], position, head_count, 1.0).astype(jnp.bfloat16)
    value_rows = projected[:, kv_width:].astype(jnp.bfloat16)
    q_stack = query_heads(queries, head_count, repeat)
    g_stack = query_heads(grad_out, head_count, repeat)
    head_width = q_stack.shape[2]
    query_places = jnp.tile(my_places, repeat)
    query_starts = jnp.tile(my_starts, repeat)
    first_start = my_starts[0]
    last_place = my_places[local_rows - 1]

    def scores_for(key_block, key_start):
        block_rows = key_block.shape[0]
        key_places = key_start + jnp.arange(block_rows, dtype=jnp.int32)
        allowed = (key_places[None, :] <= query_places[:, None]) & (
            key_places[None, :] >= query_starts[:, None]
        )
        scores = (
            jnp.einsum(
                "gqd,gkd->gqk",
                q_stack,
                key_heads(key_block, head_count),
                preferred_element_type=jnp.float32,
            )
            * score_scale
        )
        return (scores, allowed)

    def needed(key_start, block_rows):
        return (key_start <= last_place) & (key_start + block_rows > first_start)

    stack_shape = (head_count, repeat * local_rows)
    run_max = jnp.full(stack_shape, masked_score, jnp.float32)
    run_sum = jnp.zeros(stack_shape, jnp.float32)
    key_piece = lax.all_gather(rotated_keys, "ctx", axis=0, tiled=True)
    value_piece = lax.all_gather(value_rows, "ctx", axis=0, tiled=True)
    piece_rows = key_piece.shape[0]
    sub_rows = math.gcd(piece_rows, 512)

    def visit_step(step_index, running):
        key_start = step_index * sub_rows

        def visit_block(state_pair):
            old_max, old_sum = state_pair
            key_block = lax.dynamic_slice_in_dim(key_piece, step_index * sub_rows, sub_rows, 0)
            scores, allowed = scores_for(key_block, key_start)
            masked = jnp.where(allowed[None], scores, masked_score)
            new_max = jnp.maximum(old_max, jnp.max(masked, axis=-1))
            block_total = jnp.sum(
                jnp.where(allowed[None], jnp.exp(masked - new_max[..., None]), 0.0), axis=-1
            )
            return (new_max, old_sum * jnp.exp(old_max - new_max) + block_total)

        return lax.cond(
            needed(key_start, sub_rows), visit_block, lambda state_pair: state_pair, running
        )

    run_max, run_sum = lax.fori_loop(0, piece_rows // sub_rows, visit_step, (run_max, run_sum))
    run_max, run_sum, key_store, value_store = (run_max, run_sum, key_piece, value_piece)
    log_total = run_max + jnp.log(run_sum)
    block_rows = math.gcd(group_rows, 512)
    block_total = group_rows // block_rows

    def output_step(step_index, summed):
        key_start = step_index * block_rows

        def output_add_block(partial_sum):
            key_block = lax.dynamic_slice_in_dim(key_store, key_start, block_rows, 0)
            value_block = lax.dynamic_slice_in_dim(value_store, key_start, block_rows, 0)
            scores, allowed = scores_for(key_block, key_start)
            weights = jnp.where(allowed[None], jnp.exp(scores - log_total[..., None]), 0.0).astype(
                jnp.bfloat16
            )
            return partial_sum + jnp.einsum(
                "gqk,gkd->gqd",
                weights,
                key_heads(value_block, head_count),
                preferred_element_type=jnp.float32,
            )

        return lax.cond(
            needed(key_start, block_rows), output_add_block, lambda partial_sum: partial_sum, summed
        )

    output_sum = lax.fori_loop(
        0,
        block_total,
        output_step,
        jnp.zeros((head_count, repeat * local_rows, head_width), jnp.float32),
    )
    output_stack = output_sum.astype(jnp.bfloat16)
    attention_out = query_rows(output_stack, repeat)
    delta = jnp.sum(g_stack.astype(jnp.float32) * output_stack.astype(jnp.float32), axis=-1)

    def grad_step(step_index, folded):
        key_start = step_index * block_rows

        def grad_add_block(sums_pair):
            query_sum, key_sums = sums_pair
            key_block = lax.dynamic_slice_in_dim(key_store, key_start, block_rows, 0)
            value_block = lax.dynamic_slice_in_dim(value_store, key_start, block_rows, 0)
            key_stack = key_heads(key_block, head_count)
            value_stack = key_heads(value_block, head_count)
            scores, allowed = scores_for(key_block, key_start)
            weights = jnp.where(allowed[None], jnp.exp(scores - log_total[..., None]), 0.0)
            rounded = weights.astype(jnp.bfloat16)
            through = jnp.einsum(
                "gqd,gkd->gqk", g_stack, value_stack, preferred_element_type=jnp.float32
            )
            slopes = (weights * (through - delta[..., None]) * score_scale).astype(jnp.bfloat16)
            query_sum = query_sum + jnp.einsum(
                "gqk,gkd->gqd", slopes, key_stack, preferred_element_type=jnp.float32
            )
            key_part = jnp.einsum(
                "gqk,gqd->gkd", slopes, q_stack, preferred_element_type=jnp.float32
            )
            value_part = jnp.einsum(
                "gqk,gqd->gkd", rounded, g_stack, preferred_element_type=jnp.float32
            )
            block_sums = jnp.concatenate([key_rows(key_part), key_rows(value_part)], axis=1)
            return (query_sum, lax.dynamic_update_slice_in_dim(key_sums, block_sums, key_start, 0))

        return lax.cond(
            needed(key_start, block_rows), grad_add_block, lambda sums_pair: sums_pair, folded
        )

    grad_initial = (
        jnp.zeros((head_count, repeat * local_rows, head_width), jnp.float32),
        jnp.zeros((group_rows, 2 * kv_width), jnp.float32),
    )
    query_sum, key_sums = lax.fori_loop(0, block_total, grad_step, grad_initial)
    query_grad = query_rows(query_sum.astype(jnp.bfloat16), repeat)
    own_sums = lax.psum_scatter(
        key_sums.astype(jnp.bfloat16), "ctx", scatter_dimension=0, tiled=True
    ).astype(jnp.float32)
    key_part = rotary(own_sums[:, :kv_width], position, head_count, -1.0)
    kv_grad = jnp.concatenate([key_part, own_sums[:, kv_width:]], axis=1).astype(jnp.bfloat16)
    grad_scale = (local_rows * dp_count * ctx_count) ** (-0.5)
    contract = (((0,), (0,)), ((), ()))
    summed = lax.psum_scatter(
        lax.dot_general(packed, kv_grad, contract, preferred_element_type=jnp.float32),
        ("dp", "ctx"),
        scatter_dimension=0,
        tiled=True,
    )
    return (attention_out, query_grad, summed * grad_scale)


def solution(mesh):
    placed = (
        P(("dp", "ctx"), None),
        P(("dp", "ctx")),
        P(("dp", "ctx")),
        P(("dp", "ctx"), None),
        P(("dp", "ctx"), None),
        P(),
        P(),
        P(),
    )
    return jax.shard_map(
        shards,
        mesh=mesh,
        in_specs=placed,
        out_specs=(P(("dp", "ctx"), None), P(("dp", "ctx"), None), P(("dp", "ctx"), None)),
        check_vma=False,
    )
```

profile of v0, /device:TPU:0, one launch (start us, length us, event | category | flops | bytes accessed | tf_op | source)
XLA Modules:
  0.0 989.5 jit_solution(3937600028734171048)
XLA Ops:
  11.4 7.7 all-to-all-start
  19.1 4.3 scatter_custom_fusion.1
  23.4 3.3 all-to-all-done
  26.7 3.9 all-to-all-start.1
  33.4 16.7 %all-to-all-done.1 = bf16[8,16,5120]{2,1,0:T(8,128)(2,1)S(1)} async-done(((bf16[8,16,5120]{2,1,0:T(8,128)(2,1)}), bf16[8,16,5120]{2,1,0:T(8,128)(2,1)S(1)}, u32[]{:S(2)}, u32[]{:S(2)}) %all-to-all-start.1) | async-done | bytes 1310752 | tf_op jit(solution)/shard_map/all_to_all | solution.py:81
  50.1 2.7 scatter_custom_fusion.2
  52.8 6.1 convolution_add_fusion.1
  64.8 30.6 %all-gather.3.cloned.1.call-done = bf16[2048,512]{0,1:T(8,128)(2,1)} async-done(((bf16[128,512]{0,1:T(8,128)(2,1)}), bf16[2048,512]{0,1:T(8,128)(2,1)}) %all-gather.3.cloned.1.call-update) | async-done | bytes 2097168 | tf_op jit(solution)/shard_map/all_gather | solution.py:129
  95.4 7.2 while.49
  96.1 4.2 conditional.9
  99.0 1.3 select_reduce_fusion
  103.2 28.4 %all-gather.5.cloned.1.call-done = bf16[2048,512]{1,0:T(8,128)(2,1)} async-done(((bf16[128,512]{1,0:T(8,128)(2,1)}), bf16[2048,512]{1,0:T(8,128)(2,1)}) %all-gather.5.cloned.1.call-update) | async-done | bytes 2097168 | tf_op jit(solution)/shard_map/all_gather | solution.py:130
  131.7 4.0 copy.148
  135.6 1.2 broadcast.248.clone
  136.8 9.8 while.50
  137.5 6.9 conditional.10
  137.9 1.3 constant_dynamic-slice_fusion.1
  139.7 4.7 fusion.24
  146.6 3.2 multiply_reduce_fusion
  149.9 2.5 broadcast_in_dim.90
  152.4 15.4 %while.51 = (s32[]{:T(128)}, f32[4,640,128]{2,1,0:T(8,128)S(1)}, bf16[2048,1024]{0,1:T(8,128)(2,1)}, s32[]{:T(128)}, s32[]{:T(128)S(1)}, /*index=5*/bf16[2048,51...) while((s32[]{:T(128)}, f32[4,640,128]{2,1,0:T(8,128)S(1)}, ...), condition=%wide.region_21.22_spmd.clone, body=%wide.region_18.21_spmd.clone.sunk | while | flops 1695547904 | bytes 42751424 | solution.py:225
  153.2 12.4 %conditional.11 = ((f32[4,640,128]{2,1,0:T(8,128)S(1)}, bf16[2048,1024]{0,1:T(8,128)(2,1)})) conditional(s32[]{:T(128)} %convert_element_type.97, (f32[4,640,128]{2,1,0:T(8,128)S(1)}, bf16[2048,1024]{0,1:T(8,128)(2,1)}) %tuple.154, (s32[]{:T(128)}, s32[128]{0:T(128)S(1)}, s32[128]{0:T(128)S(1)}, bf16[2048,512]{0,1:T(8,128)(2,1)}, ...), branch_computations={%region_19.19_spmd, %region_20.20_spmd} | conditional | flops 1695547904 | bytes 42751132 | solution.py:217
  154.2 1.3 constant_dynamic-slice_fusion.3
  157.3 2.0 fusion.35
  159.3 2.6 fusion.33
  162.9 1.5 convolution_add_fusion
  167.8 6.4 copy.167
  174.3 123.6 %reduce-scatter.7.cloned.1.call-done = bf16[128,1024]{1,0:T(8,128)(2,1)} async-done(((bf16[2048,1024]{1,0:T(8,128)(2,1)}), bf16[128,1024]{1,0:T(8,128)(2,1)}) %reduce-scatter.7.cloned.1.call-update) | async-done | bytes 262160
  300.1 9.0 fusion.51
  312.1 1.1 copy.160
  313.2 668.2 %reduce-scatter.5.cloned.1.call-done = f32[40,1024]{1,0:T(8,128)} async-done(((f32[5120,1024]{1,0:T(8,128)}), f32[40,1024]{1,0:T(8,128)}) %reduce-scatter.5.cloned.1.call-update) | async-done | bytes 163856 | tf_op jit(solution)/shard_map/reduce_scatter | solution.py:234
  981.4 1.6 broadcast_multiply_fusion
  (117 shorter events, 27.1 us)
Async XLA Ops:
  7.2 23.5 %copy-start = (s32[8,4]{0,1:T(4,128)S(1)}, s32[8,4]{0,1:T(4,128)}, u32[]{:S(2)}) copy-start(s32[8,4]{0,1:T(4,128)} %param.27) | copy-start | bytes 388
  7.2 23.8 %copy-start.14 = (bf16[1024]{0:T(1024)(128)(2,1)S(1)}, bf16[1024]{0:T(1024)(128)(2,1)}, u32[]{:S(2)}) copy-start(bf16[1024]{0:T(1024)(128)(2,1)} %param.26) | copy-start | bytes 6148
  11.4 15.3 %all-to-all-start = ((s32[8,16,1]{1,2,0:T(1,128)}), s32[8,16,1]{1,2,0:T(1,128)S(1)}, u32[]{:S(2)}, u32[]{:S(2)}) async-start(s32[8,16,1]{1,2,0:T(1,128)} %bitcast.27), calls=%async_computation | async-start | bytes 8192 | tf_op jit(solution)/shard_map/all_to_all | solution.py:82
  26.7 23.4 %all-to-all-start.1 = ((bf16[8,16,5120]{2,1,0:T(8,128)(2,1)}), bf16[8,16,5120]{2,1,0:T(8,128)(2,1)S(1)}, u32[]{:S(2)}, u32[]{:S(2)}) async-start(bf16[8,16,5120]{2,1,0:T(8,128)(2,1)} %bitcast.29), calls=%async_computation.1 | async-start | bytes 2621440 | tf_op jit(solution)/shard_map/all_to_all | solution.py:81
  30.6 64.8 %all-gather.3.cloned.1.call-start = ((), (), s32[]{:S(2)}) async-start(), calls=%async_computation.4 | async-start | bytes 2228224 | tf_op jit(solution)/shard_map/all_gather | solution.py:129
  32.1 26.9 %copy-start.10 = (f32[128,64]{1,0:T(8,128)}, f32[128,64]{1,0:T(8,128)S(1)}, u32[]{:S(2)}) copy-start(f32[128,64]{1,0:T(8,128)S(1)} %get-tuple-element.982) | copy-start | bytes 98308
  52.8 6.1 copy-start.2
  58.9 3.1 copy-start.7
  59.3 3.7 copy-start.8
  60.4 71.3 %all-gather.5.cloned.1.call-start = ((), (), s32[]{:S(2)}) async-start(), calls=%async_computation.5 | async-start | bytes 2228224 | tf_op jit(solution)/shard_map/all_gather | solution.py:130
  61.1 236.9 %reduce-scatter.7.cloned.1.call-start = ((), (), s32[]{:S(2)}) async-start(), calls=%async_computation.7 | async-start | bytes 4456448
  63.7 31.7 %copy-start.5 = (bf16[4,5,128,128]{3,2,1,0:T(8,128)(2,1)}, bf16[4,5,128,128]{3,2,1,0:T(8,128)(2,1)S(1)}, u32[]{:S(2)}) copy-start(bf16[4,5,128,128]{3,2,1,0:T(8,128)(2,1)S(1)} %copy.151) | copy-start | bytes 1966084
  156.1 1.0 copy-start.4
  156.1 1.2 copy-start.9
  157.3 2.0 copy-start.13
  174.2 125.3 %copy-start.11 = (f32[128,64]{1,0:T(8,128)S(1)}, f32[128,64]{1,0:T(8,128)}, u32[]{:S(2)}) copy-start(f32[128,64]{1,0:T(8,128)} %copy-done.10) | copy-start | bytes 98308
  174.3 125.3 %copy-start.12 = (f32[128,64]{1,0:T(8,128)S(1)}, f32[128,64]{1,0:T(8,128)}, u32[]{:S(2)}) copy-start(f32[128,64]{1,0:T(8,128)} %get-tuple-element.980) | copy-start | bytes 98308
  174.3 125.8 %copy-start.3 = (bf16[128,5120]{1,0:T(8,128)(2,1)S(1)}, bf16[128,5120]{1,0:T(8,128)(2,1)}, u32[]{:S(2)}) copy-start(bf16[128,5120]{1,0:T(8,128)(2,1)} %copy-done.2) | copy-start | bytes 3932164
  174.3 807.1 %reduce-scatter.5.cloned.1.call-start = ((), (), s32[]{:S(2)}) async-start(), calls=%async_computation.6 | async-start | bytes 21135360 | tf_op jit(solution)/shard_map/reduce_scatter | solution.py:234
  309.1 1.1 copy-start.6
  310.5 672.4 %copy-start.1 = (s32[8,4]{0,1:T(4,128)S(1)}, s32[8,4]{0,1:T(4,128)}, u32[]{:S(2)}) copy-start(s32[8,4]{0,1:T(4,128)} %param.27) | copy-start | bytes 388
Sparse Core Ops, SparseCore 0:
  60.5 34.8 all-gather.2
  97.7 33.9 all-gather.4
  174.4 123.5 reduce-scatter.6
  309.2 672.0 reduce-scatter.4
where the time goes:
time: 991 us; the launch traced here: 990 us
  waiting for transfers between devices  871 us (88%)
  local copies, waits for them, and re-layouts  39.8 us (4%)
  matrix products  28.8 us (3%)
  other arithmetic  14.8 us (1%)
  between operations  14.1 us (1%)
  starting transfers between devices  12 us (1%)
    reduce_scatter x1, waiting for transfers between devices, shards(): lax.psum_scatter(lax.dot_general(packed, kv_grad, contract, preferred_ele...  668 us
    unnamed x5, waiting for transfers between devices  124 us
    all_gather x1, waiting for transfers between devices, shards(): key_piece = lax.all_gather(rotated_keys, 'ctx', axis=0, tiled=True)  30.6 us
    all_gather x1, waiting for transfers between devices, shards(): value_piece = lax.all_gather(value_rows, 'ctx', axis=0, tiled=True)  28.4 us
  transfers between devices with their start and end apart: 6, of which 6 were waited for; matrix products, arithmetic and copies ran while one was open for 2% of the time, Pallas kernels for 0%

commit v1 on v0

v1 whole, which is shorter than its diff:
```python
import functools

import jax
import jax.numpy as jnp
import numpy as np
from jax import lax
from jax.experimental import pallas as pl
from jax.experimental.pallas import tpu as pltpu
from jax.sharding import Mesh
from jax.sharding import PartitionSpec as P

D = 5120
HD = 128
HEADS = 4
REP = 5
NSEQ = 4
N_DP = 8
N_Y = 4
N_Q = 4
N_CTX = N_Y * N_Q
ROWS = 128
CAP = ROWS // N_DP
GROUP = N_CTX * ROWS
KVW = HEADS * HD
QH = REP * HD
SHARE = D // (N_DP * N_CTX)
PART = D // N_Q
COLS = 640
CHUNK = 256
N_CHUNK = GROUP // CHUNK
MASKED = -1e30
SCALE = HD**-0.5
LOG2E = 1.4426950408889634
AXES = ("zh", "x", "y", "zl", "c")
DP = ("zh", "x")
Q = ("zl", "c")
bf16 = jnp.bfloat16
f32 = jnp.float32
VMEM_LIMIT = 56 * 1024 * 1024


def iota(shape, axis):
    return lax.broadcasted_iota(jnp.int32, shape, axis)


def dot(a, b):
    return jnp.dot(a, b, preferred_element_type=f32)


def starts_of(places, end_of):
    start = jnp.zeros_like(places)
    for j in range(NSEQ):
        end = end_of(j)
        start = jnp.maximum(start, jnp.where(end <= places, end, 0))
    return start


def project_kernel(where_ref, lengths_ref, dp_ref, pos_ref, freq_ref, bias_ref, x_ref, w_ref,
                   kv_ref, xt_ref, order, total):
    step = pl.program_id(0)

    @pl.when(step == 0)
    def _():
        one_hot = (dp_ref[...] == iota((N_DP, ROWS), 0)).astype(f32)
        before = (iota((ROWS, ROWS), 0) < iota((ROWS, ROWS), 1)).astype(bf16)
        earlier = dot(one_hot.astype(bf16), before)
        rank = jnp.sum(earlier * one_hot, axis=0, keepdims=True).astype(jnp.int32)
        slot = dp_ref[...] * CAP + rank
        order[...] = (iota((ROWS, ROWS), 0) == slot).astype(f32).astype(bf16)
        total[...] = jnp.zeros_like(total)

    rows = dot(order[...], x_ref[...])
    total[...] += dot(rows.astype(bf16), w_ref[...])
    turned = rows.T
    for q in range(N_Q):
        pieces = [
            turned[(j * N_Q + q) * SHARE : (j * N_Q + q + 1) * SHARE] for j in range(COLS // (N_Q * SHARE))
        ]
        xt_ref[q] = jnp.concatenate(pieces, axis=0).astype(bf16)

    @pl.when(step == pl.num_programs(0) - 1)
    def _():
        pos = jnp.sum(order[...].astype(f32) * pos_ref[...].astype(f32), axis=1, keepdims=True)
        pos = jnp.broadcast_to(pos, (ROWS, HD))
        places = pos.astype(jnp.int32) + where_ref[1] * ROWS
        group = iota((ROWS, HD), 0) // CAP
        ends = []
        for b in range(N_DP):
            run = 0
            row = []
            for j in range(NSEQ):
                run = run + lengths_ref[b, j]
                row.append(run)
            ends.append(row)

        def end_of(j):
            end = jnp.zeros((ROWS, HD), jnp.int32)
            for b in range(N_DP):
                end = jnp.where(group == b, ends[b][j], end)
            return end

        angle = (places - starts_of(places, end_of)).astype(f32) * freq_ref[...]
        cosine = jnp.cos(angle)
        sine = jnp.where(iota((ROWS, HD), 1) < HD // 2, -1.0, 1.0) * jnp.sin(angle)
        pos = pos.astype(bf16)
        projected = total[...] + bias_ref[...].astype(f32)
        for g in range(HEADS):
            key = projected[:, g * HD : (g + 1) * HD]
            key = key * cosine + pltpu.roll(key, HD // 2, 1) * sine
            value = projected[:, KVW + g * HD : KVW + (g + 1) * HD]
            packed = jnp.concatenate([key.astype(bf16), value.astype(bf16), pos], axis=1)
            for b in range(N_DP):
                for q in range(N_Q):
                    kv_ref[b, g, q] = packed[b * CAP : (b + 1) * CAP]


def project(where, lengths, dest_dp, dest_pos, freq, bias, x, w):
    smem = pl.BlockSpec(memory_space=pltpu.SMEM)
    whole = lambda *shape: pl.BlockSpec(shape, lambda i: (0,) * len(shape))
    return pl.pallas_call(
        project_kernel,
        grid=(D // COLS,),
        in_specs=[
            smem,
            smem,
            whole(1, ROWS),
            whole(1, ROWS),
            whole(1, HD),
            whole(1, 2 * KVW),
            pl.BlockSpec((ROWS, COLS), lambda i: (0, i)),
            pl.BlockSpec((COLS, 2 * KVW), lambda i: (i, 0)),
        ],
        out_specs=[
            whole(N_DP, HEADS, N_Q, CAP, 3 * HD),
            pl.BlockSpec((N_Q, COLS // N_Q, ROWS), lambda i: (0, i, 0)),
        ],
        out_shape=[
            jax.ShapeDtypeStruct((N_DP, HEADS, N_Q, CAP, 3 * HD), bf16),
            jax.ShapeDtypeStruct((N_Q, PART, ROWS), bf16),
        ],
        scratch_shapes=[pltpu.VMEM((ROWS, ROWS), bf16), pltpu.VMEM((ROWS, 2 * KVW), f32)],
        compiler_params=pltpu.CompilerParams(vmem_limit_bytes=VMEM_LIMIT),
        cost_estimate=pl.CostEstimate(flops=1600000000, bytes_accessed=16000000, transcendentals=0),
        name="project",
    )(where, lengths, dest_dp, dest_pos, freq, bias, x, w)


def attention_kernel(where_ref, lengths_ref, kv_ref, qd_ref, od_ref, dkv_ref, posn_ref,
                     keys, values, keys_t, values_t, places, probs, q_rows, d_rows, q_t, d_t,
                     out_t, dq_t, dk, dv):
    own = where_ref[0]
    q_own = where_ref[2]
    ends = []
    run = 0
    for j in range(NSEQ):
        run = run + lengths_ref[own, j]
        ends.append(run)

    for ctx in range(N_CTX):
        block = kv_ref[:, ctx].reshape(ROWS, 3 * HD)
        rows = slice(ctx * ROWS, (ctx + 1) * ROWS)
        lanes = slice(ctx * ROWS % CHUNK, ctx * ROWS % CHUNK + ROWS)
        key = block[:, :HD]
        value = block[:, HD : 2 * HD]
        keys[rows] = key
        values[rows] = value
        keys_t[ctx * ROWS // CHUNK, :, lanes] = key.astype(f32).T.astype(bf16)
        values_t[ctx * ROWS // CHUNK, :, lanes] = value.astype(f32).T.astype(bf16)
        places[rows] = block[:, 2 * HD :].astype(f32).astype(jnp.int32) + ctx * ROWS
    dk[...] = jnp.zeros_like(dk)
    dv[...] = jnp.zeros_like(dv)

    for y in range(N_Y):
        first = (y * N_Q + q_own) * ROWS
        own_places = places[pl.ds(pl.multiple_of(first, ROWS), ROWS)]
        posn_ref[y] = (own_places - starts_of(own_places, lambda j: ends[j])).astype(f32)
        for h in range(REP):
            lanes = slice(h * HD, (h + 1) * HD)
            query = qd_ref[y, 0, :, lanes]
            cotangent = qd_ref[y, 1, :, lanes]
            q_rows[lanes] = query
            d_rows[lanes] = cotangent
            q_t[:, lanes] = query.astype(f32).T.astype(bf16)
            d_t[:, lanes] = cotangent.astype(f32).T.astype(bf16)
        row_places = first + iota((1, ROWS), 1)
        row_starts = starts_of(row_places, lambda j: ends[j])
        first_start = starts_of(first, lambda j: ends[j])
        low = first_start // CHUNK
        high = (first + ROWS - 1) // CHUNK + 1

        def rows_of(c):
            return pl.ds(pl.multiple_of(c * CHUNK, CHUNK), CHUNK)

        def score(c, top):
            at = rows_of(c)
            key_places = places[at]
            allowed = (key_places <= row_places) & (key_places >= row_starts)
            bias = jnp.where(allowed, 0.0, MASKED)
            s = dot(keys[at], q_t[...]) * (SCALE * LOG2E) + jnp.concatenate([bias] * REP, axis=1)
            probs[at] = s
            return jnp.maximum(top, jnp.max(s, axis=0, keepdims=True))

        top = lax.fori_loop(low, high, score, jnp.full((1, QH), MASKED, f32))
        out_t[...] = jnp.zeros_like(out_t)

        def add_out(c, summed):
            at = rows_of(c)
            p = jnp.exp2(probs[at] - top)
            probs[at] = p
            out_t[...] += dot(values_t[c], p.astype(bf16))
            return summed + jnp.sum(p, axis=0, keepdims=True)

        summed = lax.fori_loop(low, high, add_out, jnp.zeros((1, QH), f32))
        inverse = 1.0 / summed
        rounded = (out_t[...] * inverse).astype(bf16).astype(f32)
        delta = jnp.sum(d_t[...].astype(f32) * rounded, axis=0, keepdims=True)
        for h in range(REP):
            lanes = slice(h * HD, (h + 1) * HD)
            od_ref[y, 0, :, lanes] = rounded[:, lanes].T.astype(bf16)
        dq_t[...] = jnp.zeros_like(dq_t)

        def add_grad(c, carry):
            at = rows_of(c)
            w = probs[at] * inverse
            slope = (w * (dot(values[at], d_t[...]) - delta)).astype(bf16)
            dq_t[...] += dot(keys_t[c], slope)
            dk[at] += dot(slope, q_rows[...])
            dv[at] += dot(w.astype(bf16), d_rows[...])
            return carry

        lax.fori_loop(low, high, add_grad, 0)
        for h in range(REP):
            lanes = slice(h * HD, (h + 1) * HD)
            od_ref[y, 1, :, lanes] = (dq_t[:, lanes] * SCALE).T.astype(bf16)

    for ctx in range(N_CTX):
        rows = slice(ctx * ROWS, (ctx + 1) * ROWS)
        dkv_ref[ctx % N_Q, ctx // N_Q, :, :HD] = (dk[rows] * SCALE).astype(bf16)
        dkv_ref[ctx % N_Q, ctx // N_Q, :, HD:] = dv[rows].astype(bf16)


def attention(where, lengths, kv, qd):
    smem = pl.BlockSpec(memory_space=pltpu.SMEM)
    vmem = pl.BlockSpec(memory_space=pltpu.VMEM)
    return pl.pallas_call(
        attention_kernel,
        in_specs=[smem, smem, vmem, vmem],
        out_specs=[vmem, vmem, vmem],
        out_shape=[
            jax.ShapeDtypeStruct((N_Y, 2, ROWS, QH), bf16),
            jax.ShapeDtypeStruct((N_Q, N_Y, ROWS, 2 * HD), bf16),
            jax.ShapeDtypeStruct((N_Y, ROWS, HD), f32),
        ],
        scratch_shapes=[
            pltpu.VMEM((GROUP, HD), bf16),
            pltpu.VMEM((GROUP, HD), bf16),
            pltpu.VMEM((N_CHUNK, HD, CHUNK), bf16),
            pltpu.VMEM((N_CHUNK, HD, CHUNK), bf16),
            pltpu.VMEM((GROUP, HD), jnp.int32),
            pltpu.VMEM((GROUP, QH), f32),
            pltpu.VMEM((QH, HD), bf16),
            pltpu.VMEM((QH, HD), bf16),
            pltpu.VMEM((HD, QH), bf16),
            pltpu.VMEM((HD, QH), bf16),
            pltpu.VMEM((HD, QH), f32),
            pltpu.VMEM((HD, QH), f32),
            pltpu.VMEM((GROUP, HD), f32),
            pltpu.VMEM((GROUP, HD), f32),
        ],
        compiler_params=pltpu.CompilerParams(vmem_limit_bytes=VMEM_LIMIT),
        cost_estimate=pl.CostEstimate(flops=20000000000, bytes_accessed=8000000, transcendentals=3000000),
        name="attention",
    )(where, lengths, kv, qd)


def key_grad_kernel(parts_ref, cos_ref, sin_ref, out_ref):
    for y in range(N_Y):
        summed = parts_ref[0, y].astype(f32)
        for q in range(1, N_Q):
            summed = summed + parts_ref[q, y].astype(f32)
        key = summed[:, :HD]
        key = key * cos_ref[y] - pltpu.roll(key, HD // 2, 1) * sin_ref[y]
        both = jnp.concatenate([key, summed[:, HD:]], axis=1).astype(bf16)
        for b in range(N_DP):
            for q in range(N_Q):
                out_ref[b, q, y] = both[b * CAP : (b + 1) * CAP]


def key_grad(parts, cosine, sine):
    vmem = pl.BlockSpec(memory_space=pltpu.VMEM)
    return pl.pallas_call(
        key_grad_kernel,
        in_specs=[vmem] * 3,
        out_specs=vmem,
        out_shape=jax.ShapeDtypeStruct((N_DP, N_Q, N_Y, CAP, 2 * HD), bf16),
        compiler_params=pltpu.CompilerParams(vmem_limit_bytes=VMEM_LIMIT),
        name="key_grad",
    )(parts, cosine, sine)


def weight_grad_kernel(xt_ref, kv_ref, out_ref):
    total = None
    for pair in range(N_CTX // 2):
        both = []
        for ctx in (2 * pair, 2 * pair + 1):
            both.append(kv_ref[:, ctx % N_Q, ctx // N_Q].reshape(ROWS, 2 * HD))
        left = jnp.concatenate([xt_ref[2 * pair], xt_ref[2 * pair + 1]], axis=1)
        term = dot(left, jnp.concatenate(both, axis=0))
        total = term if total is None else total + term
    for j in range(out_ref.shape[0]):
        piece = total[j * SHARE : (j + 1) * SHARE]
        out_ref[j] = jnp.concatenate([piece[:, :HD], piece[:, HD:]], axis=0).astype(bf16)


def weight_grad(xt, kv):
    steps = 4
    return pl.pallas_call(
        weight_grad_kernel,
        grid=(steps,),
        in_specs=[
            pl.BlockSpec((N_CTX, PART // steps, ROWS), lambda i: (0, i, 0)),
            pl.BlockSpec((N_DP, N_Q, N_Y, CAP, 2 * HD), lambda i: (0,) * 5),
        ],
        out_specs=pl.BlockSpec((N_DP * N_Y // steps, 2 * SHARE, HD), lambda i: (i, 0, 0)),
        out_shape=jax.ShapeDtypeStruct((N_DP * N_Y, 2 * SHARE, HD), bf16),
        compiler_params=pltpu.CompilerParams(vmem_limit_bytes=VMEM_LIMIT),
        cost_estimate=pl.CostEstimate(flops=1400000000, bytes_accessed=7000000, transcendentals=0),
        name="weight_grad",
    )(xt, kv)


def final_kernel(parts_ref, out_ref):
    for g in range(HEADS):
        summed = parts_ref[0, g].astype(f32)
        for b in range(1, N_DP):
            summed = summed + parts_ref[b, g].astype(f32)
        summed = summed * ((N_DP * GROUP) ** -0.5)
        out_ref[:, g * HD : (g + 1) * HD] = summed[:SHARE]
        out_ref[:, KVW + g * HD : KVW + (g + 1) * HD] = summed[SHARE:]


def final(parts):
    vmem = pl.BlockSpec(memory_space=pltpu.VMEM)
    return pl.pallas_call(
        final_kernel,
        in_specs=[vmem],
        out_specs=vmem,
        out_shape=jax.ShapeDtypeStruct((SHARE, 2 * KVW), f32),
        name="final_sum",
    )(parts)


def swap(array, axes):
    return lax.all_to_all(array, axes, split_axis=0, concat_axis=0, tiled=True)


def shards(loaded_x, dest_dp, dest_pos, queries, grad_out, kv_weight, kv_bias, lengths):
    dp = lax.axis_index(DP)
    y = lax.axis_index("y")
    q = lax.axis_index(Q)
    where = jnp.stack([dp, y * N_Q + q, q]).astype(jnp.int32)
    half = np.power(np.float32(1000000.0), -np.arange(HD // 2, dtype=np.float32) * np.float32(2.0 / HD))
    freq = jnp.asarray(np.concatenate([half, half])[None, :].astype(np.float32))

    qd = jnp.stack([queries, grad_out]).reshape(2, ROWS, HEADS, QH).transpose(2, 0, 1, 3)
    qd = swap(qd, "y")
    kv, xt = project(
        where, lengths, dest_dp.reshape(1, ROWS), dest_pos.reshape(1, ROWS), freq,
        kv_bias.reshape(1, 2 * KVW), loaded_x, kv_weight,
    )
    kv = swap(kv.reshape(N_DP * N_CTX, CAP, 3 * HD), AXES)
    kv, xt = lax.optimization_barrier((kv, xt))
    xt = swap(jnp.broadcast_to(xt[None], (N_Y, N_Q, PART, ROWS)).reshape(N_CTX, PART, ROWS), ("y", "zl", "c"))

    od, dkv, posn = attention(where, lengths, kv.reshape(N_DP, N_CTX, CAP, 3 * HD), qd)
    angle = posn * freq
    cosine = jnp.cos(angle)
    sine = jnp.sin(angle) * jnp.where(jnp.arange(HD) < HD // 2, -1.0, 1.0).astype(f32)
    dkv = swap(dkv, Q)
    od = swap(od, "y")
    kv_grad = key_grad(dkv, cosine, sine)
    kv_grad = swap(kv_grad.reshape(N_DP * N_Q, N_Y * CAP, 2 * HD), ("zh", "x", "zl", "c"))
    dw = weight_grad(xt, kv_grad.reshape(N_DP, N_Q, N_Y, CAP, 2 * HD))
    dw = swap(dw, ("zh", "x", "y"))
    kv_weight_grad = final(dw.reshape(N_DP, HEADS, 2 * SHARE, HD))
    od = od.transpose(1, 2, 0, 3).reshape(2, ROWS, HEADS * QH)
    return od[0], od[1], kv_weight_grad


def solution(mesh):
    split = Mesh(mesh.devices.reshape(2, 4, N_Y, 2, 2), AXES)
    rows = P(AXES, None)
    return jax.shard_map(
        shards,
        mesh=split,
        in_specs=(rows, P(AXES), P(AXES), rows, rows, P(), P(), P()),
        out_specs=(rows, rows, rows),
        check_vma=False,
    )
```

time: 991 us -> 249 us (0.25)
  waiting for transfers between devices: 871 us -> 74.2 us
  blocking collectives: 0 us -> 87.7 us
  Pallas kernels: 0 us -> 43.6 us
  matrix products: 28.8 us -> 0 us
  local copies, waits for them, and re-layouts: 39.8 us -> 12.5 us
  starting transfers between devices: 12 us -> 25.8 us
  between operations: 14.1 us -> 0.78 us
  other arithmetic: 14.8 us -> 3.51 us
    reduce_scatter x1 -> x0, waiting for transfers between devices: 668 us -> none  [shards(): lax.psum_scatter(lax.dot_general(packed, kv_grad, contract, preferred_ele...]
    unnamed x5 -> x0, waiting for transfers between devices: 124 us -> none
    all_to_all x0 -> x2, blocking collectives: none -> 87.7 us  [swap(): return lax.all_to_all(array, axes, split_axis=0, concat_axis=0, tiled=True)]
    all_gather x2 -> x0, waiting for transfers between devices: 59 us -> none  [the longest x1 30.6 us: shards(): key_piece = lax.all_gather(rotated_keys, 'ctx', axis=0, tiled=True)]
    all_to_all x2 -> x5, waiting for transfers between devices: 20 us -> 74.2 us  [swap(): return lax.all_to_all(array, axes, split_axis=0, concat_axis=0, tiled=True)]
    pallas_call x0 -> x5, Pallas kernels: none -> 43.6 us  [the longest x1 23.2 us: attention(): pl.pallas_call(attention_kernel, in_specs=[smem, smem, vmem, vmem], out_s...]
    dot_general x9 -> x0, matrix products: 28.8 us -> none  [the longest x1 9.03 us: shards(): lax.dot_general(packed, kv_grad, contract, preferred_element_type=jnp.flo...]
    all_to_all x2 -> x5, starting transfers between devices: 11.6 us -> 25.8 us  [swap(): return lax.all_to_all(array, axes, split_axis=0, concat_axis=0, tiled=True)]
  transfers between devices with their start and end apart: 6 -> 5, of which waited for: 6 -> 5; matrix products, arithmetic and copies ran while one was open for 2% -> 3% of each run, Pallas kernels for 0% -> 2%
where the time goes in v1:
time: 249 us; the launch traced here: 248 us
  blocking collectives  87.7 us (35%)
  waiting for transfers between devices  74.2 us (30%)
  Pallas kernels  43.6 us (18%)
  starting transfers between devices  25.8 us (10%)
  local copies, waits for them, and re-layouts  12.5 us (5%)
  other arithmetic  3.51 us (1%)
    all_to_all x2, blocking collectives, swap(): return lax.all_to_all(array, axes, split_axis=0, concat_axis=0, tiled=True)  87.7 us
    all_to_all x5, waiting for transfers between devices, swap(): return lax.all_to_all(array, axes, split_axis=0, concat_axis=0, tiled=True)  74.2 us
    all_to_all x5, starting transfers between devices, swap(): return lax.all_to_all(array, axes, split_axis=0, concat_axis=0, tiled=True)  25.8 us
    pallas_call x1, Pallas kernels, attention(): pl.pallas_call(attention_kernel, in_specs=[smem, smem, vmem, vmem], out_s...  23.2 us
    pallas_call x1, Pallas kernels, project(): pl.pallas_call(project_kernel, grid=(D // COLS,), in_specs=[smem, smem, w...  10.5 us
    unnamed x23, local copies, waits for them, and re-layouts  8.72 us
    pallas_call x1, Pallas kernels, weight_grad(): pl.pallas_call(weight_grad_kernel, grid=(steps,), in_specs=[pl.BlockSpec(...  5.4 us
  transfers between devices with their start and end apart: 5, of which 5 were waited for; matrix products, arithmetic and copies ran while one was open for 3% of the time, Pallas kernels for 2%

profile of v1, /device:TPU:0, one launch (start us, length us, event | category | flops | bytes accessed | tf_op | source)
XLA Modules:
  0.0 248.0 jit_solution(15910794671518319309)
XLA Ops:
  0.6 1.3 copy.19.lengths_ref
  2.0 1.3 reshape.52.bias_ref
  3.3 0.6 pad_add_fusion.where_ref
  3.9 10.5 %project.1 = (bf16[8,4,4,16,384]{4,3,2,1,0:T(8,128)(2,1)}, bf16[4,1280,128]{2,1,0:T(8,128)(2,1)}) custom-call(s32[3]{0:T(128)} %pad_add_fusion.where_ref, s32[8,4]{1,0:T(8,128)} %copy.19.lengths_ref, s32[1,128]{1,0:T(1,128)} %bitcast.29, s32[1,128]{1,0:T(1,128)} %bitcast.30, f32[1,128]{1,0:T(1,128)} %constant.31.clone.freq_ref, ...), custom_call_target="tpu_custom_call" | custom-call | flops 1600000000 | bytes 16000000 | tf_op jit(solution)/shard_map/project/pallas_call | solution.py:120
  14.4 11.2 %all-to-all-start = ((bf16[128,16,384]{2,1,0:T(8,128)(2,1)}), bf16[128,16,384]{2,1,0:T(8,128)(2,1)S(1)}, u32[]{:S(2)}, u32[]{:S(2)}) async-start(bf16[128,16,384]{2,1,0:T(8,128)(2,1)} %bitcast.28), calls=%async_computation | async-start | bytes 3145728 | tf_op jit(solution)/shard_map/all_to_all | solution.py:354
  26.2 0.4 copy-done.6
  27.3 1.2 maximum_bitcast_fusion
  28.5 21.6 %all-to-all-done = bf16[128,16,384]{2,1,0:T(8,128)(2,1)S(1)} async-done(((bf16[128,16,384]{2,1,0:T(8,128)(2,1)}), bf16[128,16,384]{2,1,0:T(8,128)(2,1)S(1)}, u32[]{:S(2)}, u32[]{:S(2)}) %all-to-all-start) | async-done | bytes 1572896 | tf_op jit(solution)/shard_map/all_to_all | solution.py:354
  50.1 1.2 copy-done.2
  51.3 3.5 %all-to-all-start.1 = ((bf16[4,2,128,640]{3,2,1,0:T(8,128)(2,1)}), bf16[4,2,128,640]{3,2,1,0:T(8,128)(2,1)S(1)}, u32[]{:S(2)}, u32[]{:S(2)}) async-start(bf16[4,2,128,640]{3,2,1,0:T(8,128)(2,1)} %maximum_bitcast_fusion), calls=%async_computation.1 | async-start | bytes 2621440 | tf_op jit(solution)/shard_map/all_to_all | solution.py:354
  54.8 17.8 %all-to-all-done.1.qd_ref = bf16[4,2,128,640]{3,2,1,0:T(8,128)(2,1)S(1)} async-done(((bf16[4,2,128,640]{3,2,1,0:T(8,128)(2,1)}), bf16[4,2,128,640]{3,2,1,0:T(8,128)(2,1)S(1)}, u32[]{:S(2)}, u32[]{:S(2)}) %all-to-all-start.1) | async-done | bytes 1310752 | tf_op jit(solution)/shard_map/all_to_all | solution.py:354
  72.6 1.1 copy-done.3
  73.7 23.2 %attention.1 = (bf16[4,2,128,640]{3,2,1,0:T(8,128)(2,1)}, bf16[4,4,128,256]{3,2,1,0:T(8,128)(2,1)}, f32[4,128,128]{2,1,0:T(8,128)}) custom-call(s32[3]{0:T(128)} %pad_add_fusion.where_ref, s32[8,4]{1,0:T(8,128)} %copy.19.lengths_ref, bf16[8,16,16,384]{3,2,1,0:T(8,128)(2,1)} %bitcast.27, bf16[4,2,128,640]{3,2,1,0:T(8,128)(2,1)} %copy-done.3), custom_call_target="tpu_custom_call" | custom-call | flops 20000000000 | bytes 8000000 | tf_op jit(solution)/shard_map/attention/pallas_call | solution.py:245
  96.9 3.6 %all-to-all-start.4 = ((bf16[4,4,128,256]{3,2,1,0:T(8,128)(2,1)}), bf16[4,4,128,256]{3,2,1,0:T(8,128)(2,1)S(1)}, u32[]{:S(2)}, u32[]{:S(2)}) async-start(bf16[4,4,128,256]{3,2,1,0:T(8,128)(2,1)} %get-tuple-element.15), calls=%async_computation.4 | async-start | bytes 2097152 | tf_op jit(solution)/shard_map/all_to_all | solution.py:354
  100.6 1.7 sine_multiply_fusion
  102.3 12.7 %all-to-all-done.4.parts_ref = bf16[4,4,128,256]{3,2,1,0:T(8,128)(2,1)S(1)} async-done(((bf16[4,4,128,256]{3,2,1,0:T(8,128)(2,1)}), bf16[4,4,128,256]{3,2,1,0:T(8,128)(2,1)S(1)}, u32[]{:S(2)}, u32[]{:S(2)}) %all-to-all-start.4) | async-done | bytes 1048608 | tf_op jit(solution)/shard_map/all_to_all | solution.py:354
  115.0 1.0 copy-done
  116.0 2.5 %key_grad.1 = bf16[8,4,4,16,256]{4,3,2,1,0:T(8,128)(2,1)} custom-call(bf16[4,4,128,256]{3,2,1,0:T(8,128)(2,1)} %copy-done, f32[4,128,128]{2,1,0:T(8,128)} %get-tuple-element.23.cos_ref, f32[4,128,128]{2,1,0:T(8,128)} %get-tuple-element.22.sin_ref), custom_call_target="tpu_custom_call" | custom-call | tf_op jit(solution)/shard_map/key_grad/pallas_call | solution.py:291
  118.6 22.9 %all_to_all.35 = bf16[32,64,256]{2,1,0:T(8,128)(2,1)} all-to-all(bf16[32,64,256]{2,1,0:T(8,128)(2,1)} %bitcast.20), channel_id=1, replica_groups=mesh['zh'=2,'x'=4,'y'=4,'zl'=2,'c'=2] {'zh','x','zl','c'}, dimensions={0} | all-to-all | bytes 2097152 | tf_op jit(solution)/shard_map/all_to_all | solution.py:354
  141.4 1.1 broadcast_in_dim.16
  142.5 64.8 %all_to_all.36.xt_ref = bf16[16,1280,128]{2,1,0:T(8,128)(2,1)} all-to-all(bf16[16,1280,128]{2,1,0:T(8,128)(2,1)S(1)} %bitcast.18), channel_id=1, replica_groups=mesh['zh'=2,'x'=4,'y'=4,'zl'=2,'c'=2] {'y','zl','c'}, dimensions={0} | all-to-all | bytes 10485760 | tf_op jit(solution)/shard_map/all_to_all | solution.py:354
  207.3 3.5 %all-to-all-start.2 = ((bf16[4,2,128,640]{3,2,1,0:T(8,128)(2,1)}), bf16[4,2,128,640]{3,2,1,0:T(8,128)(2,1)S(1)}, u32[]{:S(2)}, u32[]{:S(2)}) async-start(bf16[4,2,128,640]{3,2,1,0:T(8,128)(2,1)} %get-tuple-element.13), calls=%async_computation.2 | async-start | bytes 2621440 | tf_op jit(solution)/shard_map/all_to_all | solution.py:354
  210.9 5.4 %weight_grad.1 = bf16[32,80,128]{2,1,0:T(8,128)(2,1)} custom-call(bf16[16,1280,128]{2,1,0:T(8,128)(2,1)} %all_to_all.36.xt_ref, bf16[8,4,4,16,256]{4,3,2,1,0:T(8,128)(2,1)} %bitcast.21), custom_call_target="tpu_custom_call" | custom-call | flops 1400000000 | bytes 7000000 | tf_op jit(solution)/shard_map/weight_grad/pallas_call | solution.py:317
  216.3 12.1 %all-to-all-done.2 = bf16[4,2,128,640]{3,2,1,0:T(8,128)(2,1)S(1)} async-done(((bf16[4,2,128,640]{3,2,1,0:T(8,128)(2,1)}), bf16[4,2,128,640]{3,2,1,0:T(8,128)(2,1)S(1)}, u32[]{:S(2)}, u32[]{:S(2)}) %all-to-all-start.2) | async-done | bytes 1310752 | tf_op jit(solution)/shard_map/all_to_all | solution.py:354
  228.3 3.9 %all-to-all-start.6 = ((bf16[32,80,128]{2,1,0:T(8,128)(2,1)}), bf16[32,80,128]{2,1,0:T(8,128)(2,1)S(1)}, u32[]{:S(2)}, u32[]{:S(2)}) async-start(bf16[32,80,128]{2,1,0:T(8,128)(2,1)} %weight_grad.1), calls=%async_computation.6 | async-start | bytes 1310720 | tf_op jit(solution)/shard_map/all_to_all | solution.py:354
  232.4 0.3 copy.21
  232.7 1.1 copy.23
  233.8 0.3 copy.20
  234.1 1.1 copy.22
  235.2 10.0 %all-to-all-done.6 = bf16[32,80,128]{2,1,0:T(8,128)(2,1)S(1)} async-done(((bf16[32,80,128]{2,1,0:T(8,128)(2,1)}), bf16[32,80,128]{2,1,0:T(8,128)(2,1)S(1)}, u32[]{:S(2)}, u32[]{:S(2)}) %all-to-all-start.6) | async-done | bytes 655392 | tf_op jit(solution)/shard_map/all_to_all | solution.py:354
  245.3 0.9 copy-done.1
  246.1 1.8 final_sum.1
  (19 shorter events, 1.4 us)
Async XLA Ops:
  14.4 11.2 %copy-start.5 = (bf16[128,2560]{1,0:T(8,128)(2,1)S(1)}, bf16[128,2560]{1,0:T(8,128)(2,1)}, u32[]{:S(2)}) copy-start(bf16[128,2560]{1,0:T(8,128)(2,1)} %param.12) | copy-start | bytes 1966084
  14.4 35.7 %all-to-all-start = ((bf16[128,16,384]{2,1,0:T(8,128)(2,1)}), bf16[128,16,384]{2,1,0:T(8,128)(2,1)S(1)}, u32[]{:S(2)}, u32[]{:S(2)}) async-start(bf16[128,16,384]{2,1,0:T(8,128)(2,1)} %bitcast.28), calls=%async_computation | async-start | bytes 3145728 | tf_op jit(solution)/shard_map/all_to_all | solution.py:354
  25.6 1.1 copy-start.6
  50.1 1.2 copy-start.2
  51.3 21.4 %all-to-all-start.1 = ((bf16[4,2,128,640]{3,2,1,0:T(8,128)(2,1)}), bf16[4,2,128,640]{3,2,1,0:T(8,128)(2,1)S(1)}, u32[]{:S(2)}, u32[]{:S(2)}) async-start(bf16[4,2,128,640]{3,2,1,0:T(8,128)(2,1)} %maximum_bitcast_fusion), calls=%async_computation.1 | async-start | bytes 2621440 | tf_op jit(solution)/shard_map/all_to_all | solution.py:354
  72.6 1.1 copy-start.3
  96.9 3.7 %copy-start.7 = (f32[4,128,128]{2,1,0:T(8,128)S(1)}, f32[4,128,128]{2,1,0:T(8,128)}, u32[]{:S(2)}) copy-start(f32[4,128,128]{2,1,0:T(8,128)} %get-tuple-element.16) | copy-start | bytes 786436
  96.9 3.7 %copy-start.8 = (f32[128]{0:T(128)S(1)}, f32[128]{0:T(128)}, u32[]{:S(2)}) copy-start(f32[128]{0:T(128)} %constant.32) | copy-start | bytes 1540
  96.9 18.1 %all-to-all-start.4 = ((bf16[4,4,128,256]{3,2,1,0:T(8,128)(2,1)}), bf16[4,4,128,256]{3,2,1,0:T(8,128)(2,1)S(1)}, u32[]{:S(2)}, u32[]{:S(2)}) async-start(bf16[4,4,128,256]{3,2,1,0:T(8,128)(2,1)} %get-tuple-element.15), calls=%async_computation.4 | async-start | bytes 2097152 | tf_op jit(solution)/shard_map/all_to_all | solution.py:354
  115.0 1.0 copy-start
  118.6 22.9 %copy-start.4 = (bf16[4,1280,128]{2,1,0:T(8,128)(2,1)S(1)}, bf16[4,1280,128]{2,1,0:T(8,128)(2,1)}, u32[]{:S(2)}) copy-start(bf16[4,1280,128]{2,1,0:T(8,128)(2,1)} %get-tuple-element.14) | copy-start | bytes 3932164
  207.3 21.0 %all-to-all-start.2 = ((bf16[4,2,128,640]{3,2,1,0:T(8,128)(2,1)}), bf16[4,2,128,640]{3,2,1,0:T(8,128)(2,1)S(1)}, u32[]{:S(2)}, u32[]{:S(2)}) async-start(bf16[4,2,128,640]{3,2,1,0:T(8,128)(2,1)} %get-tuple-element.13), calls=%async_computation.2 | async-start | bytes 2621440 | tf_op jit(solution)/shard_map/all_to_all | solution.py:354
  228.3 16.9 %all-to-all-start.6 = ((bf16[32,80,128]{2,1,0:T(8,128)(2,1)}), bf16[32,80,128]{2,1,0:T(8,128)(2,1)S(1)}, u32[]{:S(2)}, u32[]{:S(2)}) async-start(bf16[32,80,128]{2,1,0:T(8,128)(2,1)} %weight_grad.1), calls=%async_computation.6 | async-start | bytes 1310720 | tf_op jit(solution)/shard_map/all_to_all | solution.py:354
  245.2 0.9 copy-start.1

commit v2 on v1

v2 whole, which is shorter than its diff:
```python
import functools

import jax
import jax.numpy as jnp
import numpy as np
from jax import lax
from jax.experimental import pallas as pl
from jax.experimental.pallas import tpu as pltpu
from jax.sharding import Mesh
from jax.sharding import PartitionSpec as P

D = 5120
HD = 128
HEADS = 4
REP = 5
NSEQ = 4
N_DP = 8
N_Y = 4
N_Q = 4
N_CTX = N_Y * N_Q
ROWS = 128
CAP = ROWS // N_DP
GROUP = N_CTX * ROWS
KVW = HEADS * HD
QH = REP * HD
SHARE = D // (N_DP * N_CTX)
PART = D // N_Q
COLS = 640
TURN = 1280
CHUNK = 256
N_CHUNK = GROUP // CHUNK
MASKED = -1e30
SCALE = HD**-0.5
LOG2E = 1.4426950408889634
AXES = ("zh", "x", "y", "zl", "c")
DP = ("zh", "x")
Q = ("zl", "c")
bf16 = jnp.bfloat16
f32 = jnp.float32
VMEM_LIMIT = 56 * 1024 * 1024


def iota(shape, axis):
    return lax.broadcasted_iota(jnp.int32, shape, axis)


def dot(a, b):
    return jnp.dot(a, b, preferred_element_type=f32)


def starts_of(places, end_of):
    start = jnp.zeros_like(places)
    for j in range(NSEQ):
        end = end_of(j)
        start = jnp.maximum(start, jnp.where(end <= places, end, 0))
    return start


def coordinates():
    dp = lax.axis_index("zh") * 4 + lax.axis_index("x")
    return dp, lax.axis_index("y"), lax.axis_index("zl") * 2 + lax.axis_index("c")


def order_of(dp_row):
    one_hot = (dp_row == iota((N_DP, ROWS), 0)).astype(f32)
    before = (iota((ROWS, ROWS), 0) < iota((ROWS, ROWS), 1)).astype(bf16)
    earlier = dot(one_hot.astype(bf16), before)
    rank = jnp.sum(earlier * one_hot, axis=0, keepdims=True).astype(jnp.int32)
    slot = dp_row * CAP + rank
    return (iota((ROWS, ROWS), 0) == slot).astype(f32).astype(bf16)


def split_kernel(q_ref, d_ref, *out_refs):
    y = lax.axis_index("y")
    for s in range(N_Y):
        lanes = pl.ds(pl.multiple_of(lax.rem(y + s, N_Y) * QH, HD), QH)
        out_refs[s][0] = q_ref[:, lanes]
        out_refs[s][1] = d_ref[:, lanes]


def split_heads(queries, grad_out):
    vmem = pl.BlockSpec(memory_space=pltpu.VMEM)
    return pl.pallas_call(
        split_kernel,
        in_specs=[vmem] * 2,
        out_specs=[vmem] * N_Y,
        out_shape=[jax.ShapeDtypeStruct((2, ROWS, QH), bf16)] * N_Y,
        name="split_heads",
    )(queries, grad_out)


def merge_kernel(*refs):
    y = lax.axis_index("y")
    out_ref, dq_ref = refs[N_Y:]
    for s in range(N_Y):
        lanes = pl.ds(pl.multiple_of(lax.rem(y + s, N_Y) * QH, HD), QH)
        out_ref[:, lanes] = refs[s][0]
        dq_ref[:, lanes] = refs[s][1]


def merge_heads(pieces):
    vmem = pl.BlockSpec(memory_space=pltpu.VMEM)
    return pl.pallas_call(
        merge_kernel,
        in_specs=[vmem] * N_Y,
        out_specs=[vmem] * 2,
        out_shape=[jax.ShapeDtypeStruct((ROWS, HEADS * QH), bf16)] * 2,
        name="merge_heads",
    )(*pieces)


def project_kernel(lengths_ref, dp_ref, pos_ref, freq_ref, bias_ref, x_ref, w_ref, kv_ref, total):
    step = pl.program_id(0)

    @pl.when(step == 0)
    def _():
        total[...] = jnp.zeros_like(total)

    total[...] += dot(x_ref[...], w_ref[...])

    @pl.when(step == pl.num_programs(0) - 1)
    def _():
        _, y, q = coordinates()

        def column(row):
            diagonal = iota((ROWS, ROWS), 0) == iota((ROWS, ROWS), 1)
            picked = jnp.sum(jnp.where(diagonal, row.astype(f32), 0.0), axis=1, keepdims=True)
            return jnp.broadcast_to(picked, (ROWS, HD)).astype(jnp.int32)

        group = column(dp_ref[...])
        pos = column(pos_ref[...])
        places = pos + (y * N_Q + q) * ROWS
        ends = jnp.zeros((N_DP, 1), jnp.int32)
        columns = []
        for j in range(NSEQ):
            ends = ends + lengths_ref[:, j : j + 1]
            columns.append(ends)

        def end_of(j):
            end = jnp.zeros((ROWS, HD), jnp.int32)
            for b in range(N_DP):
                end = jnp.where(group == b, columns[j][b : b + 1], end)
            return end

        angle = (places - starts_of(places, end_of)).astype(f32) * freq_ref[...]
        cosine = jnp.cos(angle)
        sine = jnp.where(iota((ROWS, HD), 1) < HD // 2, -1.0, 1.0) * jnp.sin(angle)
        order = order_of(dp_ref[...])
        bias = bias_ref[...].reshape(1, 2 * KVW).astype(f32)
        pos = pos.astype(f32).astype(bf16)
        for g in range(HEADS):
            lanes = slice(g * HD, (g + 1) * HD)
            key = total[:, lanes] + bias[:, lanes]
            key = key * cosine + pltpu.roll(key, HD // 2, 1) * sine
            lanes = slice(KVW + g * HD, KVW + (g + 1) * HD)
            value = total[:, lanes] + bias[:, lanes]
            packed = jnp.concatenate([key.astype(bf16), value.astype(bf16), pos], axis=1)
            packed = dot(order, packed).astype(bf16)
            for b in range(N_DP):
                for z in range(2):
                    kv_ref[b, g, z] = packed[b * CAP : (b + 1) * CAP]


def project(lengths, dest_dp, dest_pos, freq, bias, x, w):
    whole = lambda *shape: pl.BlockSpec(shape, lambda i: (0,) * len(shape))
    return pl.pallas_call(
        project_kernel,
        grid=(D // COLS,),
        in_specs=[
            whole(N_DP, NSEQ),
            whole(1, ROWS),
            whole(1, ROWS),
            whole(1, HD),
            whole(2 * KVW),
            pl.BlockSpec((ROWS, COLS), lambda i: (0, i)),
            pl.BlockSpec((COLS, 2 * KVW), lambda i: (i, 0)),
        ],
        out_specs=whole(N_DP, HEADS, 2, CAP, 3 * HD),
        out_shape=jax.ShapeDtypeStruct((N_DP, HEADS, 2, CAP, 3 * HD), bf16),
        scratch_shapes=[pltpu.VMEM((ROWS, 2 * KVW), f32)],
        compiler_params=pltpu.CompilerParams(vmem_limit_bytes=VMEM_LIMIT),
        cost_estimate=pl.CostEstimate(flops=1600000000, bytes_accessed=16000000, transcendentals=0),
        name="project",
    )(lengths, dest_dp, dest_pos, freq, bias, x, w)


def turn_kernel(dp_ref, x_ref, *refs):
    out_refs, order, pieces = refs[:N_Q], refs[N_Q], refs[N_Q + 1]
    own = coordinates()[2]

    @pl.when(pl.program_id(0) == 0)
    def _():
        order[...] = order_of(dp_ref[...])

    turned = dot(order[...], x_ref[...]).T
    for q in range(N_Q):
        rows = [turned[(j * N_Q + q) * SHARE : (j * N_Q + q + 1) * SHARE] for j in range(TURN // (N_Q * SHARE))]
        pieces[q] = jnp.concatenate(rows, axis=0).astype(bf16)
    for m in range(N_Q):
        out_refs[m][...] = pieces[own ^ m]


def turn(dest_dp, x):
    return pl.pallas_call(
        turn_kernel,
        grid=(D // TURN,),
        in_specs=[
            pl.BlockSpec((1, ROWS), lambda i: (0, 0)),
            pl.BlockSpec((ROWS, TURN), lambda i: (0, i)),
        ],
        out_specs=[pl.BlockSpec((TURN // N_Q, ROWS), lambda i: (i, 0))] * N_Q,
        out_shape=[jax.ShapeDtypeStruct((PART, ROWS), bf16)] * N_Q,
        scratch_shapes=[pltpu.VMEM((ROWS, ROWS), bf16), pltpu.VMEM((N_Q, TURN // N_Q, ROWS), bf16)],
        compiler_params=pltpu.CompilerParams(vmem_limit_bytes=VMEM_LIMIT),
        cost_estimate=pl.CostEstimate(flops=2000000000, bytes_accessed=2600000, transcendentals=0),
        name="turn",
    )(dest_dp, x)


def attention_kernel(lengths_ref, kv_own_ref, kv_other_ref, *refs):
    qd_refs, od_refs, dkv_refs = refs[:N_Y], refs[N_Y : 2 * N_Y], refs[2 * N_Y : 2 * N_Y + N_Q]
    posn_ref = refs[2 * N_Y + N_Q]
    (keys, values, keys_t, values_t, places, probs, q_rows, d_rows, q_t, d_t,
                     out_t, dq_t, dk, dv) = refs[2 * N_Y + N_Q + 1 :]
    own, y_own, q_own = coordinates()
    ends = []
    for j in range(NSEQ):
        counted = (iota((N_DP, NSEQ), 0) == own) & (iota((N_DP, NSEQ), 1) <= j)
        ends.append(jnp.sum(jnp.where(counted, lengths_ref[...], 0).astype(f32)).astype(jnp.int32))

    core = q_own % 2
    for kv_ref, c in ((kv_own_ref, core), (kv_other_ref, 1 - core)):
        for chunk in range(N_CHUNK):
            block = kv_ref[:, chunk // 2, chunk % 2].reshape(ROWS, 3 * HD)
            first = pl.multiple_of(chunk * CHUNK + c * ROWS, ROWS)
            rows = pl.ds(first, ROWS)
            lanes = pl.ds(pl.multiple_of(c * ROWS, ROWS), ROWS)
            key = block[:, :HD]
            value = block[:, HD : 2 * HD]
            keys[rows] = key
            values[rows] = value
            keys_t[chunk, :, lanes] = key.astype(f32).T.astype(bf16)
            values_t[chunk, :, lanes] = value.astype(f32).T.astype(bf16)
            places[rows] = block[:, 2 * HD :].astype(f32).astype(jnp.int32) + first
    dk[...] = jnp.zeros_like(dk)
    dv[...] = jnp.zeros_like(dv)

    for s in range(N_Y):
        qd_ref, od_ref = qd_refs[s], od_refs[s]
        own_places = places[pl.ds(pl.multiple_of((s * N_Q + q_own) * ROWS, ROWS), ROWS)]
        first = (lax.rem(y_own + N_Y - s, N_Y) * N_Q + q_own) * ROWS
        posn_ref[s] = (own_places - starts_of(own_places, lambda j: ends[j])).astype(f32)
        for h in range(REP):
            lanes = slice(h * HD, (h + 1) * HD)
            query = qd_ref[0, :, lanes]
            cotangent = qd_ref[1, :, lanes]
            q_rows[lanes] = query
            d_rows[lanes] = cotangent
            q_t[:, lanes] = query.astype(f32).T.astype(bf16)
            d_t[:, lanes] = cotangent.astype(f32).T.astype(bf16)
        row_places = first + iota((1, ROWS), 1)
        row_starts = starts_of(row_places, lambda j: ends[j])
        first_start = starts_of(first, lambda j: ends[j])
        low = first_start // CHUNK
        high = (first + ROWS - 1) // CHUNK + 1

        def rows_of(c):
            return pl.ds(pl.multiple_of(c * CHUNK, CHUNK), CHUNK)

        def score(c, top):
            at = rows_of(c)
            key_places = places[at]
            allowed = (key_places <= row_places) & (key_places >= row_starts)
            bias = jnp.where(allowed, 0.0, MASKED)
            s = dot(keys[at], q_t[...]) * (SCALE * LOG2E) + jnp.concatenate([bias] * REP, axis=1)
            probs[at] = s
            return jnp.maximum(top, jnp.max(s, axis=0, keepdims=True))

        top = lax.fori_loop(low, high, score, jnp.full((1, QH), MASKED, f32))
        out_t[...] = jnp.zeros_like(out_t)

        def add_out(c, summed):
            at = rows_of(c)
            p = jnp.exp2(probs[at] - top)
            probs[at] = p
            out_t[...] += dot(values_t[c], p.astype(bf16))
            return summed + jnp.sum(p, axis=0, keepdims=True)

        summed = lax.fori_loop(low, high, add_out, jnp.zeros((1, QH), f32))
        inverse = 1.0 / summed
        rounded = (out_t[...] * inverse).astype(bf16).astype(f32)
        delta = jnp.sum(d_t[...].astype(f32) * rounded, axis=0, keepdims=True)
        for h in range(REP):
            lanes = slice(h * HD, (h + 1) * HD)
            od_ref[0, :, lanes] = rounded[:, lanes].T.astype(bf16)
        dq_t[...] = jnp.zeros_like(dq_t)

        def add_grad(c, carry):
            at = rows_of(c)
            w = probs[at] * inverse
            slope = (w * (dot(values[at], d_t[...]) - delta)).astype(bf16)
            dq_t[...] += dot(keys_t[c], slope)
            dk[at] += dot(slope, q_rows[...])
            dv[at] += dot(w.astype(bf16), d_rows[...])
            return carry

        lax.fori_loop(low, high, add_grad, 0)
        for h in range(REP):
            lanes = slice(h * HD, (h + 1) * HD)
            od_ref[1, :, lanes] = (dq_t[:, lanes] * SCALE).T.astype(bf16)

    for m in range(N_Q):
        for y in range(N_Y):
            rows = pl.ds(pl.multiple_of((y * N_Q + (q_own ^ m)) * ROWS, ROWS), ROWS)
            dkv_refs[m][y, :, :HD] = (dk[rows] * SCALE).astype(bf16)
            dkv_refs[m][y, :, HD:] = dv[rows].astype(bf16)


def attention(lengths, kv_own, kv_other, qd):
    vmem = pl.BlockSpec(memory_space=pltpu.VMEM)
    return pl.pallas_call(
        attention_kernel,
        in_specs=[vmem] * (3 + N_Y),
        out_specs=[vmem] * (N_Y + N_Q + 1),
        out_shape=[jax.ShapeDtypeStruct((2, ROWS, QH), bf16)] * N_Y
        + [jax.ShapeDtypeStruct((N_Y, ROWS, 2 * HD), bf16)] * N_Q
        + [jax.ShapeDtypeStruct((N_Y, ROWS, HD), f32)],
        scratch_shapes=[
            pltpu.VMEM((GROUP, HD), bf16),
            pltpu.VMEM((GROUP, HD), bf16),
            pltpu.VMEM((N_CHUNK, HD, CHUNK), bf16),
            pltpu.VMEM((N_CHUNK, HD, CHUNK), bf16),
            pltpu.VMEM((GROUP, HD), jnp.int32),
            pltpu.VMEM((GROUP, QH), f32),
            pltpu.VMEM((QH, HD), bf16),
            pltpu.VMEM((QH, HD), bf16),
            pltpu.VMEM((HD, QH), bf16),
            pltpu.VMEM((HD, QH), bf16),
            pltpu.VMEM((HD, QH), f32),
            pltpu.VMEM((HD, QH), f32),
            pltpu.VMEM((GROUP, HD), f32),
            pltpu.VMEM((GROUP, HD), f32),
        ],
        compiler_params=pltpu.CompilerParams(vmem_limit_bytes=VMEM_LIMIT),
        cost_estimate=pl.CostEstimate(flops=20000000000, bytes_accessed=8000000, transcendentals=3000000),
        name="attention",
    )(lengths, kv_own, kv_other, *qd)


def key_grad_kernel(cos_ref, sin_ref, *refs):
    out_ref = refs[N_Q]
    for y in range(N_Y):
        summed = refs[0][y].astype(f32)
        for q in range(1, N_Q):
            summed = summed + refs[q][y].astype(f32)
        key = summed[:, :HD]
        key = key * cos_ref[y] - pltpu.roll(key, HD // 2, 1) * sin_ref[y]
        both = jnp.concatenate([key, summed[:, HD:]], axis=1).astype(bf16)
        for b in range(N_DP):
            for z in range(2):
                out_ref[b, z, y] = both[b * CAP : (b + 1) * CAP]


def key_grad(parts, cosine, sine):
    vmem = pl.BlockSpec(memory_space=pltpu.VMEM)
    return pl.pallas_call(
        key_grad_kernel,
        in_specs=[vmem] * (2 + N_Q),
        out_specs=vmem,
        out_shape=jax.ShapeDtypeStruct((N_DP, 2, N_Y, CAP, 2 * HD), bf16),
        compiler_params=pltpu.CompilerParams(vmem_limit_bytes=VMEM_LIMIT),
        name="key_grad",
    )(cosine, sine, *parts)


def weight_grad_kernel(kv_own_ref, kv_other_ref, xt_ref, out_ref):
    zl = lax.axis_index("zl")
    total = None
    for y in range(N_Y):
        for z in range(2):
            kv = [ref[:, zl ^ z, y].reshape(ROWS, 2 * HD) for ref in (kv_own_ref, kv_other_ref)]
            left = jnp.concatenate([xt_ref[y, 2 * z], xt_ref[y, 2 * z + 1]], axis=1)
            term = dot(left, jnp.concatenate(kv, axis=0))
            total = term if total is None else total + term
    for j in range(out_ref.shape[0]):
        piece = total[j * SHARE : (j + 1) * SHARE]
        out_ref[j] = jnp.concatenate([piece[:, :HD], piece[:, HD:]], axis=0).astype(bf16)


def weight_grad(xt, kv_own, kv_other):
    steps = 4
    return pl.pallas_call(
        weight_grad_kernel,
        grid=(steps,),
        in_specs=[
            pl.BlockSpec((N_DP, 2, N_Y, CAP, 2 * HD), lambda i: (0,) * 5),
            pl.BlockSpec((N_DP, 2, N_Y, CAP, 2 * HD), lambda i: (0,) * 5),
            pl.BlockSpec((N_Y, N_Q, PART // steps, ROWS), lambda i: (0, 0, i, 0)),
        ],
        out_specs=pl.BlockSpec((N_DP * N_Y // steps, 2 * SHARE, HD), lambda i: (i, 0, 0)),
        out_shape=jax.ShapeDtypeStruct((N_DP * N_Y, 2 * SHARE, HD), bf16),
        compiler_params=pltpu.CompilerParams(vmem_limit_bytes=VMEM_LIMIT),
        cost_estimate=pl.CostEstimate(flops=1400000000, bytes_accessed=7000000, transcendentals=0),
        name="weight_grad",
    )(kv_own, kv_other, xt)


def final_kernel(parts_ref, out_ref):
    for g in range(HEADS):
        summed = parts_ref[0, g].astype(f32)
        for b in range(1, N_DP):
            summed = summed + parts_ref[b, g].astype(f32)
        summed = summed * ((N_DP * GROUP) ** -0.5)
        out_ref[:, g * HD : (g + 1) * HD] = summed[:SHARE]
        out_ref[:, KVW + g * HD : KVW + (g + 1) * HD] = summed[SHARE:]


def final(parts):
    vmem = pl.BlockSpec(memory_space=pltpu.VMEM)
    return pl.pallas_call(
        final_kernel,
        in_specs=[vmem],
        out_specs=vmem,
        out_shape=jax.ShapeDtypeStruct((SHARE, 2 * KVW), f32),
        name="final_sum",
    )(parts)


def swap(array, axes):
    return lax.all_to_all(array, axes, split_axis=0, concat_axis=0, tiled=True)


def flip(array, m):
    return lax.ppermute(array, Q, [(i, i ^ m) for i in range(N_Q)])


def along_y(array, s):
    return lax.ppermute(array, "y", [(i, (i + s) % N_Y) for i in range(N_Y)])


def shards(loaded_x, dest_dp, dest_pos, queries, grad_out, kv_weight, kv_bias, lengths):
    half = np.power(np.float32(1000000.0), -np.arange(HD // 2, dtype=np.float32) * np.float32(2.0 / HD))
    freq = jnp.asarray(np.concatenate([half, half])[None, :].astype(np.float32))
    dest_dp = dest_dp.reshape(1, ROWS)

    xt = turn(dest_dp, loaded_x)
    queries, xt = lax.optimization_barrier((queries, xt))
    qd = split_heads(queries, grad_out)
    x, qd, xt = lax.optimization_barrier((loaded_x, qd, xt))
    xt = [xt[0]] + [flip(xt[m], m) for m in range(1, N_Q)]
    qd = [qd[0]] + [along_y(qd[s], s) for s in range(1, N_Y)]
    kv = project(lengths, dest_dp, dest_pos.reshape(1, ROWS), freq, kv_bias, x, kv_weight)
    kv, xt, qd = lax.optimization_barrier((kv, xt, qd))
    xt = jnp.stack(xt)
    kv, xt = lax.optimization_barrier((kv, xt))
    xt = lax.all_gather(xt, "y", axis=0)
    kv = swap(kv.reshape(-1, CAP, 3 * HD), ("zh", "x", "y", "zl")).reshape(N_DP, N_Y, 2, CAP, 3 * HD)
    kv_other = lax.ppermute(kv, "c", [(0, 1), (1, 0)])

    results = attention(lengths, kv, kv_other, qd)
    od, dkv, posn = results[:N_Y], results[N_Y : N_Y + N_Q], results[-1]
    angle = posn * freq
    cosine = jnp.cos(angle)
    sine = jnp.sin(angle) * jnp.where(jnp.arange(HD) < HD // 2, -1.0, 1.0).astype(f32)
    dkv = [dkv[0]] + [flip(dkv[m], m) for m in range(1, N_Q)]
    od = [od[0]] + [along_y(od[s], -s) for s in range(1, N_Y)]
    dkv, od = lax.optimization_barrier((dkv, od))
    kv_grad = key_grad(dkv, cosine, sine)
    kv_grad = swap(kv_grad.reshape(-1, N_Y * CAP, 2 * HD), ("zh", "x", "zl")).reshape(N_DP, 2, N_Y, CAP, 2 * HD)
    attention_out, query_grad = merge_heads(od)
    kv_grad, attention_out, query_grad = lax.optimization_barrier((kv_grad, attention_out, query_grad))
    kv_grad_other = lax.ppermute(kv_grad, "c", [(0, 1), (1, 0)])
    dw = weight_grad(xt, kv_grad, kv_grad_other)
    dw = swap(dw, ("zh", "x", "y"))
    kv_weight_grad = final(dw.reshape(N_DP, HEADS, 2 * SHARE, HD))
    return attention_out, query_grad, kv_weight_grad


def solution(mesh):
    split = Mesh(mesh.devices.reshape(2, 4, N_Y, 2, 2), AXES)
    rows = P(AXES, None)
    return jax.shard_map(
        shards,
        mesh=split,
        in_specs=(rows, P(AXES), P(AXES), rows, rows, P(), P(), P()),
        out_specs=(rows, rows, rows),
        check_vma=False,
    )
```

time: 249 us -> 174 us (0.70)
  blocking collectives: 87.7 us -> 44.9 us
  waiting for transfers between devices: 74.2 us -> 35.1 us
  between operations: 0.78 us -> 14.1 us
  local copies, waits for them, and re-layouts: 12.5 us -> 3.61 us
  Pallas kernels: 43.6 us -> 48.3 us
  starting transfers between devices: 25.8 us -> 23 us
    all_to_all x5 -> x1, waiting for transfers between devices: 74.2 us -> 9.09 us  [swap(): return lax.all_to_all(array, axes, split_axis=0, concat_axis=0, tiled=True)]
    all_to_all x2, blocking collectives: 87.7 us -> 44.9 us  [swap(): return lax.all_to_all(array, axes, split_axis=0, concat_axis=0, tiled=True)]
    ppermute x0 -> x14, waiting for transfers between devices: none -> 26 us  [the longest x6 15.3 us: along_y(): return lax.ppermute(array, 'y', [(i, (i + s) % N_Y) for i in range(N_Y)])]
    all_to_all x5 -> x1, starting transfers between devices: 25.8 us -> 6.24 us  [swap(): return lax.all_to_all(array, axes, split_axis=0, concat_axis=0, tiled=True)]
    ppermute x0 -> x14, starting transfers between devices: none -> 16.7 us  [the longest x6 9.1 us: along_y(): return lax.ppermute(array, 'y', [(i, (i + s) % N_Y) for i in range(N_Y)])]
    unnamed x23 -> x41, local copies, waits for them, and re-layouts: 8.72 us -> 3.61 us
    pallas_call x3 -> x6, Pallas kernels: 36.3 us -> 41.1 us  [the longest x1 19.8 us: attention(): pl.pallas_call(attention_kernel, in_specs=[vmem] * (3 + N_Y), out_specs=[...]
  transfers between devices with their start and end apart: 5 -> 16, of which waited for: 5 -> 9; matrix products, arithmetic and copies ran while one was open for 3% -> 2% of each run, Pallas kernels for 2% -> 20%
where the time goes in v2:
time: 174 us; the launch traced here: 173 us
  Pallas kernels  48.3 us (28%)
  blocking collectives  44.9 us (26%)
  waiting for transfers between devices  35.1 us (20%)
  starting transfers between devices  23 us (13%)
  between operations  14.1 us (8%)
  other arithmetic  3.85 us (2%)
  local copies, waits for them, and re-layouts  3.61 us (2%)
    all_to_all x2, blocking collectives, swap(): return lax.all_to_all(array, axes, split_axis=0, concat_axis=0, tiled=True)  44.9 us
    pallas_call x1, Pallas kernels, attention(): pl.pallas_call(attention_kernel, in_specs=[vmem] * (3 + N_Y), out_specs=[...  19.8 us
    ppermute x6, waiting for transfers between devices, along_y(): return lax.ppermute(array, 'y', [(i, (i + s) % N_Y) for i in range(N_Y)])  15.3 us
    pallas_call x1, Pallas kernels, project(): pl.pallas_call(project_kernel, grid=(D // COLS,), in_specs=[whole(N_DP, N...  9.55 us
    ppermute x6, starting transfers between devices, along_y(): return lax.ppermute(array, 'y', [(i, (i + s) % N_Y) for i in range(N_Y)])  9.1 us
    all_to_all x1, waiting for transfers between devices, swap(): return lax.all_to_all(array, axes, split_axis=0, concat_axis=0, tiled=True)  9.09 us
    ppermute x6, starting transfers between devices, flip(): return lax.ppermute(array, Q, [(i, i ^ m) for i in range(N_Q)])  7.58 us
    ppermute x6, waiting for transfers between devices, flip(): return lax.ppermute(array, Q, [(i, i ^ m) for i in range(N_Q)])  6.52 us
  transfers between devices with their start and end apart: 16, of which 9 were waited for; matrix products, arithmetic and copies ran while one was open for 2% of the time, Pallas kernels for 20%

profile of v2, /device:TPU:0, one launch (start us, length us, event | category | flops | bytes accessed | tf_op | source)
XLA Modules:
  0.0 172.8 jit_solution(2026501830212450212)
XLA Ops:
  7.2 4.3 %turn.1 = (bf16[1280,128]{1,0:T(8,128)(2,1)}, bf16[1280,128]{1,0:T(8,128)(2,1)}, bf16[1280,128]{1,0:T(8,128)(2,1)}, bf16[1280,128]{1,0:T(8,128)(2,1)}) custom-call(s32[1,128]{1,0:T(1,128)} %bitcast.24, bf16[128,5120]{1,0:T(8,128)(2,1)} %x_ref.2), custom_call_target="tpu_custom_call" | custom-call | flops 2000000000 | bytes 2600000 | tf_op jit(solution)/shard_map/turn/pallas_call | solution.py:204
  11.5 2.5 %split_heads.1 = (bf16[2,128,640]{2,1,0:T(8,128)(2,1)}, bf16[2,128,640]{2,1,0:T(8,128)(2,1)}, bf16[2,128,640]{2,1,0:T(8,128)(2,1)}, bf16[2,128,640]{2,1,0:T(8,128)(2,1)}) custom-call(bf16[128,2560]{1,0:T(8,128)(2,1)} %q_ref, bf16[128,2560]{1,0:T(8,128)(2,1)} %d_ref.1), custom_call_target="tpu_custom_call" | custom-call | tf_op jit(solution)/shard_map/split_heads/pallas_call | solution.py:83
  14.1 2.1 %collective-permute-start.1 = (bf16[1280,128]{1,0:T(8,128)(2,1)S(1)}, bf16[1280,128]{1,0:T(8,128)(2,1)S(1)}, u32[]{:S(2)}, u32[]{:S(2)}) collective-permute-start(bf16[1280,128]{1,0:T(8,128)(2,1)S(1)} %copy-done.18), channel_id=1, source_target_pairs={{0,2},{1,3},{2,0},{3,1},{4,6},{5,7},{6,4},{7,5},{8,10},{9,11},{10,... | collective-permute-start | bytes 983048 | tf_op jit(solution)/shard_map/ppermute | solution.py:434
  16.3 1.6 collective-permute-start.3
  17.8 2.9 %collective-permute-start.4 = (bf16[2,128,640]{2,1,0:T(8,128)(2,1)}, bf16[2,128,640]{2,1,0:T(8,128)(2,1)S(1)}, u32[]{:S(2)}, u32[]{:S(2)}) collective-permute-start(bf16[2,128,640]{2,1,0:T(8,128)(2,1)} %get-tuple-element.78), channel_id=1, source_target_pairs={{0,8},{4,12},{8,0},{12,4},{1,9},{5,13},{9,1},{13,5},{2,10},{6,14},... | collective-permute-start | bytes 983048 | tf_op jit(solution)/shard_map/ppermute | solution.py:438
  20.7 1.3 collective-permute-start.5
  22.8 9.6 %project.1 = bf16[8,4,2,16,384]{4,3,2,1,0:T(8,128)(2,1)} custom-call(s32[8,4]{1,0:T(8,128)} %copy.15.lengths_ref, s32[1,128]{1,0:T(1,128)} %bitcast.25, s32[1,128]{1,0:T(1,128)} %bitcast.26, f32[1,128]{1,0:T(1,128)} %constant.8.clone.freq_ref, bf16[1024]{0:T(1024)(128)(2,1)} %bias_ref.1, bf16[128,5120]{1,0:T(8,128)(2,1)} %x_ref.2, bf16[5120,1024]{1,0:T(8,128)(2,1)} %w_ref.1), custom_call_target="tpu_custom_call" | custom-call | flops 1600000000 | bytes 16000000 | tf_op jit(solution)/shard_map/project/pallas_call | solution.py:166
  32.4 3.4 %collective-permute-done.4.refs_2_ = bf16[2,128,640]{2,1,0:T(8,128)(2,1)S(1)} collective-permute-done((bf16[2,128,640]{2,1,0:T(8,128)(2,1)}, bf16[2,128,640]{2,1,0:T(8,128)(2,1)S(1)}, u32[]{:S(2)}, u32[]{:S(2)}) %collective-permute-start.4) | collective-permute-done | bytes 327712 | tf_op jit(solution)/shard_map/ppermute | solution.py:438
  35.7 1.3 pad_maximum_fusion
  37.0 1.1 copy-done
  38.1 25.3 %all_to_all.15 = bf16[64,16,384]{2,1,0:T(8,128)(2,1)S(1)} all-to-all(bf16[64,16,384]{2,1,0:T(8,128)(2,1)S(1)} %bitcast.13), channel_id=1, replica_groups=mesh['zh'=2,'x'=4,'y'=4,'zl'=2,'c'=2] {'zh','x','y','zl'}, dimensions={0} | all-to-all | bytes 1572864 | tf_op jit(solution)/shard_map/all_to_all | solution.py:430
  63.4 2.3 %collective-permute-done.6.kv_other_ref = bf16[8,4,2,16,384]{4,3,2,1,0:T(8,128)(2,1)S(1)} collective-permute-done((bf16[8,4,2,16,384]{4,3,2,1,0:T(8,128)(2,1)S(1)}, bf16[8,4,2,16,384]{4,3,2,1,0:T(8,128)(2,1)S(1)}, u32[]{:S(2)}, u32[]{:S(2)}) %collective-permute-start.6) | collective-permute-done | bytes 786464 | tf_op jit(solution)/shard_map/ppermute | solution.py:458
  65.7 1.0 copy-done.13
  66.7 19.8 %attention.1 = (bf16[2,128,640]{2,1,0:T(8,128)(2,1)}, bf16[2,128,640]{2,1,0:T(8,128)(2,1)}, bf16[2,128,640]{2,1,0:T(8,128)(2,1)}, bf16[2,128,640]{2,1,0:T(8,128)...) custom-call(s32[8,4]{1,0:T(8,128)} %copy.15.lengths_ref, ...), custom_call_target="tpu_custom_call" | custom-call | flops 20000000000 | bytes 8000000 | tf_op jit(solution)/shard_map/attention/pallas_call | solution.py:321
  86.7 5.2 %collective-permute-start.8 = (bf16[4,128,256]{2,1,0:T(8,128)(2,1)}, bf16[4,128,256]{2,1,0:T(8,128)(2,1)S(1)}, u32[]{:S(2)}, u32[]{:S(2)}) collective-permute-start(bf16[4,128,256]{2,1,0:T(8,128)(2,1)} %get-tuple-element.93), channel_id=1, source_target_pairs={{0,2},{1,3},{2,0},{3,1},{4,6},{5,7},{6,4},{7,5},{8,10},{9,11},{10,... | collective-permute-start | bytes 786440 | tf_op jit(solution)/shard_map/ppermute | solution.py:434
  91.9 1.6 collective-permute-start.10
  93.5 1.3 collective-permute-start.11
  95.2 2.6 %sine_multiply_fusion = (f32[4,128,128]{2,1,0:T(8,128)}, f32[4,128,128]{2,1,0:T(8,128)}) fusion(f32[4,128,128]{2,1,0:T(8,128)} %get-tuple-element.90, f32[128]{0:T(128)S(1)} %compare_select_fusion, f32[128]{0:T(128)S(1)} %copy-done.12), kind=kLoop, calls=%fused_computation.1 | loop fusion | flops 131072 | bytes 787456 | tf_op jit(solution)/shard_map/mul | solution.py:464
  97.8 1.4 collective-permute-done.8.refs_2_
  99.2 5.1 %collective-permute-done.9.refs_3_ = bf16[4,128,256]{2,1,0:T(8,128)(2,1)S(1)} collective-permute-done((bf16[4,128,256]{2,1,0:T(8,128)(2,1)}, bf16[4,128,256]{2,1,0:T(8,128)(2,1)S(1)}, u32[]{:S(2)}, u32[]{:S(2)}) %collective-permute-start.9) | collective-permute-done | bytes 262176 | tf_op jit(solution)/shard_map/ppermute | solution.py:434
  104.3 4.1 %collective-permute-done.10.refs_1_ = bf16[2,128,640]{2,1,0:T(8,128)(2,1)S(1)} collective-permute-done((bf16[2,128,640]{2,1,0:T(8,128)(2,1)}, bf16[2,128,640]{2,1,0:T(8,128)(2,1)S(1)}, u32[]{:S(2)}, u32[]{:S(2)}) %collective-permute-start.10) | collective-permute-done | bytes 327712 | tf_op jit(solution)/shard_map/ppermute | solution.py:438
  108.4 1.1 collective-permute-done.11.refs_2_
  109.5 6.7 %collective-permute-done.12.refs_3_ = bf16[2,128,640]{2,1,0:T(8,128)(2,1)S(1)} collective-permute-done((bf16[2,128,640]{2,1,0:T(8,128)(2,1)}, bf16[2,128,640]{2,1,0:T(8,128)(2,1)S(1)}, u32[]{:S(2)}, u32[]{:S(2)}) %collective-permute-start.12) | collective-permute-done | bytes 327712 | tf_op jit(solution)/shard_map/ppermute | solution.py:438
  116.2 2.4 %key_grad.1 = bf16[8,2,4,16,256]{4,3,2,1,0:T(8,128)(2,1)} custom-call(f32[4,128,128]{2,1,0:T(8,128)} %get-tuple-element.114.cos_ref, f32[4,128,128]{2,1,0:T(8,128)} %get-tuple-element.113.sin_ref, bf16[4,128,256]{2,1,0:T(8,128)(2,1)} %get-tuple-element.99.refs_0_, bf16[4,128,256]{2,1,0:T(8,128)(2,1)} %copy-done.8, bf16[4,128,256]{2,1,0:T(8,128)(2,1)} %copy-done.9, ...), custom_call_target="tpu_custom_call" | custom-call | tf_op jit(solution)/shard_map/key_grad/pallas_call | solution.py:366
  118.7 6.2 %all-to-all-start.1 = ((bf16[16,64,256]{2,1,0:T(8,128)(2,1)}), bf16[16,64,256]{2,1,0:T(8,128)(2,1)S(1)}, u32[]{:S(2)}, u32[]{:S(2)}) async-start(bf16[16,64,256]{2,1,0:T(8,128)(2,1)} %bitcast.15), calls=%async_computation.1 | async-start | bytes 1048576 | tf_op jit(solution)/shard_map/all_to_all | solution.py:430
  124.9 2.4 %merge_heads.1 = (bf16[128,2560]{1,0:T(8,128)(2,1)}, bf16[128,2560]{1,0:T(8,128)(2,1)}) custom-call(bf16[2,128,640]{2,1,0:T(8,128)(2,1)} %get-tuple-element.103.refs_0_, bf16[2,128,640]{2,1,0:T(8,128)(2,1)} %copy-done.5, bf16[2,128,640]{2,1,0:T(8,128)(2,1)} %copy-done.6, bf16[2,128,640]{2,1,0:T(8,128)(2,1)} %copy-done.7), custom_call_target="tpu_custom_call" | custom-call | tf_op jit(solution)/shard_map/merge_heads/pallas_call | solution.py:103
  127.4 9.1 %all-to-all-done.1 = bf16[16,64,256]{2,1,0:T(8,128)(2,1)S(1)} async-done(((bf16[16,64,256]{2,1,0:T(8,128)(2,1)}), bf16[16,64,256]{2,1,0:T(8,128)(2,1)S(1)}, u32[]{:S(2)}, u32[]{:S(2)}) %all-to-all-start.1) | async-done | bytes 524320 | tf_op jit(solution)/shard_map/all_to_all | solution.py:430
  136.5 1.9 %collective-permute-done.13.kv_other_ref = bf16[8,2,4,16,256]{4,3,2,1,0:T(8,128)(2,1)S(1)} collective-permute-done((bf16[8,2,4,16,256]{4,3,2,1,0:T(8,128)(2,1)S(1)}, bf16[8,2,4,16,256]{4,3,2,1,0:T(8,128)(2,1)S(1)}, u32[]{:S(2)}, u32[]{:S(2)}) %collective-permute-start.13) | collective-permute-done | bytes 524320 | tf_op jit(solution)/shard_map/ppermute | solution.py:472
  138.4 0.8 copy-done.3
  139.2 5.3 %weight_grad.1 = bf16[32,80,128]{2,1,0:T(8,128)(2,1)} custom-call(bf16[8,2,4,16,256]{4,3,2,1,0:T(8,128)(2,1)} %bitcast.17, bf16[8,2,4,16,256]{4,3,2,1,0:T(8,128)(2,1)} %copy-done.3, bf16[4,4,1280,128]{3,2,1,0:T(8,128)(2,1)} %bitcast.12), custom_call_target="tpu_custom_call" | custom-call | flops 1400000000 | bytes 7000000 | tf_op jit(solution)/shard_map/weight_grad/pallas_call | solution.py:392
  144.5 19.6 %all_to_all.16 = bf16[32,80,128]{2,1,0:T(8,128)(2,1)} all-to-all(bf16[32,80,128]{2,1,0:T(8,128)(2,1)} %weight_grad.1), channel_id=1, replica_groups=mesh['zh'=2,'x'=4,'y'=4,'zl'=2,'c'=2] {'zh','x','y'}, dimensions={0} | all-to-all | bytes 1310720 | tf_op jit(solution)/shard_map/all_to_all | solution.py:430
  164.1 1.8 %final_sum.1 = f32[40,1024]{1,0:T(8,128)} custom-call(bf16[8,4,80,128]{3,2,1,0:T(8,128)(2,1)} %bitcast.14), custom_call_target="tpu_custom_call" | custom-call | tf_op jit(solution)/shard_map/final_sum/pallas_call | solution.py:420
  (55 shorter events, 1.6 us)
Async XLA Ops:
  7.2 131.2 %all-gather.3.cloned.1.call-start = ((), (), s32[]{:S(2)}) async-start(), calls=%async_computation.3 | async-start | bytes 6553600 | tf_op jit(solution)/shard_map/all_gather | solution.py:456
  11.5 2.6 %copy-start.19 = (bf16[1280,128]{1,0:T(8,128)(2,1)S(1)}, bf16[1280,128]{1,0:T(8,128)(2,1)}, u32[]{:S(2)}) copy-start(bf16[1280,128]{1,0:T(8,128)(2,1)} %get-tuple-element.73) | copy-start | bytes 983044
  11.5 2.6 %copy-start.18 = (bf16[1280,128]{1,0:T(8,128)(2,1)S(1)}, bf16[1280,128]{1,0:T(8,128)(2,1)}, u32[]{:S(2)}) copy-start(bf16[1280,128]{1,0:T(8,128)(2,1)} %get-tuple-element.74) | copy-start | bytes 983044
  11.5 4.6 %copy-start.17 = (bf16[1280,128]{1,0:T(8,128)(2,1)S(1)}, bf16[1280,128]{1,0:T(8,128)(2,1)}, u32[]{:S(2)}) copy-start(bf16[1280,128]{1,0:T(8,128)(2,1)} %get-tuple-element.75) | copy-start | bytes 983044
  11.5 10.6 %copy-start.11 = (s32[8,4]{0,1:T(4,128)S(1)}, s32[8,4]{0,1:T(4,128)}, u32[]{:S(2)}) copy-start(s32[8,4]{0,1:T(4,128)} %param.16) | copy-start | bytes 388
  14.1 6.7 %collective-permute-start = (bf16[1280,128]{1,0:T(8,128)(2,1)S(1)}, bf16[1280,128]{1,0:T(8,128)(2,1)S(1)}, u32[]{:S(2)}, u32[]{:S(2)}) collective-permute-start(bf16[1280,128]{1,0:T(8,128)(2,1)S(1)} %copy-done.19), channel_id=1, source_target_pairs={{0,1},{1,0},{2,3},{3,2},{4,5},{5,4},{6,7},{7,6},{8,9},{9,8},{10,11... | collective-permute-start | bytes 983048 | tf_op jit(solution)/shard_map/ppermute | solution.py:434
  14.1 18.2 %collective-permute-start.1 = (bf16[1280,128]{1,0:T(8,128)(2,1)S(1)}, bf16[1280,128]{1,0:T(8,128)(2,1)S(1)}, u32[]{:S(2)}, u32[]{:S(2)}) collective-permute-start(bf16[1280,128]{1,0:T(8,128)(2,1)S(1)} %copy-done.18), channel_id=1, source_target_pairs={{0,2},{1,3},{2,0},{3,1},{4,6},{5,7},{6,4},{7,5},{8,10},{9,11},{10,... | collective-permute-start | bytes 983048 | tf_op jit(solution)/shard_map/ppermute | solution.py:434
  16.1 16.2 %collective-permute-start.2 = (bf16[1280,128]{1,0:T(8,128)(2,1)S(1)}, bf16[1280,128]{1,0:T(8,128)(2,1)S(1)}, u32[]{:S(2)}, u32[]{:S(2)}) collective-permute-start(bf16[1280,128]{1,0:T(8,128)(2,1)S(1)} %copy-done.17), channel_id=1, source_target_pairs={{0,3},{1,2},{2,1},{3,0},{4,7},{5,6},{6,5},{7,4},{8,11},{9,10},{10,... | collective-permute-start | bytes 983048 | tf_op jit(solution)/shard_map/ppermute | solution.py:434
  16.3 16.0 %collective-permute-start.3 = (bf16[2,128,640]{2,1,0:T(8,128)(2,1)}, bf16[2,128,640]{2,1,0:T(8,128)(2,1)S(1)}, u32[]{:S(2)}, u32[]{:S(2)}) collective-permute-start(bf16[2,128,640]{2,1,0:T(8,128)(2,1)} %get-tuple-element.77), channel_id=1, source_target_pairs={{0,4},{4,8},{8,12},{12,0},{1,5},{5,9},{9,13},{13,1},{2,6},{6,10},{... | collective-permute-start | bytes 983048 | tf_op jit(solution)/shard_map/ppermute | solution.py:438
  17.8 17.9 %collective-permute-start.4 = (bf16[2,128,640]{2,1,0:T(8,128)(2,1)}, bf16[2,128,640]{2,1,0:T(8,128)(2,1)S(1)}, u32[]{:S(2)}, u32[]{:S(2)}) collective-permute-start(bf16[2,128,640]{2,1,0:T(8,128)(2,1)} %get-tuple-element.78), channel_id=1, source_target_pairs={{0,8},{4,12},{8,0},{12,4},{1,9},{5,13},{9,1},{13,5},{2,10},{6,14},... | collective-permute-start | bytes 983048 | tf_op jit(solution)/shard_map/ppermute | solution.py:438
  20.7 15.0 %collective-permute-start.5 = (bf16[2,128,640]{2,1,0:T(8,128)(2,1)}, bf16[2,128,640]{2,1,0:T(8,128)(2,1)S(1)}, u32[]{:S(2)}, u32[]{:S(2)}) collective-permute-start(bf16[2,128,640]{2,1,0:T(8,128)(2,1)} %get-tuple-element.79), channel_id=1, source_target_pairs={{0,12},{4,0},{8,4},{12,8},{1,13},{5,1},{9,5},{13,9},{2,14},{6,2},{... | collective-permute-start | bytes 983048 | tf_op jit(solution)/shard_map/ppermute | solution.py:438
  22.8 13.0 %copy-start.4 = (bf16[1280,128]{1,0:T(8,128)(2,1)S(1)}, bf16[1280,128]{1,0:T(8,128)(2,1)}, u32[]{:S(2)}) copy-start(bf16[1280,128]{1,0:T(8,128)(2,1)} %get-tuple-element.81) | copy-start | bytes 983044
  32.3 4.7 %copy-start.14 = (bf16[2,128,640]{2,1,0:T(8,128)(2,1)}, bf16[2,128,640]{2,1,0:T(8,128)(2,1)S(1)}, u32[]{:S(2)}) copy-start(bf16[2,128,640]{2,1,0:T(8,128)(2,1)S(1)} %collective-permute-done.3.refs_1_) | copy-start | bytes 983044
  35.7 1.3 copy-start.15
  63.4 2.3 %copy-start.2 = (bf16[64,16,384]{2,1,0:T(8,128)(2,1)}, bf16[64,16,384]{2,1,0:T(8,128)(2,1)S(1)}, u32[]{:S(2)}) copy-start(bf16[64,16,384]{2,1,0:T(8,128)(2,1)S(1)} %all_to_all.15) | copy-start | bytes 2359300
  63.4 31.8 %copy-start.12 = (f32[128]{0:T(128)S(1)}, f32[128]{0:T(128)}, u32[]{:S(2)}) copy-start(f32[128]{0:T(128)} %constant.9) | copy-start | bytes 1540
  63.4 2.3 %collective-permute-start.6 = (bf16[8,4,2,16,384]{4,3,2,1,0:T(8,128)(2,1)S(1)}, bf16[8,4,2,16,384]{4,3,2,1,0:T(8,128)(2,1)S(1)}, u32[]{:S(2)}, u32[]{:S(2)}) collective-permute-start(bf16[8,4,2,16,384]{4,3,2,1,0:T(8,128)(2,1)S(1)} %bitcast.18), channel_id=1, source_target_pairs={{0,1},{1,0},{2,3},{3,2},{4,5},{5,4},{6,7},{7,6},{8,9},{9,8},{10,11... | collective-permute-start | bytes 2359304 | tf_op jit(solution)/shard_map/ppermute | solution.py:458
  86.5 8.2 %collective-permute-start.7 = (bf16[4,128,256]{2,1,0:T(8,128)(2,1)}, bf16[4,128,256]{2,1,0:T(8,128)(2,1)S(1)}, u32[]{:S(2)}, u32[]{:S(2)}) collective-permute-start(bf16[4,128,256]{2,1,0:T(8,128)(2,1)} %get-tuple-element.92), channel_id=1, source_target_pairs={{0,1},{1,0},{2,3},{3,2},{4,5},{5,4},{6,7},{7,6},{8,9},{9,8},{10,11... | collective-permute-start | bytes 786440 | tf_op jit(solution)/shard_map/ppermute | solution.py:434
  86.7 12.5 %collective-permute-start.8 = (bf16[4,128,256]{2,1,0:T(8,128)(2,1)}, bf16[4,128,256]{2,1,0:T(8,128)(2,1)S(1)}, u32[]{:S(2)}, u32[]{:S(2)}) collective-permute-start(bf16[4,128,256]{2,1,0:T(8,128)(2,1)} %get-tuple-element.93), channel_id=1, source_target_pairs={{0,2},{1,3},{2,0},{3,1},{4,6},{5,7},{6,4},{7,5},{8,10},{9,11},{10,... | collective-permute-start | bytes 786440 | tf_op jit(solution)/shard_map/ppermute | solution.py:434
  91.8 12.5 %collective-permute-start.9 = (bf16[4,128,256]{2,1,0:T(8,128)(2,1)}, bf16[4,128,256]{2,1,0:T(8,128)(2,1)S(1)}, u32[]{:S(2)}, u32[]{:S(2)}) collective-permute-start(bf16[4,128,256]{2,1,0:T(8,128)(2,1)} %get-tuple-element.94), channel_id=1, source_target_pairs={{0,3},{1,2},{2,1},{3,0},{4,7},{5,6},{6,5},{7,4},{8,11},{9,10},{10,... | collective-permute-start | bytes 786440 | tf_op jit(solution)/shard_map/ppermute | solution.py:434
  91.9 16.5 %collective-permute-start.10 = (bf16[2,128,640]{2,1,0:T(8,128)(2,1)}, bf16[2,128,640]{2,1,0:T(8,128)(2,1)S(1)}, u32[]{:S(2)}, u32[]{:S(2)}) collective-permute-start(bf16[2,128,640]{2,1,0:T(8,128)(2,1)} %get-tuple-element.96), channel_id=1, source_target_pairs={{0,12},{4,0},{8,4},{12,8},{1,13},{5,1},{9,5},{13,9},{2,14},{6,2},{... | collective-permute-start | bytes 983048 | tf_op jit(solution)/shard_map/ppermute | solution.py:438
  93.5 16.0 %collective-permute-start.11 = (bf16[2,128,640]{2,1,0:T(8,128)(2,1)}, bf16[2,128,640]{2,1,0:T(8,128)(2,1)S(1)}, u32[]{:S(2)}, u32[]{:S(2)}) collective-permute-start(bf16[2,128,640]{2,1,0:T(8,128)(2,1)} %get-tuple-element.97), channel_id=1, source_target_pairs={{0,8},{4,12},{8,0},{12,4},{1,9},{5,13},{9,1},{13,5},{2,10},{6,14},... | collective-permute-start | bytes 983048 | tf_op jit(solution)/shard_map/ppermute | solution.py:438
  94.8 21.5 %copy-start.8 = (bf16[4,128,256]{2,1,0:T(8,128)(2,1)}, bf16[4,128,256]{2,1,0:T(8,128)(2,1)S(1)}, u32[]{:S(2)}) copy-start(bf16[4,128,256]{2,1,0:T(8,128)(2,1)S(1)} %collective-permute-done.7.refs_1_) | copy-start | bytes 786436
  94.8 21.5 %collective-permute-start.12 = (bf16[2,128,640]{2,1,0:T(8,128)(2,1)}, bf16[2,128,640]{2,1,0:T(8,128)(2,1)S(1)}, u32[]{:S(2)}, u32[]{:S(2)}) collective-permute-start(bf16[2,128,640]{2,1,0:T(8,128)(2,1)} %get-tuple-element.98), channel_id=1, source_target_pairs={{0,4},{4,8},{8,12},{12,0},{1,5},{5,9},{9,13},{13,1},{2,6},{6,10},{... | collective-permute-start | bytes 983048 | tf_op jit(solution)/shard_map/ppermute | solution.py:438
  99.2 17.0 %copy-start.9 = (bf16[4,128,256]{2,1,0:T(8,128)(2,1)}, bf16[4,128,256]{2,1,0:T(8,128)(2,1)S(1)}, u32[]{:S(2)}) copy-start(bf16[4,128,256]{2,1,0:T(8,128)(2,1)S(1)} %collective-permute-done.8.refs_2_) | copy-start | bytes 786436
  104.3 11.9 %copy-start.10 = (bf16[4,128,256]{2,1,0:T(8,128)(2,1)}, bf16[4,128,256]{2,1,0:T(8,128)(2,1)S(1)}, u32[]{:S(2)}) copy-start(bf16[4,128,256]{2,1,0:T(8,128)(2,1)S(1)} %collective-permute-done.9.refs_3_) | copy-start | bytes 786436
  108.4 10.3 %copy-start.5 = (bf16[2,128,640]{2,1,0:T(8,128)(2,1)}, bf16[2,128,640]{2,1,0:T(8,128)(2,1)S(1)}, u32[]{:S(2)}) copy-start(bf16[2,128,640]{2,1,0:T(8,128)(2,1)S(1)} %collective-permute-done.10.refs_1_) | copy-start | bytes 983044
  109.5 9.2 %copy-start.6 = (bf16[2,128,640]{2,1,0:T(8,128)(2,1)}, bf16[2,128,640]{2,1,0:T(8,128)(2,1)S(1)}, u32[]{:S(2)}) copy-start(bf16[2,128,640]{2,1,0:T(8,128)(2,1)S(1)} %collective-permute-done.11.refs_2_) | copy-start | bytes 983044
  116.2 2.5 %copy-start.7 = (bf16[2,128,640]{2,1,0:T(8,128)(2,1)}, bf16[2,128,640]{2,1,0:T(8,128)(2,1)S(1)}, u32[]{:S(2)}) copy-start(bf16[2,128,640]{2,1,0:T(8,128)(2,1)S(1)} %collective-permute-done.12.refs_3_) | copy-start | bytes 983044
  118.7 17.8 %all-to-all-start.1 = ((bf16[16,64,256]{2,1,0:T(8,128)(2,1)}), bf16[16,64,256]{2,1,0:T(8,128)(2,1)S(1)}, u32[]{:S(2)}, u32[]{:S(2)}) async-start(bf16[16,64,256]{2,1,0:T(8,128)(2,1)} %bitcast.15), calls=%async_computation.1 | async-start | bytes 1048576 | tf_op jit(solution)/shard_map/all_to_all | solution.py:430
  136.5 1.9 %copy-start.1 = (bf16[16,64,256]{2,1,0:T(8,128)(2,1)}, bf16[16,64,256]{2,1,0:T(8,128)(2,1)S(1)}, u32[]{:S(2)}) copy-start(bf16[16,64,256]{2,1,0:T(8,128)(2,1)S(1)} %all-to-all-done.1) | copy-start | bytes 1572868
  136.5 1.9 %collective-permute-start.13 = (bf16[8,2,4,16,256]{4,3,2,1,0:T(8,128)(2,1)S(1)}, bf16[8,2,4,16,256]{4,3,2,1,0:T(8,128)(2,1)S(1)}, u32[]{:S(2)}, u32[]{:S(2)}) collective-permute-start(bf16[8,2,4,16,256]{4,3,2,1,0:T(8,128)(2,1)S(1)} %bitcast.16), channel_id=1, source_target_pairs={{0,1},{1,0},{2,3},{3,2},{4,5},{5,4},{6,7},{7,6},{8,9},{9,8},{10,11... | collective-permute-start | bytes 1572872 | tf_op jit(solution)/shard_map/ppermute | solution.py:472
  (4 other events, 4.2 us)
Sparse Core Ops, SparseCore 0:
  37.2 76.2 all-gather.2

commit v3 on v2

--- a/solution.py
+++ b/solution.py
@@ -25,9 +25,10 @@
 QH = REP * HD
 SHARE = D // (N_DP * N_CTX)
 PART = D // N_Q
-COLS = 640
-TURN = 1280
-CHUNK = 256
+COLS = 2560
+TURN = 2560
+CHUNK = 512
+PAIR = 2 * ROWS
 N_CHUNK = GROUP // CHUNK
 MASKED = -1e30
 SCALE = HD**-0.5
@@ -70,39 +71,68 @@
     return (iota((ROWS, ROWS), 0) == slot).astype(f32).astype(bf16)
 
 
-def split_kernel(q_ref, d_ref, *out_refs):
-    y = lax.axis_index("y")
+def cut_kernel(dp_ref, x_ref, q_ref, d_ref, *refs):
+    head_refs, piece_refs, order, pieces = refs[:N_Y], refs[N_Y : N_Y + N_Q], refs[-2], refs[-1]
+    _, y, own = coordinates()
+
+    @pl.when(pl.program_id(0) == 0)
+    def _():
+        order[...] = order_of(dp_ref[...])
+
     for s in range(N_Y):
         lanes = pl.ds(pl.multiple_of(lax.rem(y + s, N_Y) * QH, HD), QH)
-        out_refs[s][0] = q_ref[:, lanes]
-        out_refs[s][1] = d_ref[:, lanes]
-
-
-def split_heads(queries, grad_out):
-    vmem = pl.BlockSpec(memory_space=pltpu.VMEM)
-    return pl.pallas_call(
-        split_kernel,
-        in_specs=[vmem] * 2,
-        out_specs=[vmem] * N_Y,
-        out_shape=[jax.ShapeDtypeStruct((2, ROWS, QH), bf16)] * N_Y,
-        name="split_heads",
-    )(queries, grad_out)
-
-
-def merge_kernel(*refs):
+        head_refs[s][0] = q_ref[:, lanes]
+        head_refs[s][1] = d_ref[:, lanes]
+    turned = dot(order[...], x_ref[...]).T
+    for q in range(N_Q):
+        rows = [turned[(j * N_Q + q) * SHARE : (j * N_Q + q + 1) * SHARE] for j in range(TURN // (N_Q * SHARE))]
+        pieces[q] = jnp.concatenate(rows, axis=0).astype(bf16)
+    for m in range(N_Q):
+        piece_refs[m][...] = pieces[own ^ m]
+
+
+def cut(dest_dp, x, queries, grad_out):
+    steps = D // TURN
+    rows = ROWS // steps
+    return pl.pallas_call(
+        cut_kernel,
+        grid=(steps,),
+        in_specs=[
+            pl.BlockSpec((1, ROWS), lambda i: (0, 0)),
+            pl.BlockSpec((ROWS, TURN), lambda i: (0, i)),
+            pl.BlockSpec((rows, HEADS * QH), lambda i: (i, 0)),
+            pl.BlockSpec((rows, HEADS * QH), lambda i: (i, 0)),
+        ],
+        out_specs=[pl.BlockSpec((2, rows, QH), lambda i: (0, i, 0))] * N_Y
+        + [pl.BlockSpec((TURN // N_Q, ROWS), lambda i: (i, 0))] * N_Q,
+        out_shape=[jax.ShapeDtypeStruct((2, ROWS, QH), bf16)] * N_Y
+        + [jax.ShapeDtypeStruct((PART, ROWS), bf16)] * N_Q,
+        scratch_shapes=[pltpu.VMEM((ROWS, ROWS), bf16), pltpu.VMEM((N_Q, TURN // N_Q, ROWS), bf16)],
+        compiler_params=pltpu.CompilerParams(vmem_limit_bytes=VMEM_LIMIT),
+        cost_estimate=pl.CostEstimate(flops=2000000000, bytes_accessed=5200000, transcendentals=0),
+        name="cut",
+    )(dest_dp, x, queries, grad_out)
+
+
+def merge_kernel(stay_ref, back_ref, ahead_ref, dq_ref, out_ref, *refs):
     y = lax.axis_index("y")
-    out_ref, dq_ref = refs[N_Y:]
+    pieces = [
+        (stay_ref.at[0], stay_ref.at[1]),
+        (back_ref.at[0], back_ref.at[1]),
+        (out_ref.at[0], dq_ref.at[0]),
+        (ahead_ref.at[0], ahead_ref.at[1]),
+    ]
     for s in range(N_Y):
         lanes = pl.ds(pl.multiple_of(lax.rem(y + s, N_Y) * QH, HD), QH)
-        out_ref[:, lanes] = refs[s][0]
-        dq_ref[:, lanes] = refs[s][1]
-
-
-def merge_heads(pieces):
+        for k in range(2):
+            refs[k][:, lanes] = pieces[s][k][...]
+
+
+def merge_heads(*pieces):
     vmem = pl.BlockSpec(memory_space=pltpu.VMEM)
     return pl.pallas_call(
         merge_kernel,
-        in_specs=[vmem] * N_Y,
+        in_specs=[vmem] * len(pieces),
         out_specs=[vmem] * 2,
         out_shape=[jax.ShapeDtypeStruct((ROWS, HEADS * QH), bf16)] * 2,
         name="merge_heads",
@@ -184,44 +214,15 @@
     )(lengths, dest_dp, dest_pos, freq, bias, x, w)
 
 
-def turn_kernel(dp_ref, x_ref, *refs):
-    out_refs, order, pieces = refs[:N_Q], refs[N_Q], refs[N_Q + 1]
-    own = coordinates()[2]
-
-    @pl.when(pl.program_id(0) == 0)
-    def _():
-        order[...] = order_of(dp_ref[...])
-
-    turned = dot(order[...], x_ref[...]).T
-    for q in range(N_Q):
-        rows = [turned[(j * N_Q + q) * SHARE : (j * N_Q + q + 1) * SHARE] for j in range(TURN // (N_Q * SHARE))]
-        pieces[q] = jnp.concatenate(rows, axis=0).astype(bf16)
-    for m in range(N_Q):
-        out_refs[m][...] = pieces[own ^ m]
-
-
-def turn(dest_dp, x):
-    return pl.pallas_call(
-        turn_kernel,
-        grid=(D // TURN,),
-        in_specs=[
-            pl.BlockSpec((1, ROWS), lambda i: (0, 0)),
-            pl.BlockSpec((ROWS, TURN), lambda i: (0, i)),
-        ],
-        out_specs=[pl.BlockSpec((TURN // N_Q, ROWS), lambda i: (i, 0))] * N_Q,
-        out_shape=[jax.ShapeDtypeStruct((PART, ROWS), bf16)] * N_Q,
-        scratch_shapes=[pltpu.VMEM((ROWS, ROWS), bf16), pltpu.VMEM((N_Q, TURN // N_Q, ROWS), bf16)],
-        compiler_params=pltpu.CompilerParams(vmem_limit_bytes=VMEM_LIMIT),
-        cost_estimate=pl.CostEstimate(flops=2000000000, bytes_accessed=2600000, transcendentals=0),
-        name="turn",
-    )(dest_dp, x)
-
-
 def attention_kernel(lengths_ref, kv_own_ref, kv_other_ref, *refs):
-    qd_refs, od_refs, dkv_refs = refs[:N_Y], refs[N_Y : 2 * N_Y], refs[2 * N_Y : 2 * N_Y + N_Q]
-    posn_ref = refs[2 * N_Y + N_Q]
+    qd_refs, refs = refs[:N_Y], refs[N_Y:]
+    stay_ref, back_ref, ahead_ref = refs[:3]
+    out_refs = [stay_ref.at[0], back_ref.at[0], ahead_ref.at[2], ahead_ref.at[0]]
+    dq_refs = [stay_ref.at[1], back_ref.at[1], back_ref.at[2], ahead_ref.at[1]]
+    dkv_refs = refs[3 : 3 + N_Q]
+    posn_ref = refs[3 + N_Q]
     (keys, values, keys_t, values_t, places, probs, q_rows, d_rows, q_t, d_t,
-                     out_t, dq_t, dk, dv) = refs[2 * N_Y + N_Q + 1 :]
+                     out_t, dq_t, dk, dv) = refs[4 + N_Q :]
     own, y_own, q_own = coordinates()
     ends = []
     for j in range(NSEQ):
@@ -230,23 +231,24 @@
 
     core = q_own % 2
     for kv_ref, c in ((kv_own_ref, core), (kv_other_ref, 1 - core)):
-        for chunk in range(N_CHUNK):
-            block = kv_ref[:, chunk // 2, chunk % 2].reshape(ROWS, 3 * HD)
-            first = pl.multiple_of(chunk * CHUNK + c * ROWS, ROWS)
+        for pair in range(GROUP // PAIR):
+            block = kv_ref[:, pair // 2, pair % 2].reshape(ROWS, 3 * HD)
+            first = pl.multiple_of(pair * PAIR + c * ROWS, ROWS)
             rows = pl.ds(first, ROWS)
-            lanes = pl.ds(pl.multiple_of(c * ROWS, ROWS), ROWS)
+            chunk = pair * PAIR // CHUNK
+            lanes = pl.ds(pl.multiple_of(pair * PAIR % CHUNK + c * ROWS, ROWS), ROWS)
             key = block[:, :HD]
             value = block[:, HD : 2 * HD]
             keys[rows] = key
             values[rows] = value
-            keys_t[chunk, :, lanes] = key.astype(f32).T.astype(bf16)
-            values_t[chunk, :, lanes] = value.astype(f32).T.astype(bf16)
+            keys_t[chunk, :, lanes] = key.T
+            values_t[chunk, :, lanes] = value.T
             places[rows] = block[:, 2 * HD :].astype(f32).astype(jnp.int32) + first
     dk[...] = jnp.zeros_like(dk)
     dv[...] = jnp.zeros_like(dv)
 
     for s in range(N_Y):
-        qd_ref, od_ref = qd_refs[s], od_refs[s]
+        qd_ref = qd_refs[s]
         own_places = places[pl.ds(pl.multiple_of((s * N_Q + q_own) * ROWS, ROWS), ROWS)]
         first = (lax.rem(y_own + N_Y - s, N_Y) * N_Q + q_own) * ROWS
         posn_ref[s] = (own_places - starts_of(own_places, lambda j: ends[j])).astype(f32)
@@ -256,8 +258,8 @@
             cotangent = qd_ref[1, :, lanes]
             q_rows[lanes] = query
             d_rows[lanes] = cotangent
-            q_t[:, lanes] = query.astype(f32).T.astype(bf16)
-            d_t[:, lanes] = cotangent.astype(f32).T.astype(bf16)
+            q_t[:, lanes] = query.T
+            d_t[:, lanes] = cotangent.T
         row_places = first + iota((1, ROWS), 1)
         row_starts = starts_of(row_places, lambda j: ends[j])
         first_start = starts_of(first, lambda j: ends[j])
@@ -292,7 +294,7 @@
         delta = jnp.sum(d_t[...].astype(f32) * rounded, axis=0, keepdims=True)
         for h in range(REP):
             lanes = slice(h * HD, (h + 1) * HD)
-            od_ref[0, :, lanes] = rounded[:, lanes].T.astype(bf16)
+            out_refs[s][:, lanes] = rounded[:, lanes].astype(bf16).T
         dq_t[...] = jnp.zeros_like(dq_t)
 
         def add_grad(c, carry):
@@ -307,7 +309,7 @@
         lax.fori_loop(low, high, add_grad, 0)
         for h in range(REP):
             lanes = slice(h * HD, (h + 1) * HD)
-            od_ref[1, :, lanes] = (dq_t[:, lanes] * SCALE).T.astype(bf16)
+            dq_refs[s][:, lanes] = (dq_t[:, lanes] * SCALE).astype(bf16).T
 
     for m in range(N_Q):
         for y in range(N_Y):
@@ -321,8 +323,8 @@
     return pl.pallas_call(
         attention_kernel,
         in_specs=[vmem] * (3 + N_Y),
-        out_specs=[vmem] * (N_Y + N_Q + 1),
-        out_shape=[jax.ShapeDtypeStruct((2, ROWS, QH), bf16)] * N_Y
+        out_specs=[vmem] * (4 + N_Q),
+        out_shape=[jax.ShapeDtypeStruct((n, ROWS, QH), bf16) for n in (2, 3, 3)]
         + [jax.ShapeDtypeStruct((N_Y, ROWS, 2 * HD), bf16)] * N_Q
         + [jax.ShapeDtypeStruct((N_Y, ROWS, HD), f32)],
         scratch_shapes=[
@@ -388,7 +390,7 @@
 
 
 def weight_grad(xt, kv_own, kv_other):
-    steps = 4
+    steps = 2
     return pl.pallas_call(
         weight_grad_kernel,
         grid=(steps,),
@@ -443,35 +445,36 @@
     freq = jnp.asarray(np.concatenate([half, half])[None, :].astype(np.float32))
     dest_dp = dest_dp.reshape(1, ROWS)
 
-    xt = turn(dest_dp, loaded_x)
-    queries, xt = lax.optimization_barrier((queries, xt))
-    qd = split_heads(queries, grad_out)
-    x, qd, xt = lax.optimization_barrier((loaded_x, qd, xt))
+    barrier = lax.optimization_barrier
+
+    pieces = cut(dest_dp, loaded_x, queries, grad_out)
+    x, qd, xt = barrier((loaded_x, pieces[:N_Y], pieces[N_Y:]))
     xt = [xt[0]] + [flip(xt[m], m) for m in range(1, N_Q)]
     qd = [qd[0]] + [along_y(qd[s], s) for s in range(1, N_Y)]
     kv = project(lengths, dest_dp, dest_pos.reshape(1, ROWS), freq, kv_bias, x, kv_weight)
-    kv, xt, qd = lax.optimization_barrier((kv, xt, qd))
+    kv, xt = barrier((kv, xt))
     xt = jnp.stack(xt)
-    kv, xt = lax.optimization_barrier((kv, xt))
+    kv, xt, qd = barrier((kv, xt, qd))
     xt = lax.all_gather(xt, "y", axis=0)
     kv = swap(kv.reshape(-1, CAP, 3 * HD), ("zh", "x", "y", "zl")).reshape(N_DP, N_Y, 2, CAP, 3 * HD)
     kv_other = lax.ppermute(kv, "c", [(0, 1), (1, 0)])
 
-    results = attention(lengths, kv, kv_other, qd)
-    od, dkv, posn = results[:N_Y], results[N_Y : N_Y + N_Q], results[-1]
+    stay, back, ahead, *dkv, posn = attention(lengths, kv, kv_other, qd)
     angle = posn * freq
     cosine = jnp.cos(angle)
     sine = jnp.sin(angle) * jnp.where(jnp.arange(HD) < HD // 2, -1.0, 1.0).astype(f32)
     dkv = [dkv[0]] + [flip(dkv[m], m) for m in range(1, N_Q)]
-    od = [od[0]] + [along_y(od[s], -s) for s in range(1, N_Y)]
-    dkv, od = lax.optimization_barrier((dkv, od))
+    back, ahead = along_y(back, -1), along_y(ahead, 1)
     kv_grad = key_grad(dkv, cosine, sine)
+    kv_grad, back, ahead = barrier((kv_grad, back, ahead))
     kv_grad = swap(kv_grad.reshape(-1, N_Y * CAP, 2 * HD), ("zh", "x", "zl")).reshape(N_DP, 2, N_Y, CAP, 2 * HD)
-    attention_out, query_grad = merge_heads(od)
-    kv_grad, attention_out, query_grad = lax.optimization_barrier((kv_grad, attention_out, query_grad))
     kv_grad_other = lax.ppermute(kv_grad, "c", [(0, 1), (1, 0)])
+    last_dq, last_out = along_y(back[2:], -1), along_y(ahead[2:], 1)
     dw = weight_grad(xt, kv_grad, kv_grad_other)
+    dw, last_dq, last_out = barrier((dw, last_dq, last_out))
     dw = swap(dw, ("zh", "x", "y"))
+    attention_out, query_grad = merge_heads(stay, back, ahead, last_dq, last_out)
+    dw, attention_out, query_grad = barrier((dw, attention_out, query_grad))
     kv_weight_grad = final(dw.reshape(N_DP, HEADS, 2 * SHARE, HD))
     return attention_out, query_grad, kv_weight_grad
 

time: 174 us -> 161 us (0.925)
  Pallas kernels: 48.3 us -> 43.2 us
  starting transfers between devices: 23 us -> 18.7 us
  blocking collectives: 44.9 us -> 42.7 us
    ppermute x6 -> x7, waiting for transfers between devices: 15.3 us -> 8.7 us  [along_y(): return lax.ppermute(array, 'y', [(i, (i + s) % N_Y) for i in range(N_Y)])]
    ppermute x6, waiting for transfers between devices: 6.52 us -> 11.4 us  [flip(): return lax.ppermute(array, Q, [(i, i ^ m) for i in range(N_Q)])]
    ppermute x6, starting transfers between devices: 7.58 us -> 4.07 us  [flip(): return lax.ppermute(array, Q, [(i, i ^ m) for i in range(N_Q)])]
    pallas_call x3 -> x2, Pallas kernels: 9.26 us -> 6.21 us  [the longest x1 3.65 us: cut(): pl.pallas_call(cut_kernel, grid=(steps,), in_specs=[pl.BlockSpec((1, ROWS...]
    all_to_all x1, waiting for transfers between devices: 9.09 us -> 11.9 us  [swap(): return lax.all_to_all(array, axes, split_axis=0, concat_axis=0, tiled=True)]
    pallas_call x1, Pallas kernels: 9.55 us -> 7.03 us  [project(): pl.pallas_call(project_kernel, grid=(D // COLS,), in_specs=[whole(N_DP, N...]
    all_to_all x2, blocking collectives: 44.9 us -> 42.7 us  [swap(): return lax.all_to_all(array, axes, split_axis=0, concat_axis=0, tiled=True)]
    all_to_all x1, starting transfers between devices: 6.24 us -> 4.17 us  [swap(): return lax.all_to_all(array, axes, split_axis=0, concat_axis=0, tiled=True)]
  transfers between devices with their start and end apart: 16 -> 17, of which waited for: 9 -> 9; matrix products, arithmetic and copies ran while one was open for 2% -> 3% of each run, Pallas kernels for 20% -> 23%
where the time goes in v3:
time: 161 us
  Pallas kernels  43.2 us (27%)
  blocking collectives  42.7 us (27%)
  waiting for transfers between devices  34.2 us (21%)
  starting transfers between devices  18.7 us (12%)
  between operations  14.2 us (9%)
  local copies, waits for them, and re-layouts  4.08 us (3%)
  other arithmetic  3.83 us (2%)
    all_to_all x2, blocking collectives, swap(): return lax.all_to_all(array, axes, split_axis=0, concat_axis=0, tiled=True)  42.7 us
    pallas_call x1, Pallas kernels, attention(): pl.pallas_call(attention_kernel, in_specs=[vmem] * (3 + N_Y), out_specs=[...  21.3 us
    all_to_all x1, waiting for transfers between devices, swap(): return lax.all_to_all(array, axes, split_axis=0, concat_axis=0, tiled=True)  11.9 us
    ppermute x6, waiting for transfers between devices, flip(): return lax.ppermute(array, Q, [(i, i ^ m) for i in range(N_Q)])  11.4 us
    ppermute x7, starting transfers between devices, along_y(): return lax.ppermute(array, 'y', [(i, (i + s) % N_Y) for i in range(N_Y)])  10.3 us
    ppermute x7, waiting for transfers between devices, along_y(): return lax.ppermute(array, 'y', [(i, (i + s) % N_Y) for i in range(N_Y)])  8.7 us
    pallas_call x1, Pallas kernels, project(): pl.pallas_call(project_kernel, grid=(D // COLS,), in_specs=[whole(N_DP, N...  7.03 us
    pallas_call x1, Pallas kernels, weight_grad(): pl.pallas_call(weight_grad_kernel, grid=(steps,), in_specs=[pl.BlockSpec(...  4.45 us
  transfers between devices with their start and end apart: 17, of which 9 were waited for; matrix products, arithmetic and copies ran while one was open for 3% of the time, Pallas kernels for 23%

profile of v3, /device:TPU:0, one launch (start us, length us, event | category | flops | bytes accessed | tf_op | source)
XLA Modules:
  0.0 160.8 jit_solution(522353851887851768)
XLA Ops:
  7.2 3.7 %cut.1 = (bf16[2,128,640]{2,1,0:T(8,128)(2,1)}, bf16[2,128,640]{2,1,0:T(8,128)(2,1)}, bf16[2,128,640]{2,1,0:T(8,128)(2,1)}, bf16[2,128,640]{2,1,0:T(8,128)(2,1)}...) custom-call(s32[1,128]{1,0:T(1,128)} %bitcast.24, ...), custom_call_target="tpu_custom_call" | custom-call | flops 2000000000 | bytes 5200000 | tf_op jit(solution)/shard_map/cut/pallas_call | solution.py:97
  10.9 2.1 %collective-permute-start.1 = (bf16[1280,128]{1,0:T(8,128)(2,1)}, bf16[1280,128]{1,0:T(8,128)(2,1)S(1)}, u32[]{:S(2)}, u32[]{:S(2)}) collective-permute-start(bf16[1280,128]{1,0:T(8,128)(2,1)} %get-tuple-element.61), channel_id=1, source_target_pairs={{0,2},{1,3},{2,0},{3,1},{4,6},{5,7},{6,4},{7,5},{8,10},{9,11},{10,... | collective-permute-start | bytes 983048 | tf_op jit(solution)/shard_map/ppermute | solution.py:436
  13.1 1.6 collective-permute-start.3
  14.7 2.9 %collective-permute-start.4 = (bf16[2,128,640]{2,1,0:T(8,128)(2,1)}, bf16[2,128,640]{2,1,0:T(8,128)(2,1)S(1)}, u32[]{:S(2)}, u32[]{:S(2)}) collective-permute-start(bf16[2,128,640]{2,1,0:T(8,128)(2,1)} %get-tuple-element.70), channel_id=1, source_target_pairs={{0,8},{4,12},{8,0},{12,4},{1,9},{5,13},{9,1},{13,5},{2,10},{6,14},... | collective-permute-start | bytes 983048 | tf_op jit(solution)/shard_map/ppermute | solution.py:440
  17.6 0.7 copy.15.lengths_ref
  18.2 1.3 collective-permute-start.5
  19.6 7.0 %project.1 = bf16[8,4,2,16,384]{4,3,2,1,0:T(8,128)(2,1)} custom-call(s32[8,4]{1,0:T(8,128)} %copy.15.lengths_ref, s32[1,128]{1,0:T(1,128)} %bitcast.25, s32[1,128]{1,0:T(1,128)} %bitcast.26, f32[1,128]{1,0:T(1,128)} %constant.8.clone.freq_ref, bf16[1024]{0:T(1024)(128)(2,1)} %bias_ref.1, bf16[128,5120]{1,0:T(8,128)(2,1)} %x_ref.2, bf16[5120,1024]{1,0:T(8,128)(2,1)} %w_ref.1), custom_call_target="tpu_custom_call" | custom-call | flops 1600000000 | bytes 16000000 | tf_op jit(solution)/shard_map/project/pallas_call | solution.py:196
  26.6 1.6 %collective-permute-done.2 = bf16[1280,128]{1,0:T(8,128)(2,1)S(1)} collective-permute-done((bf16[1280,128]{1,0:T(8,128)(2,1)}, bf16[1280,128]{1,0:T(8,128)(2,1)S(1)}, u32[]{:S(2)}, u32[]{:S(2)}) %collective-permute-start.2) | collective-permute-done | bytes 327712 | tf_op jit(solution)/shard_map/ppermute | solution.py:436
  28.2 1.2 pad_maximum_fusion
  29.5 3.1 %collective-permute-done.4.refs_2_ = bf16[2,128,640]{2,1,0:T(8,128)(2,1)S(1)} collective-permute-done((bf16[2,128,640]{2,1,0:T(8,128)(2,1)}, bf16[2,128,640]{2,1,0:T(8,128)(2,1)S(1)}, u32[]{:S(2)}, u32[]{:S(2)}) %collective-permute-start.4) | collective-permute-done | bytes 327712 | tf_op jit(solution)/shard_map/ppermute | solution.py:440
  32.6 25.4 %all_to_all.15 = bf16[64,16,384]{2,1,0:T(8,128)(2,1)S(1)} all-to-all(bf16[64,16,384]{2,1,0:T(8,128)(2,1)S(1)} %bitcast.13), channel_id=1, replica_groups=mesh['zh'=2,'x'=4,'y'=4,'zl'=2,'c'=2] {'zh','x','y','zl'}, dimensions={0} | all-to-all | bytes 1572864 | tf_op jit(solution)/shard_map/all_to_all | solution.py:432
  58.1 2.3 %collective-permute-done.6.kv_other_ref = bf16[8,4,2,16,384]{4,3,2,1,0:T(8,128)(2,1)S(1)} collective-permute-done((bf16[8,4,2,16,384]{4,3,2,1,0:T(8,128)(2,1)S(1)}, bf16[8,4,2,16,384]{4,3,2,1,0:T(8,128)(2,1)S(1)}, u32[]{:S(2)}, u32[]{:S(2)}) %collective-permute-start.6) | collective-permute-done | bytes 786464 | tf_op jit(solution)/shard_map/ppermute | solution.py:460
  60.3 1.0 copy-done.15
  61.3 21.3 %attention.1 = (bf16[2,128,640]{2,1,0:T(8,128)(2,1)}, bf16[3,128,640]{2,1,0:T(8,128)(2,1)}, bf16[3,128,640]{2,1,0:T(8,128)(2,1)}, bf16[4,128,256]{2,1,0:T(8,128)...) custom-call(s32[8,4]{1,0:T(8,128)} %copy.15.lengths_ref, ...), custom_call_target="tpu_custom_call" | custom-call | flops 20000000000 | bytes 8000000 | tf_op jit(solution)/shard_map/attention/pallas_call | solution.py:323
  82.7 2.3 %collective-permute-start.10 = (bf16[3,128,640]{2,1,0:T(8,128)(2,1)}, bf16[3,128,640]{2,1,0:T(8,128)(2,1)S(1)}, u32[]{:S(2)}, u32[]{:S(2)}) collective-permute-start(bf16[3,128,640]{2,1,0:T(8,128)(2,1)} %get-tuple-element.82), channel_id=1, source_target_pairs={{0,12},{4,0},{8,4},{12,8},{1,13},{5,1},{9,5},{13,9},{2,14},{6,2},{... | collective-permute-start | bytes 1474568 | tf_op jit(solution)/shard_map/ppermute | solution.py:440
  85.0 1.9 %collective-permute-start.9 = (bf16[4,128,256]{2,1,0:T(8,128)(2,1)}, bf16[4,128,256]{2,1,0:T(8,128)(2,1)S(1)}, u32[]{:S(2)}, u32[]{:S(2)}) collective-permute-start(bf16[4,128,256]{2,1,0:T(8,128)(2,1)} %get-tuple-element.81), channel_id=1, source_target_pairs={{0,3},{1,2},{2,1},{3,0},{4,7},{5,6},{6,5},{7,4},{8,11},{9,10},{10,... | collective-permute-start | bytes 786440 | tf_op jit(solution)/shard_map/ppermute | solution.py:436
  86.9 2.6 %sine_multiply_fusion = (f32[4,128,128]{2,1,0:T(8,128)}, f32[4,128,128]{2,1,0:T(8,128)}) fusion(f32[4,128,128]{2,1,0:T(8,128)} %get-tuple-element.77, f32[128]{0:T(128)S(1)} %compare_select_fusion, f32[128]{0:T(128)S(1)} %copy-done.14), kind=kLoop, calls=%fused_computation.1 | loop fusion | flops 131072 | bytes 787456 | tf_op jit(solution)/shard_map/mul | solution.py:465
  89.5 4.8 %collective-permute-done.8.refs_2_ = bf16[4,128,256]{2,1,0:T(8,128)(2,1)S(1)} collective-permute-done((bf16[4,128,256]{2,1,0:T(8,128)(2,1)}, bf16[4,128,256]{2,1,0:T(8,128)(2,1)S(1)}, u32[]{:S(2)}, u32[]{:S(2)}) %collective-permute-start.8) | collective-permute-done | bytes 262176 | tf_op jit(solution)/shard_map/ppermute | solution.py:436
  94.3 4.9 %collective-permute-done.9.refs_3_ = bf16[4,128,256]{2,1,0:T(8,128)(2,1)S(1)} collective-permute-done((bf16[4,128,256]{2,1,0:T(8,128)(2,1)}, bf16[4,128,256]{2,1,0:T(8,128)(2,1)S(1)}, u32[]{:S(2)}, u32[]{:S(2)}) %collective-permute-start.9) | collective-permute-done | bytes 262176 | tf_op jit(solution)/shard_map/ppermute | solution.py:436
  99.2 0.7 copy-done.10
  99.9 2.3 %key_grad.1 = bf16[8,2,4,16,256]{4,3,2,1,0:T(8,128)(2,1)} custom-call(f32[4,128,128]{2,1,0:T(8,128)} %get-tuple-element.98.cos_ref, f32[4,128,128]{2,1,0:T(8,128)} %get-tuple-element.97.sin_ref, bf16[4,128,256]{2,1,0:T(8,128)(2,1)} %get-tuple-element.78.refs_0_, bf16[4,128,256]{2,1,0:T(8,128)(2,1)} %copy-done.8, bf16[4,128,256]{2,1,0:T(8,128)(2,1)} %copy-done.9, ...), custom_call_target="tpu_custom_call" | custom-call | tf_op jit(solution)/shard_map/key_grad/pallas_call | solution.py:368
  102.2 3.9 %collective-permute-done.10.back_ref = bf16[3,128,640]{2,1,0:T(8,128)(2,1)S(1)} collective-permute-done((bf16[3,128,640]{2,1,0:T(8,128)(2,1)}, bf16[3,128,640]{2,1,0:T(8,128)(2,1)S(1)}, u32[]{:S(2)}, u32[]{:S(2)}) %collective-permute-start.10) | collective-permute-done | bytes 491552 | tf_op jit(solution)/shard_map/ppermute | solution.py:440
  106.1 1.1 collective-permute-done.11.ahead_ref
  107.2 17.3 %all_to_all.16 = bf16[16,64,256]{2,1,0:T(8,128)(2,1)S(1)} all-to-all(bf16[16,64,256]{2,1,0:T(8,128)(2,1)} %bitcast.15), channel_id=1, replica_groups=mesh['zh'=2,'x'=4,'y'=4,'zl'=2,'c'=2] {'zh','x','zl'}, dimensions={0} | all-to-all | bytes 1048576 | tf_op jit(solution)/shard_map/all_to_all | solution.py:432
  125.0 1.7 %collective-permute-start.14 = (bf16[1,128,640]{2,1,0:T(8,128)(2,1)S(1)}, bf16[1,128,640]{2,1,0:T(8,128)(2,1)S(1)}, u32[]{:S(2)}, u32[]{:S(2)}) collective-permute-start(bf16[1,128,640]{2,1,0:T(8,128)(2,1)S(1)} %slice.7), channel_id=1, source_target_pairs={{0,4},{4,8},{8,12},{12,0},{1,5},{5,9},{9,13},{13,1},{2,6},{6,10},{... | collective-permute-start | bytes 491528 | tf_op jit(solution)/shard_map/ppermute | solution.py:440
  126.8 0.8 copy-done.6
  127.6 4.5 %weight_grad.1 = bf16[32,80,128]{2,1,0:T(8,128)(2,1)} custom-call(bf16[8,2,4,16,256]{4,3,2,1,0:T(8,128)(2,1)} %bitcast.17, bf16[8,2,4,16,256]{4,3,2,1,0:T(8,128)(2,1)} %copy-done.6, bf16[4,4,1280,128]{3,2,1,0:T(8,128)(2,1)} %bitcast.12), custom_call_target="tpu_custom_call" | custom-call | flops 1400000000 | bytes 7000000 | tf_op jit(solution)/shard_map/weight_grad/pallas_call | solution.py:394
  132.7 4.2 %all-to-all-start.2 = ((bf16[32,80,128]{2,1,0:T(8,128)(2,1)}), bf16[32,80,128]{2,1,0:T(8,128)(2,1)S(1)}, u32[]{:S(2)}, u32[]{:S(2)}) async-start(bf16[32,80,128]{2,1,0:T(8,128)(2,1)} %weight_grad.1), calls=%async_computation.2 | async-start | bytes 1310720 | tf_op jit(solution)/shard_map/all_to_all | solution.py:432
  136.9 2.6 %merge_heads.1 = (bf16[128,2560]{1,0:T(8,128)(2,1)}, bf16[128,2560]{1,0:T(8,128)(2,1)}) custom-call(bf16[2,128,640]{2,1,0:T(8,128)(2,1)} %get-tuple-element.89.stay_ref, bf16[3,128,640]{2,1,0:T(8,128)(2,1)} %copy-done.3, bf16[3,128,640]{2,1,0:T(8,128)(2,1)} %copy-done.4, bf16[1,128,640]{2,1,0:T(8,128)(2,1)} %copy-done.11, bf16[1,128,640]{2,1,0:T(8,128)(2,1)} %copy-done.12), custom_call_target="tpu_custom_call" | custom-call | tf_op jit(solution)/shard_map/merge_heads/pallas_call | solution.py:133
  139.4 11.9 %all-to-all-done.2 = bf16[32,80,128]{2,1,0:T(8,128)(2,1)S(1)} async-done(((bf16[32,80,128]{2,1,0:T(8,128)(2,1)}), bf16[32,80,128]{2,1,0:T(8,128)(2,1)S(1)}, u32[]{:S(2)}, u32[]{:S(2)}) %all-to-all-start.2) | async-done | bytes 655392 | tf_op jit(solution)/shard_map/all_to_all | solution.py:432
  151.3 0.8 copy-done.1
  152.1 1.8 %final_sum.1 = f32[40,1024]{1,0:T(8,128)} custom-call(bf16[8,4,80,128]{3,2,1,0:T(8,128)(2,1)} %bitcast.14), custom_call_target="tpu_custom_call" | custom-call | tf_op jit(solution)/shard_map/final_sum/pallas_call | solution.py:422
  (56 shorter events, 1.5 us)
Async XLA Ops:
  7.2 119.6 %all-gather.3.cloned.1.call-start = ((), (), s32[]{:S(2)}) async-start(), calls=%async_computation.3 | async-start | bytes 6553600 | tf_op jit(solution)/shard_map/all_gather | solution.py:458
  7.2 10.3 %copy-start.13 = (s32[8,4]{0,1:T(4,128)S(1)}, s32[8,4]{0,1:T(4,128)}, u32[]{:S(2)}) copy-start(s32[8,4]{0,1:T(4,128)} %param.16) | copy-start | bytes 388
  10.9 7.4 %collective-permute-start = (bf16[1280,128]{1,0:T(8,128)(2,1)}, bf16[1280,128]{1,0:T(8,128)(2,1)S(1)}, u32[]{:S(2)}, u32[]{:S(2)}) collective-permute-start(bf16[1280,128]{1,0:T(8,128)(2,1)} %get-tuple-element.60), channel_id=1, source_target_pairs={{0,1},{1,0},{2,3},{3,2},{4,5},{5,4},{6,7},{7,6},{8,9},{9,8},{10,11... | collective-permute-start | bytes 983048 | tf_op jit(solution)/shard_map/ppermute | solution.py:436
  10.9 15.7 %collective-permute-start.1 = (bf16[1280,128]{1,0:T(8,128)(2,1)}, bf16[1280,128]{1,0:T(8,128)(2,1)S(1)}, u32[]{:S(2)}, u32[]{:S(2)}) collective-permute-start(bf16[1280,128]{1,0:T(8,128)(2,1)} %get-tuple-element.61), channel_id=1, source_target_pairs={{0,2},{1,3},{2,0},{3,1},{4,6},{5,7},{6,4},{7,5},{8,10},{9,11},{10,... | collective-permute-start | bytes 983048 | tf_op jit(solution)/shard_map/ppermute | solution.py:436
  13.0 15.2 %collective-permute-start.2 = (bf16[1280,128]{1,0:T(8,128)(2,1)}, bf16[1280,128]{1,0:T(8,128)(2,1)S(1)}, u32[]{:S(2)}, u32[]{:S(2)}) collective-permute-start(bf16[1280,128]{1,0:T(8,128)(2,1)} %get-tuple-element.62), channel_id=1, source_target_pairs={{0,3},{1,2},{2,1},{3,0},{4,7},{5,6},{6,5},{7,4},{8,11},{9,10},{10,... | collective-permute-start | bytes 983048 | tf_op jit(solution)/shard_map/ppermute | solution.py:436
  13.1 16.4 %collective-permute-start.3 = (bf16[2,128,640]{2,1,0:T(8,128)(2,1)}, bf16[2,128,640]{2,1,0:T(8,128)(2,1)S(1)}, u32[]{:S(2)}, u32[]{:S(2)}) collective-permute-start(bf16[2,128,640]{2,1,0:T(8,128)(2,1)} %get-tuple-element.69), channel_id=1, source_target_pairs={{0,4},{4,8},{8,12},{12,0},{1,5},{5,9},{9,13},{13,1},{2,6},{6,10},{... | collective-permute-start | bytes 983048 | tf_op jit(solution)/shard_map/ppermute | solution.py:440
  14.7 17.9 %collective-permute-start.4 = (bf16[2,128,640]{2,1,0:T(8,128)(2,1)}, bf16[2,128,640]{2,1,0:T(8,128)(2,1)S(1)}, u32[]{:S(2)}, u32[]{:S(2)}) collective-permute-start(bf16[2,128,640]{2,1,0:T(8,128)(2,1)} %get-tuple-element.70), channel_id=1, source_target_pairs={{0,8},{4,12},{8,0},{12,4},{1,9},{5,13},{9,1},{13,5},{2,10},{6,14},... | collective-permute-start | bytes 983048 | tf_op jit(solution)/shard_map/ppermute | solution.py:440
  18.2 14.3 %collective-permute-start.5 = (bf16[2,128,640]{2,1,0:T(8,128)(2,1)}, bf16[2,128,640]{2,1,0:T(8,128)(2,1)S(1)}, u32[]{:S(2)}, u32[]{:S(2)}) collective-permute-start(bf16[2,128,640]{2,1,0:T(8,128)(2,1)} %get-tuple-element.71), channel_id=1, source_target_pairs={{0,12},{4,0},{8,4},{12,8},{1,13},{5,1},{9,5},{13,9},{2,14},{6,2},{... | collective-permute-start | bytes 983048 | tf_op jit(solution)/shard_map/ppermute | solution.py:440
  19.6 8.7 %copy-start.7 = (bf16[1280,128]{1,0:T(8,128)(2,1)S(1)}, bf16[1280,128]{1,0:T(8,128)(2,1)}, u32[]{:S(2)}) copy-start(bf16[1280,128]{1,0:T(8,128)(2,1)} %get-tuple-element.64) | copy-start | bytes 983044
  29.5 3.1 %copy-start = (bf16[8,4,2,16,384]{4,3,2,1,0:T(8,128)(2,1)S(1)}, bf16[8,4,2,16,384]{4,3,2,1,0:T(8,128)(2,1)}, u32[]{:S(2)}) copy-start(bf16[8,4,2,16,384]{4,3,2,1,0:T(8,128)(2,1)} %project.1) | copy-start | bytes 2359300
  29.5 28.5 %copy-start.16 = (bf16[2,128,640]{2,1,0:T(8,128)(2,1)}, bf16[2,128,640]{2,1,0:T(8,128)(2,1)S(1)}, u32[]{:S(2)}) copy-start(bf16[2,128,640]{2,1,0:T(8,128)(2,1)S(1)} %collective-permute-done.3.refs_1_) | copy-start | bytes 983044
  32.6 25.4 %copy-start.17 = (bf16[2,128,640]{2,1,0:T(8,128)(2,1)}, bf16[2,128,640]{2,1,0:T(8,128)(2,1)S(1)}, u32[]{:S(2)}) copy-start(bf16[2,128,640]{2,1,0:T(8,128)(2,1)S(1)} %collective-permute-done.4.refs_2_) | copy-start | bytes 983044
  32.6 25.4 %copy-start.18 = (bf16[2,128,640]{2,1,0:T(8,128)(2,1)}, bf16[2,128,640]{2,1,0:T(8,128)(2,1)S(1)}, u32[]{:S(2)}) copy-start(bf16[2,128,640]{2,1,0:T(8,128)(2,1)S(1)} %collective-permute-done.5.refs_3_) | copy-start | bytes 983044
  58.0 2.4 %copy-start.5 = (bf16[64,16,384]{2,1,0:T(8,128)(2,1)}, bf16[64,16,384]{2,1,0:T(8,128)(2,1)S(1)}, u32[]{:S(2)}) copy-start(bf16[64,16,384]{2,1,0:T(8,128)(2,1)S(1)} %all_to_all.15) | copy-start | bytes 2359300
  58.0 28.9 %copy-start.14 = (f32[128]{0:T(128)S(1)}, f32[128]{0:T(128)}, u32[]{:S(2)}) copy-start(f32[128]{0:T(128)} %constant.9) | copy-start | bytes 1540
  58.0 2.4 %collective-permute-start.6 = (bf16[8,4,2,16,384]{4,3,2,1,0:T(8,128)(2,1)S(1)}, bf16[8,4,2,16,384]{4,3,2,1,0:T(8,128)(2,1)S(1)}, u32[]{:S(2)}, u32[]{:S(2)}) collective-permute-start(bf16[8,4,2,16,384]{4,3,2,1,0:T(8,128)(2,1)S(1)} %bitcast.18), channel_id=1, source_target_pairs={{0,1},{1,0},{2,3},{3,2},{4,5},{5,4},{6,7},{7,6},{8,9},{9,8},{10,11... | collective-permute-start | bytes 2359304 | tf_op jit(solution)/shard_map/ppermute | solution.py:460
  82.7 23.4 %collective-permute-start.10 = (bf16[3,128,640]{2,1,0:T(8,128)(2,1)}, bf16[3,128,640]{2,1,0:T(8,128)(2,1)S(1)}, u32[]{:S(2)}, u32[]{:S(2)}) collective-permute-start(bf16[3,128,640]{2,1,0:T(8,128)(2,1)} %get-tuple-element.82), channel_id=1, source_target_pairs={{0,12},{4,0},{8,4},{12,8},{1,13},{5,1},{9,5},{13,9},{2,14},{6,2},{... | collective-permute-start | bytes 1474568 | tf_op jit(solution)/shard_map/ppermute | solution.py:440
  85.0 22.2 %collective-permute-start.11 = (bf16[3,128,640]{2,1,0:T(8,128)(2,1)}, bf16[3,128,640]{2,1,0:T(8,128)(2,1)S(1)}, u32[]{:S(2)}, u32[]{:S(2)}) collective-permute-start(bf16[3,128,640]{2,1,0:T(8,128)(2,1)} %get-tuple-element.83), channel_id=1, source_target_pairs={{0,4},{4,8},{8,12},{12,0},{1,5},{5,9},{9,13},{13,1},{2,6},{6,10},{... | collective-permute-start | bytes 1474568 | tf_op jit(solution)/shard_map/ppermute | solution.py:440
  85.0 4.5 %collective-permute-start.7 = (bf16[4,128,256]{2,1,0:T(8,128)(2,1)}, bf16[4,128,256]{2,1,0:T(8,128)(2,1)S(1)}, u32[]{:S(2)}, u32[]{:S(2)}) collective-permute-start(bf16[4,128,256]{2,1,0:T(8,128)(2,1)} %get-tuple-element.79), channel_id=1, source_target_pairs={{0,1},{1,0},{2,3},{3,2},{4,5},{5,4},{6,7},{7,6},{8,9},{9,8},{10,11... | collective-permute-start | bytes 786440 | tf_op jit(solution)/shard_map/ppermute | solution.py:436
  85.0 9.3 %collective-permute-start.8 = (bf16[4,128,256]{2,1,0:T(8,128)(2,1)}, bf16[4,128,256]{2,1,0:T(8,128)(2,1)S(1)}, u32[]{:S(2)}, u32[]{:S(2)}) collective-permute-start(bf16[4,128,256]{2,1,0:T(8,128)(2,1)} %get-tuple-element.80), channel_id=1, source_target_pairs={{0,2},{1,3},{2,0},{3,1},{4,6},{5,7},{6,4},{7,5},{8,10},{9,11},{10,... | collective-permute-start | bytes 786440 | tf_op jit(solution)/shard_map/ppermute | solution.py:436
  85.0 14.2 %collective-permute-start.9 = (bf16[4,128,256]{2,1,0:T(8,128)(2,1)}, bf16[4,128,256]{2,1,0:T(8,128)(2,1)S(1)}, u32[]{:S(2)}, u32[]{:S(2)}) collective-permute-start(bf16[4,128,256]{2,1,0:T(8,128)(2,1)} %get-tuple-element.81), channel_id=1, source_target_pairs={{0,3},{1,2},{2,1},{3,0},{4,7},{5,6},{6,5},{7,4},{8,11},{9,10},{10,... | collective-permute-start | bytes 786440 | tf_op jit(solution)/shard_map/ppermute | solution.py:436
  89.5 9.7 %copy-start.8 = (bf16[4,128,256]{2,1,0:T(8,128)(2,1)}, bf16[4,128,256]{2,1,0:T(8,128)(2,1)S(1)}, u32[]{:S(2)}) copy-start(bf16[4,128,256]{2,1,0:T(8,128)(2,1)S(1)} %collective-permute-done.7.refs_1_) | copy-start | bytes 786436
  94.3 4.9 %copy-start.9 = (bf16[4,128,256]{2,1,0:T(8,128)(2,1)}, bf16[4,128,256]{2,1,0:T(8,128)(2,1)S(1)}, u32[]{:S(2)}) copy-start(bf16[4,128,256]{2,1,0:T(8,128)(2,1)S(1)} %collective-permute-done.8.refs_2_) | copy-start | bytes 786436
  106.1 25.9 %copy-start.3 = (bf16[3,128,640]{2,1,0:T(8,128)(2,1)}, bf16[3,128,640]{2,1,0:T(8,128)(2,1)S(1)}, u32[]{:S(2)}) copy-start(bf16[3,128,640]{2,1,0:T(8,128)(2,1)S(1)} %collective-permute-done.10.back_ref) | copy-start | bytes 1474564
  107.2 24.8 %copy-start.4 = (bf16[3,128,640]{2,1,0:T(8,128)(2,1)}, bf16[3,128,640]{2,1,0:T(8,128)(2,1)S(1)}, u32[]{:S(2)}) copy-start(bf16[3,128,640]{2,1,0:T(8,128)(2,1)S(1)} %collective-permute-done.11.ahead_ref) | copy-start | bytes 1474564
  124.5 2.2 %copy-start.2 = (bf16[16,64,256]{2,1,0:T(8,128)(2,1)}, bf16[16,64,256]{2,1,0:T(8,128)(2,1)S(1)}, u32[]{:S(2)}) copy-start(bf16[16,64,256]{2,1,0:T(8,128)(2,1)S(1)} %all_to_all.16) | copy-start | bytes 1572868
  124.6 2.2 %collective-permute-start.12 = (bf16[8,2,4,16,256]{4,3,2,1,0:T(8,128)(2,1)S(1)}, bf16[8,2,4,16,256]{4,3,2,1,0:T(8,128)(2,1)S(1)}, u32[]{:S(2)}, u32[]{:S(2)}) collective-permute-start(bf16[8,2,4,16,256]{4,3,2,1,0:T(8,128)(2,1)S(1)} %bitcast.16), channel_id=1, source_target_pairs={{0,1},{1,0},{2,3},{3,2},{4,5},{5,4},{6,7},{7,6},{8,9},{9,8},{10,11... | collective-permute-start | bytes 1572872 | tf_op jit(solution)/shard_map/ppermute | solution.py:471
  124.6 7.4 %collective-permute-start.13 = (bf16[1,128,640]{2,1,0:T(8,128)(2,1)S(1)}, bf16[1,128,640]{2,1,0:T(8,128)(2,1)S(1)}, u32[]{:S(2)}, u32[]{:S(2)}) collective-permute-start(bf16[1,128,640]{2,1,0:T(8,128)(2,1)S(1)} %slice.6), channel_id=1, source_target_pairs={{0,12},{4,0},{8,4},{12,8},{1,13},{5,1},{9,5},{13,9},{2,14},{6,2},{... | collective-permute-start | bytes 491528 | tf_op jit(solution)/shard_map/ppermute | solution.py:440
  125.0 7.6 %collective-permute-start.14 = (bf16[1,128,640]{2,1,0:T(8,128)(2,1)S(1)}, bf16[1,128,640]{2,1,0:T(8,128)(2,1)S(1)}, u32[]{:S(2)}, u32[]{:S(2)}) collective-permute-start(bf16[1,128,640]{2,1,0:T(8,128)(2,1)S(1)} %slice.7), channel_id=1, source_target_pairs={{0,4},{4,8},{8,12},{12,0},{1,5},{5,9},{9,13},{13,1},{2,6},{6,10},{... | collective-permute-start | bytes 491528 | tf_op jit(solution)/shard_map/ppermute | solution.py:440
  132.0 4.8 %copy-start.11 = (bf16[1,128,640]{2,1,0:T(8,128)(2,1)}, bf16[1,128,640]{2,1,0:T(8,128)(2,1)S(1)}, u32[]{:S(2)}) copy-start(bf16[1,128,640]{2,1,0:T(8,128)(2,1)S(1)} %collective-permute-done.13.dq_ref) | copy-start | bytes 491524
  132.7 4.2 %copy-start.12 = (bf16[1,128,640]{2,1,0:T(8,128)(2,1)}, bf16[1,128,640]{2,1,0:T(8,128)(2,1)S(1)}, u32[]{:S(2)}) copy-start(bf16[1,128,640]{2,1,0:T(8,128)(2,1)S(1)} %collective-permute-done.14.out_ref) | copy-start | bytes 491524
  132.7 18.6 %all-to-all-start.2 = ((bf16[32,80,128]{2,1,0:T(8,128)(2,1)}), bf16[32,80,128]{2,1,0:T(8,128)(2,1)S(1)}, u32[]{:S(2)}, u32[]{:S(2)}) async-start(bf16[32,80,128]{2,1,0:T(8,128)(2,1)} %weight_grad.1), calls=%async_computation.2 | async-start | bytes 1310720 | tf_op jit(solution)/shard_map/all_to_all | solution.py:432
  (4 other events, 3.3 us)
Sparse Core Ops, SparseCore 0:
  32.7 72.9 all-gather.2

commit v4 on v3

--- a/solution.py
+++ b/solution.py
@@ -466,12 +466,12 @@
     dkv = [dkv[0]] + [flip(dkv[m], m) for m in range(1, N_Q)]
     back, ahead = along_y(back, -1), along_y(ahead, 1)
     kv_grad = key_grad(dkv, cosine, sine)
-    kv_grad, back, ahead = barrier((kv_grad, back, ahead))
     kv_grad = swap(kv_grad.reshape(-1, N_Y * CAP, 2 * HD), ("zh", "x", "zl")).reshape(N_DP, 2, N_Y, CAP, 2 * HD)
+    last_dq, last_out = along_y(back[2:], -1), along_y(ahead[2:], 1)
+    kv_grad, last_dq, last_out = barrier((kv_grad, last_dq, last_out))
     kv_grad_other = lax.ppermute(kv_grad, "c", [(0, 1), (1, 0)])
-    last_dq, last_out = along_y(back[2:], -1), along_y(ahead[2:], 1)
     dw = weight_grad(xt, kv_grad, kv_grad_other)
-    dw, last_dq, last_out = barrier((dw, last_dq, last_out))
+    dw, back, ahead = barrier((dw, back, ahead))
     dw = swap(dw, ("zh", "x", "y"))
     attention_out, query_grad = merge_heads(stay, back, ahead, last_dq, last_out)
     dw, attention_out, query_grad = barrier((dw, attention_out, query_grad))

time: 161 us -> 154 us (0.957)
  blocking collectives: 42.7 us -> 25.4 us
  starting transfers between devices: 18.7 us -> 24.1 us
  waiting for transfers between devices: 34.2 us -> 38.5 us
    all_to_all x2 -> x1, blocking collectives: 42.7 us -> 25.4 us  [swap(): return lax.all_to_all(array, axes, split_axis=0, concat_axis=0, tiled=True)]
    all_to_all x1 -> x2, starting transfers between devices: 4.17 us -> 9.62 us  [swap(): return lax.all_to_all(array, axes, split_axis=0, concat_axis=0, tiled=True)]
    ppermute x7, waiting for transfers between devices: 8.7 us -> 12.3 us  [along_y(): return lax.ppermute(array, 'y', [(i, (i + s) % N_Y) for i in range(N_Y)])]
    ppermute x6, waiting for transfers between devices: 11.4 us -> 8.82 us  [flip(): return lax.ppermute(array, Q, [(i, i ^ m) for i in range(N_Q)])]
    ppermute x1, waiting for transfers between devices: 0.01 us -> 1.91 us  [shards(): kv_grad_other = lax.ppermute(kv_grad, 'c', [(0, 1), (1, 0)])]
    all_to_all x1 -> x2, waiting for transfers between devices: 11.9 us -> 13.1 us  [swap(): return lax.all_to_all(array, axes, split_axis=0, concat_axis=0, tiled=True)]
  transfers between devices with their start and end apart: 17 -> 18, of which waited for: 9 -> 11; matrix products, arithmetic and copies ran while one was open for 3% -> 3% of each run, Pallas kernels for 23% -> 22%
where the time goes in v4:
time: 154 us; the launch traced here: 153 us
  Pallas kernels  43.2 us (28%)
  waiting for transfers between devices  38.5 us (25%)
  blocking collectives  25.4 us (16%)
  starting transfers between devices  24.1 us (16%)
  between operations  14.2 us (9%)
  local copies, waits for them, and re-layouts  4.04 us (3%)
  other arithmetic  3.86 us (3%)
    all_to_all x1, blocking collectives, swap(): return lax.all_to_all(array, axes, split_axis=0, concat_axis=0, tiled=True)  25.4 us
    pallas_call x1, Pallas kernels, attention(): pl.pallas_call(attention_kernel, in_specs=[vmem] * (3 + N_Y), out_specs=[...  21.3 us
    all_to_all x2, waiting for transfers between devices, swap(): return lax.all_to_all(array, axes, split_axis=0, concat_axis=0, tiled=True)  13.1 us
    ppermute x7, waiting for transfers between devices, along_y(): return lax.ppermute(array, 'y', [(i, (i + s) % N_Y) for i in range(N_Y)])  12.3 us
    ppermute x7, starting transfers between devices, along_y(): return lax.ppermute(array, 'y', [(i, (i + s) % N_Y) for i in range(N_Y)])  10.3 us
    all_to_all x2, starting transfers between devices, swap(): return lax.all_to_all(array, axes, split_axis=0, concat_axis=0, tiled=True)  9.62 us
    ppermute x6, waiting for transfers between devices, flip(): return lax.ppermute(array, Q, [(i, i ^ m) for i in range(N_Q)])  8.82 us
    pallas_call x1, Pallas kernels, project(): pl.pallas_call(project_kernel, grid=(D // COLS,), in_specs=[whole(N_DP, N...  7.02 us
  transfers between devices with their start and end apart: 18, of which 11 were waited for; matrix products, arithmetic and copies ran while one was open for 3% of the time, Pallas kernels for 22%

profile of v4, /device:TPU:0, one launch (start us, length us, event | category | flops | bytes accessed | tf_op | source)
XLA Modules:
  0.0 153.2 jit_solution(17160454331720933175)
XLA Ops:
  7.2 3.6 %cut.1 = (bf16[2,128,640]{2,1,0:T(8,128)(2,1)}, bf16[2,128,640]{2,1,0:T(8,128)(2,1)}, bf16[2,128,640]{2,1,0:T(8,128)(2,1)}, bf16[2,128,640]{2,1,0:T(8,128)(2,1)}...) custom-call(s32[1,128]{1,0:T(1,128)} %bitcast.24, ...), custom_call_target="tpu_custom_call" | custom-call | flops 2000000000 | bytes 5200000 | tf_op jit(solution)/shard_map/cut/pallas_call | solution.py:97
  10.9 2.1 %collective-permute-start.1 = (bf16[1280,128]{1,0:T(8,128)(2,1)}, bf16[1280,128]{1,0:T(8,128)(2,1)S(1)}, u32[]{:S(2)}, u32[]{:S(2)}) collective-permute-start(bf16[1280,128]{1,0:T(8,128)(2,1)} %get-tuple-element.61), channel_id=1, source_target_pairs={{0,2},{1,3},{2,0},{3,1},{4,6},{5,7},{6,4},{7,5},{8,10},{9,11},{10,... | collective-permute-start | bytes 983048 | tf_op jit(solution)/shard_map/ppermute | solution.py:436
  13.1 1.6 %collective-permute-start.3 = (bf16[2,128,640]{2,1,0:T(8,128)(2,1)}, bf16[2,128,640]{2,1,0:T(8,128)(2,1)S(1)}, u32[]{:S(2)}, u32[]{:S(2)}) collective-permute-start(bf16[2,128,640]{2,1,0:T(8,128)(2,1)} %get-tuple-element.69), channel_id=1, source_target_pairs={{0,4},{4,8},{8,12},{12,0},{1,5},{5,9},{9,13},{13,1},{2,6},{6,10},{... | collective-permute-start | bytes 983048 | tf_op jit(solution)/shard_map/ppermute | solution.py:440
  14.7 2.9 %collective-permute-start.4 = (bf16[2,128,640]{2,1,0:T(8,128)(2,1)}, bf16[2,128,640]{2,1,0:T(8,128)(2,1)S(1)}, u32[]{:S(2)}, u32[]{:S(2)}) collective-permute-start(bf16[2,128,640]{2,1,0:T(8,128)(2,1)} %get-tuple-element.70), channel_id=1, source_target_pairs={{0,8},{4,12},{8,0},{12,4},{1,9},{5,13},{9,1},{13,5},{2,10},{6,14},... | collective-permute-start | bytes 983048 | tf_op jit(solution)/shard_map/ppermute | solution.py:440
  18.2 1.3 collective-permute-start.5
  19.6 7.0 %project.1 = bf16[8,4,2,16,384]{4,3,2,1,0:T(8,128)(2,1)} custom-call(s32[8,4]{1,0:T(8,128)} %copy.15.lengths_ref, s32[1,128]{1,0:T(1,128)} %bitcast.25, s32[1,128]{1,0:T(1,128)} %bitcast.26, f32[1,128]{1,0:T(1,128)} %constant.8.clone.freq_ref, bf16[1024]{0:T(1024)(128)(2,1)} %bias_ref.1, bf16[128,5120]{1,0:T(8,128)(2,1)} %x_ref.2, bf16[5120,1024]{1,0:T(8,128)(2,1)} %w_ref.1), custom_call_target="tpu_custom_call" | custom-call | flops 1600000000 | bytes 16000000 | tf_op jit(solution)/shard_map/project/pallas_call | solution.py:196
  26.6 1.6 %collective-permute-done.2 = bf16[1280,128]{1,0:T(8,128)(2,1)S(1)} collective-permute-done((bf16[1280,128]{1,0:T(8,128)(2,1)}, bf16[1280,128]{1,0:T(8,128)(2,1)S(1)}, u32[]{:S(2)}, u32[]{:S(2)}) %collective-permute-start.2) | collective-permute-done | bytes 327712 | tf_op jit(solution)/shard_map/ppermute | solution.py:436
  28.2 1.3 pad_maximum_fusion
  29.5 3.0 %collective-permute-done.4.refs_2_ = bf16[2,128,640]{2,1,0:T(8,128)(2,1)S(1)} collective-permute-done((bf16[2,128,640]{2,1,0:T(8,128)(2,1)}, bf16[2,128,640]{2,1,0:T(8,128)(2,1)S(1)}, u32[]{:S(2)}, u32[]{:S(2)}) %collective-permute-start.4) | collective-permute-done | bytes 327712 | tf_op jit(solution)/shard_map/ppermute | solution.py:440
  32.6 25.4 %all_to_all.15 = bf16[64,16,384]{2,1,0:T(8,128)(2,1)S(1)} all-to-all(bf16[64,16,384]{2,1,0:T(8,128)(2,1)S(1)} %bitcast.13), channel_id=1, replica_groups=mesh['zh'=2,'x'=4,'y'=4,'zl'=2,'c'=2] {'zh','x','y','zl'}, dimensions={0} | all-to-all | bytes 1572864 | tf_op jit(solution)/shard_map/all_to_all | solution.py:432
  58.1 2.3 %collective-permute-done.6.kv_other_ref = bf16[8,4,2,16,384]{4,3,2,1,0:T(8,128)(2,1)S(1)} collective-permute-done((bf16[8,4,2,16,384]{4,3,2,1,0:T(8,128)(2,1)S(1)}, bf16[8,4,2,16,384]{4,3,2,1,0:T(8,128)(2,1)S(1)}, u32[]{:S(2)}, u32[]{:S(2)}) %collective-permute-start.6) | collective-permute-done | bytes 786464 | tf_op jit(solution)/shard_map/ppermute | solution.py:460
  60.3 1.0 copy-done.15
  61.3 21.3 %attention.1 = (bf16[2,128,640]{2,1,0:T(8,128)(2,1)}, bf16[3,128,640]{2,1,0:T(8,128)(2,1)}, bf16[3,128,640]{2,1,0:T(8,128)(2,1)}, bf16[4,128,256]{2,1,0:T(8,128)...) custom-call(s32[8,4]{1,0:T(8,128)} %copy.15.lengths_ref, ...), custom_call_target="tpu_custom_call" | custom-call | flops 20000000000 | bytes 8000000 | tf_op jit(solution)/shard_map/attention/pallas_call | solution.py:323
  83.6 0.9 collective-permute-start.9
  84.5 2.3 %collective-permute-start.10 = (bf16[3,128,640]{2,1,0:T(8,128)(2,1)}, bf16[3,128,640]{2,1,0:T(8,128)(2,1)S(1)}, u32[]{:S(2)}, u32[]{:S(2)}) collective-permute-start(bf16[3,128,640]{2,1,0:T(8,128)(2,1)} %get-tuple-element.82), channel_id=1, source_target_pairs={{0,12},{4,0},{8,4},{12,8},{1,13},{5,1},{9,5},{13,9},{2,14},{6,2},{... | collective-permute-start | bytes 1474568 | tf_op jit(solution)/shard_map/ppermute | solution.py:440
  86.9 2.6 %sine_multiply_fusion = (f32[4,128,128]{2,1,0:T(8,128)}, f32[4,128,128]{2,1,0:T(8,128)}) fusion(f32[4,128,128]{2,1,0:T(8,128)} %get-tuple-element.77, f32[128]{0:T(128)S(1)} %compare_select_fusion, f32[128]{0:T(128)S(1)} %copy-done.14), kind=kLoop, calls=%fused_computation.1 | loop fusion | flops 131072 | bytes 787456 | tf_op jit(solution)/shard_map/mul | solution.py:465
  89.5 2.7 %collective-permute-done.8.refs_2_ = bf16[4,128,256]{2,1,0:T(8,128)(2,1)S(1)} collective-permute-done((bf16[4,128,256]{2,1,0:T(8,128)(2,1)}, bf16[4,128,256]{2,1,0:T(8,128)(2,1)S(1)}, u32[]{:S(2)}, u32[]{:S(2)}) %collective-permute-start.8) | collective-permute-done | bytes 262176 | tf_op jit(solution)/shard_map/ppermute | solution.py:436
  92.2 4.5 %collective-permute-done.9.refs_3_ = bf16[4,128,256]{2,1,0:T(8,128)(2,1)S(1)} collective-permute-done((bf16[4,128,256]{2,1,0:T(8,128)(2,1)}, bf16[4,128,256]{2,1,0:T(8,128)(2,1)S(1)}, u32[]{:S(2)}, u32[]{:S(2)}) %collective-permute-start.9) | collective-permute-done | bytes 262176 | tf_op jit(solution)/shard_map/ppermute | solution.py:436
  97.3 2.3 %key_grad.1 = bf16[8,2,4,16,256]{4,3,2,1,0:T(8,128)(2,1)} custom-call(f32[4,128,128]{2,1,0:T(8,128)} %get-tuple-element.98.cos_ref, f32[4,128,128]{2,1,0:T(8,128)} %get-tuple-element.97.sin_ref, bf16[4,128,256]{2,1,0:T(8,128)(2,1)} %get-tuple-element.78.refs_0_, bf16[4,128,256]{2,1,0:T(8,128)(2,1)} %copy-done.8, bf16[4,128,256]{2,1,0:T(8,128)(2,1)} %copy-done.9, ...), custom_call_target="tpu_custom_call" | custom-call | tf_op jit(solution)/shard_map/key_grad/pallas_call | solution.py:368
  99.7 4.1 %all-to-all-start.1 = ((bf16[16,64,256]{2,1,0:T(8,128)(2,1)}), bf16[16,64,256]{2,1,0:T(8,128)(2,1)S(1)}, u32[]{:S(2)}, u32[]{:S(2)}) async-start(bf16[16,64,256]{2,1,0:T(8,128)(2,1)} %bitcast.15), calls=%async_computation.1 | async-start | bytes 1048576 | tf_op jit(solution)/shard_map/all_to_all | solution.py:432
  103.8 2.4 %collective-permute-done.10.back_ref = bf16[3,128,640]{2,1,0:T(8,128)(2,1)S(1)} collective-permute-done((bf16[3,128,640]{2,1,0:T(8,128)(2,1)}, bf16[3,128,640]{2,1,0:T(8,128)(2,1)S(1)}, u32[]{:S(2)}, u32[]{:S(2)}) %collective-permute-start.10) | collective-permute-done | bytes 491552 | tf_op jit(solution)/shard_map/ppermute | solution.py:440
  106.1 2.1 %collective-permute-start.11 = (bf16[1,128,640]{2,1,0:T(8,128)(2,1)S(1)}, bf16[1,128,640]{2,1,0:T(8,128)(2,1)S(1)}, u32[]{:S(2)}, u32[]{:S(2)}) collective-permute-start(bf16[1,128,640]{2,1,0:T(8,128)(2,1)S(1)} %slice.8), channel_id=1, source_target_pairs={{0,12},{4,0},{8,4},{12,8},{1,13},{5,1},{9,5},{13,9},{2,14},{6,2},{... | collective-permute-start | bytes 491528 | tf_op jit(solution)/shard_map/ppermute | solution.py:440
  108.3 3.9 %collective-permute-done.11.dq_ref = bf16[1,128,640]{2,1,0:T(8,128)(2,1)S(1)} collective-permute-done((bf16[1,128,640]{2,1,0:T(8,128)(2,1)S(1)}, bf16[1,128,640]{2,1,0:T(8,128)(2,1)S(1)}, u32[]{:S(2)}, u32[]{:S(2)}) %collective-permute-start.11) | collective-permute-done | bytes 163872 | tf_op jit(solution)/shard_map/ppermute | solution.py:440
  112.3 3.0 %collective-permute-done.13.out_ref = bf16[1,128,640]{2,1,0:T(8,128)(2,1)S(1)} collective-permute-done((bf16[1,128,640]{2,1,0:T(8,128)(2,1)S(1)}, bf16[1,128,640]{2,1,0:T(8,128)(2,1)S(1)}, u32[]{:S(2)}, u32[]{:S(2)}) %collective-permute-start.13) | collective-permute-done | bytes 163872 | tf_op jit(solution)/shard_map/ppermute | solution.py:440
  115.3 1.1 all-to-all-done.1
  116.4 1.9 %collective-permute-done.14.kv_other_ref = bf16[8,2,4,16,256]{4,3,2,1,0:T(8,128)(2,1)S(1)} collective-permute-done((bf16[8,2,4,16,256]{4,3,2,1,0:T(8,128)(2,1)S(1)}, bf16[8,2,4,16,256]{4,3,2,1,0:T(8,128)(2,1)S(1)}, u32[]{:S(2)}, u32[]{:S(2)}) %collective-permute-start.14) | collective-permute-done | bytes 524320 | tf_op jit(solution)/shard_map/ppermute | solution.py:472
  119.1 4.4 %weight_grad.1 = bf16[32,80,128]{2,1,0:T(8,128)(2,1)} custom-call(bf16[8,2,4,16,256]{4,3,2,1,0:T(8,128)(2,1)} %bitcast.17, bf16[8,2,4,16,256]{4,3,2,1,0:T(8,128)(2,1)} %copy-done.6, bf16[4,4,1280,128]{3,2,1,0:T(8,128)(2,1)} %bitcast.12), custom_call_target="tpu_custom_call" | custom-call | flops 1400000000 | bytes 7000000 | tf_op jit(solution)/shard_map/weight_grad/pallas_call | solution.py:394
  123.5 5.5 %all-to-all-start.2 = ((bf16[32,80,128]{2,1,0:T(8,128)(2,1)}), bf16[32,80,128]{2,1,0:T(8,128)(2,1)S(1)}, u32[]{:S(2)}, u32[]{:S(2)}) async-start(bf16[32,80,128]{2,1,0:T(8,128)(2,1)} %weight_grad.1), calls=%async_computation.2 | async-start | bytes 1310720 | tf_op jit(solution)/shard_map/all_to_all | solution.py:432
  129.1 2.6 %merge_heads.1 = (bf16[128,2560]{1,0:T(8,128)(2,1)}, bf16[128,2560]{1,0:T(8,128)(2,1)}) custom-call(bf16[2,128,640]{2,1,0:T(8,128)(2,1)} %get-tuple-element.87.stay_ref, bf16[3,128,640]{2,1,0:T(8,128)(2,1)} %copy-done.3, bf16[3,128,640]{2,1,0:T(8,128)(2,1)} %copy-done.4, bf16[1,128,640]{2,1,0:T(8,128)(2,1)} %copy-done.11, bf16[1,128,640]{2,1,0:T(8,128)(2,1)} %copy-done.12), custom_call_target="tpu_custom_call" | custom-call | tf_op jit(solution)/shard_map/merge_heads/pallas_call | solution.py:133
  131.6 12.1 %all-to-all-done.2 = bf16[32,80,128]{2,1,0:T(8,128)(2,1)S(1)} async-done(((bf16[32,80,128]{2,1,0:T(8,128)(2,1)}), bf16[32,80,128]{2,1,0:T(8,128)(2,1)S(1)}, u32[]{:S(2)}, u32[]{:S(2)}) %all-to-all-start.2) | async-done | bytes 655392 | tf_op jit(solution)/shard_map/all_to_all | solution.py:432
  143.7 0.8 copy-done.1
  144.5 1.8 %final_sum.1 = f32[40,1024]{1,0:T(8,128)} custom-call(bf16[8,4,80,128]{3,2,1,0:T(8,128)(2,1)} %bitcast.14), custom_call_target="tpu_custom_call" | custom-call | tf_op jit(solution)/shard_map/final_sum/pallas_call | solution.py:422
  (57 shorter events, 3.6 us)
Async XLA Ops:
  7.2 111.1 %all-gather.3.cloned.1.call-start = ((), (), s32[]{:S(2)}) async-start(), calls=%async_computation.3 | async-start | bytes 6553600 | tf_op jit(solution)/shard_map/all_gather | solution.py:458
  7.2 10.3 %copy-start.13 = (s32[8,4]{0,1:T(4,128)S(1)}, s32[8,4]{0,1:T(4,128)}, u32[]{:S(2)}) copy-start(s32[8,4]{0,1:T(4,128)} %param.16) | copy-start | bytes 388
  10.9 7.4 %collective-permute-start = (bf16[1280,128]{1,0:T(8,128)(2,1)}, bf16[1280,128]{1,0:T(8,128)(2,1)S(1)}, u32[]{:S(2)}, u32[]{:S(2)}) collective-permute-start(bf16[1280,128]{1,0:T(8,128)(2,1)} %get-tuple-element.60), channel_id=1, source_target_pairs={{0,1},{1,0},{2,3},{3,2},{4,5},{5,4},{6,7},{7,6},{8,9},{9,8},{10,11... | collective-permute-start | bytes 983048 | tf_op jit(solution)/shard_map/ppermute | solution.py:436
  10.9 15.7 %collective-permute-start.1 = (bf16[1280,128]{1,0:T(8,128)(2,1)}, bf16[1280,128]{1,0:T(8,128)(2,1)S(1)}, u32[]{:S(2)}, u32[]{:S(2)}) collective-permute-start(bf16[1280,128]{1,0:T(8,128)(2,1)} %get-tuple-element.61), channel_id=1, source_target_pairs={{0,2},{1,3},{2,0},{3,1},{4,6},{5,7},{6,4},{7,5},{8,10},{9,11},{10,... | collective-permute-start | bytes 983048 | tf_op jit(solution)/shard_map/ppermute | solution.py:436
  13.0 15.2 %collective-permute-start.2 = (bf16[1280,128]{1,0:T(8,128)(2,1)}, bf16[1280,128]{1,0:T(8,128)(2,1)S(1)}, u32[]{:S(2)}, u32[]{:S(2)}) collective-permute-start(bf16[1280,128]{1,0:T(8,128)(2,1)} %get-tuple-element.62), channel_id=1, source_target_pairs={{0,3},{1,2},{2,1},{3,0},{4,7},{5,6},{6,5},{7,4},{8,11},{9,10},{10,... | collective-permute-start | bytes 983048 | tf_op jit(solution)/shard_map/ppermute | solution.py:436
  13.1 16.4 %collective-permute-start.3 = (bf16[2,128,640]{2,1,0:T(8,128)(2,1)}, bf16[2,128,640]{2,1,0:T(8,128)(2,1)S(1)}, u32[]{:S(2)}, u32[]{:S(2)}) collective-permute-start(bf16[2,128,640]{2,1,0:T(8,128)(2,1)} %get-tuple-element.69), channel_id=1, source_target_pairs={{0,4},{4,8},{8,12},{12,0},{1,5},{5,9},{9,13},{13,1},{2,6},{6,10},{... | collective-permute-start | bytes 983048 | tf_op jit(solution)/shard_map/ppermute | solution.py:440
  14.7 17.9 %collective-permute-start.4 = (bf16[2,128,640]{2,1,0:T(8,128)(2,1)}, bf16[2,128,640]{2,1,0:T(8,128)(2,1)S(1)}, u32[]{:S(2)}, u32[]{:S(2)}) collective-permute-start(bf16[2,128,640]{2,1,0:T(8,128)(2,1)} %get-tuple-element.70), channel_id=1, source_target_pairs={{0,8},{4,12},{8,0},{12,4},{1,9},{5,13},{9,1},{13,5},{2,10},{6,14},... | collective-permute-start | bytes 983048 | tf_op jit(solution)/shard_map/ppermute | solution.py:440
  18.2 14.3 %collective-permute-start.5 = (bf16[2,128,640]{2,1,0:T(8,128)(2,1)}, bf16[2,128,640]{2,1,0:T(8,128)(2,1)S(1)}, u32[]{:S(2)}, u32[]{:S(2)}) collective-permute-start(bf16[2,128,640]{2,1,0:T(8,128)(2,1)} %get-tuple-element.71), channel_id=1, source_target_pairs={{0,12},{4,0},{8,4},{12,8},{1,13},{5,1},{9,5},{13,9},{2,14},{6,2},{... | collective-permute-start | bytes 983048 | tf_op jit(solution)/shard_map/ppermute | solution.py:440
  19.6 8.7 %copy-start.7 = (bf16[1280,128]{1,0:T(8,128)(2,1)S(1)}, bf16[1280,128]{1,0:T(8,128)(2,1)}, u32[]{:S(2)}) copy-start(bf16[1280,128]{1,0:T(8,128)(2,1)} %get-tuple-element.64) | copy-start | bytes 983044
  29.5 3.1 %copy-start = (bf16[8,4,2,16,384]{4,3,2,1,0:T(8,128)(2,1)S(1)}, bf16[8,4,2,16,384]{4,3,2,1,0:T(8,128)(2,1)}, u32[]{:S(2)}) copy-start(bf16[8,4,2,16,384]{4,3,2,1,0:T(8,128)(2,1)} %project.1) | copy-start | bytes 2359300
  29.5 28.4 %copy-start.16 = (bf16[2,128,640]{2,1,0:T(8,128)(2,1)}, bf16[2,128,640]{2,1,0:T(8,128)(2,1)S(1)}, u32[]{:S(2)}) copy-start(bf16[2,128,640]{2,1,0:T(8,128)(2,1)S(1)} %collective-permute-done.3.refs_1_) | copy-start | bytes 983044
  32.6 25.4 %copy-start.17 = (bf16[2,128,640]{2,1,0:T(8,128)(2,1)}, bf16[2,128,640]{2,1,0:T(8,128)(2,1)S(1)}, u32[]{:S(2)}) copy-start(bf16[2,128,640]{2,1,0:T(8,128)(2,1)S(1)} %collective-permute-done.4.refs_2_) | copy-start | bytes 983044
  32.6 25.4 %copy-start.18 = (bf16[2,128,640]{2,1,0:T(8,128)(2,1)}, bf16[2,128,640]{2,1,0:T(8,128)(2,1)S(1)}, u32[]{:S(2)}) copy-start(bf16[2,128,640]{2,1,0:T(8,128)(2,1)S(1)} %collective-permute-done.5.refs_3_) | copy-start | bytes 983044
  58.0 2.4 %copy-start.5 = (bf16[64,16,384]{2,1,0:T(8,128)(2,1)}, bf16[64,16,384]{2,1,0:T(8,128)(2,1)S(1)}, u32[]{:S(2)}) copy-start(bf16[64,16,384]{2,1,0:T(8,128)(2,1)S(1)} %all_to_all.15) | copy-start | bytes 2359300
  58.0 28.9 %copy-start.14 = (f32[128]{0:T(128)S(1)}, f32[128]{0:T(128)}, u32[]{:S(2)}) copy-start(f32[128]{0:T(128)} %constant.9) | copy-start | bytes 1540
  58.0 2.4 %collective-permute-start.6 = (bf16[8,4,2,16,384]{4,3,2,1,0:T(8,128)(2,1)S(1)}, bf16[8,4,2,16,384]{4,3,2,1,0:T(8,128)(2,1)S(1)}, u32[]{:S(2)}, u32[]{:S(2)}) collective-permute-start(bf16[8,4,2,16,384]{4,3,2,1,0:T(8,128)(2,1)S(1)} %bitcast.18), channel_id=1, source_target_pairs={{0,1},{1,0},{2,3},{3,2},{4,5},{5,4},{6,7},{7,6},{8,9},{9,8},{10,11... | collective-permute-start | bytes 2359304 | tf_op jit(solution)/shard_map/ppermute | solution.py:460
  82.7 6.8 %collective-permute-start.7 = (bf16[4,128,256]{2,1,0:T(8,128)(2,1)}, bf16[4,128,256]{2,1,0:T(8,128)(2,1)S(1)}, u32[]{:S(2)}, u32[]{:S(2)}) collective-permute-start(bf16[4,128,256]{2,1,0:T(8,128)(2,1)} %get-tuple-element.79), channel_id=1, source_target_pairs={{0,1},{1,0},{2,3},{3,2},{4,5},{5,4},{6,7},{7,6},{8,9},{9,8},{10,11... | collective-permute-start | bytes 786440 | tf_op jit(solution)/shard_map/ppermute | solution.py:436
  82.8 9.3 %collective-permute-start.8 = (bf16[4,128,256]{2,1,0:T(8,128)(2,1)}, bf16[4,128,256]{2,1,0:T(8,128)(2,1)S(1)}, u32[]{:S(2)}, u32[]{:S(2)}) collective-permute-start(bf16[4,128,256]{2,1,0:T(8,128)(2,1)} %get-tuple-element.80), channel_id=1, source_target_pairs={{0,2},{1,3},{2,0},{3,1},{4,6},{5,7},{6,4},{7,5},{8,10},{9,11},{10,... | collective-permute-start | bytes 786440 | tf_op jit(solution)/shard_map/ppermute | solution.py:436
  83.6 13.0 %collective-permute-start.9 = (bf16[4,128,256]{2,1,0:T(8,128)(2,1)}, bf16[4,128,256]{2,1,0:T(8,128)(2,1)S(1)}, u32[]{:S(2)}, u32[]{:S(2)}) collective-permute-start(bf16[4,128,256]{2,1,0:T(8,128)(2,1)} %get-tuple-element.81), channel_id=1, source_target_pairs={{0,3},{1,2},{2,1},{3,0},{4,7},{5,6},{6,5},{7,4},{8,11},{9,10},{10,... | collective-permute-start | bytes 786440 | tf_op jit(solution)/shard_map/ppermute | solution.py:436
  84.5 21.6 %collective-permute-start.10 = (bf16[3,128,640]{2,1,0:T(8,128)(2,1)}, bf16[3,128,640]{2,1,0:T(8,128)(2,1)S(1)}, u32[]{:S(2)}, u32[]{:S(2)}) collective-permute-start(bf16[3,128,640]{2,1,0:T(8,128)(2,1)} %get-tuple-element.82), channel_id=1, source_target_pairs={{0,12},{4,0},{8,4},{12,8},{1,13},{5,1},{9,5},{13,9},{2,14},{6,2},{... | collective-permute-start | bytes 1474568 | tf_op jit(solution)/shard_map/ppermute | solution.py:440
  86.9 21.4 %collective-permute-start.12 = (bf16[3,128,640]{2,1,0:T(8,128)(2,1)}, bf16[3,128,640]{2,1,0:T(8,128)(2,1)S(1)}, u32[]{:S(2)}, u32[]{:S(2)}) collective-permute-start(bf16[3,128,640]{2,1,0:T(8,128)(2,1)} %get-tuple-element.83), channel_id=1, source_target_pairs={{0,4},{4,8},{8,12},{12,0},{1,5},{5,9},{9,13},{13,1},{2,6},{6,10},{... | collective-permute-start | bytes 1474568 | tf_op jit(solution)/shard_map/ppermute | solution.py:440
  89.5 7.2 %copy-start.8 = (bf16[4,128,256]{2,1,0:T(8,128)(2,1)}, bf16[4,128,256]{2,1,0:T(8,128)(2,1)S(1)}, u32[]{:S(2)}) copy-start(bf16[4,128,256]{2,1,0:T(8,128)(2,1)S(1)} %collective-permute-done.7.refs_1_) | copy-start | bytes 786436
  92.2 4.5 %copy-start.9 = (bf16[4,128,256]{2,1,0:T(8,128)(2,1)}, bf16[4,128,256]{2,1,0:T(8,128)(2,1)S(1)}, u32[]{:S(2)}) copy-start(bf16[4,128,256]{2,1,0:T(8,128)(2,1)S(1)} %collective-permute-done.8.refs_2_) | copy-start | bytes 786436
  99.7 16.7 %all-to-all-start.1 = ((bf16[16,64,256]{2,1,0:T(8,128)(2,1)}), bf16[16,64,256]{2,1,0:T(8,128)(2,1)S(1)}, u32[]{:S(2)}, u32[]{:S(2)}) async-start(bf16[16,64,256]{2,1,0:T(8,128)(2,1)} %bitcast.15), calls=%async_computation.1 | async-start | bytes 1048576 | tf_op jit(solution)/shard_map/all_to_all | solution.py:432
  106.1 17.4 %copy-start.3 = (bf16[3,128,640]{2,1,0:T(8,128)(2,1)}, bf16[3,128,640]{2,1,0:T(8,128)(2,1)S(1)}, u32[]{:S(2)}) copy-start(bf16[3,128,640]{2,1,0:T(8,128)(2,1)S(1)} %collective-permute-done.10.back_ref) | copy-start | bytes 1474564
  106.1 6.1 %collective-permute-start.11 = (bf16[1,128,640]{2,1,0:T(8,128)(2,1)S(1)}, bf16[1,128,640]{2,1,0:T(8,128)(2,1)S(1)}, u32[]{:S(2)}, u32[]{:S(2)}) collective-permute-start(bf16[1,128,640]{2,1,0:T(8,128)(2,1)S(1)} %slice.8), channel_id=1, source_target_pairs={{0,12},{4,0},{8,4},{12,8},{1,13},{5,1},{9,5},{13,9},{2,14},{6,2},{... | collective-permute-start | bytes 491528 | tf_op jit(solution)/shard_map/ppermute | solution.py:440
  108.2 15.3 %copy-start.4 = (bf16[3,128,640]{2,1,0:T(8,128)(2,1)}, bf16[3,128,640]{2,1,0:T(8,128)(2,1)S(1)}, u32[]{:S(2)}) copy-start(bf16[3,128,640]{2,1,0:T(8,128)(2,1)S(1)} %collective-permute-done.12.ahead_ref) | copy-start | bytes 1474564
  108.3 7.0 %collective-permute-start.13 = (bf16[1,128,640]{2,1,0:T(8,128)(2,1)S(1)}, bf16[1,128,640]{2,1,0:T(8,128)(2,1)S(1)}, u32[]{:S(2)}, u32[]{:S(2)}) collective-permute-start(bf16[1,128,640]{2,1,0:T(8,128)(2,1)S(1)} %slice.9), channel_id=1, source_target_pairs={{0,4},{4,8},{8,12},{12,0},{1,5},{5,9},{9,13},{13,1},{2,6},{6,10},{... | collective-permute-start | bytes 491528 | tf_op jit(solution)/shard_map/ppermute | solution.py:440
  112.3 11.3 %copy-start.11 = (bf16[1,128,640]{2,1,0:T(8,128)(2,1)}, bf16[1,128,640]{2,1,0:T(8,128)(2,1)S(1)}, u32[]{:S(2)}) copy-start(bf16[1,128,640]{2,1,0:T(8,128)(2,1)S(1)} %collective-permute-done.11.dq_ref) | copy-start | bytes 491524
  115.3 8.2 %copy-start.12 = (bf16[1,128,640]{2,1,0:T(8,128)(2,1)}, bf16[1,128,640]{2,1,0:T(8,128)(2,1)S(1)}, u32[]{:S(2)}) copy-start(bf16[1,128,640]{2,1,0:T(8,128)(2,1)S(1)} %collective-permute-done.13.out_ref) | copy-start | bytes 491524
  116.4 1.9 %collective-permute-start.14 = (bf16[8,2,4,16,256]{4,3,2,1,0:T(8,128)(2,1)S(1)}, bf16[8,2,4,16,256]{4,3,2,1,0:T(8,128)(2,1)S(1)}, u32[]{:S(2)}, u32[]{:S(2)}) collective-permute-start(bf16[8,2,4,16,256]{4,3,2,1,0:T(8,128)(2,1)S(1)} %bitcast.16), channel_id=1, source_target_pairs={{0,1},{1,0},{2,3},{3,2},{4,5},{5,4},{6,7},{7,6},{8,9},{9,8},{10,11... | collective-permute-start | bytes 1572872 | tf_op jit(solution)/shard_map/ppermute | solution.py:472
  123.5 20.2 %all-to-all-start.2 = ((bf16[32,80,128]{2,1,0:T(8,128)(2,1)}), bf16[32,80,128]{2,1,0:T(8,128)(2,1)S(1)}, u32[]{:S(2)}, u32[]{:S(2)}) async-start(bf16[32,80,128]{2,1,0:T(8,128)(2,1)} %weight_grad.1), calls=%async_computation.2 | async-start | bytes 1310720 | tf_op jit(solution)/shard_map/all_to_all | solution.py:432
  (5 other events, 5.2 us)
Sparse Core Ops, SparseCore 0:
  32.7 70.8 all-gather.2

commit v5 on v4

--- a/solution.py
+++ b/solution.py
@@ -390,7 +390,7 @@
 
 
 def weight_grad(xt, kv_own, kv_other):
-    steps = 2
+    steps = 1
     return pl.pallas_call(
         weight_grad_kernel,
         grid=(steps,),
@@ -401,7 +401,7 @@
         ],
         out_specs=pl.BlockSpec((N_DP * N_Y // steps, 2 * SHARE, HD), lambda i: (i, 0, 0)),
         out_shape=jax.ShapeDtypeStruct((N_DP * N_Y, 2 * SHARE, HD), bf16),
-        compiler_params=pltpu.CompilerParams(vmem_limit_bytes=VMEM_LIMIT),
+        compiler_params=pltpu.CompilerParams(vmem_limit_bytes=VMEM_LIMIT // 2),
         cost_estimate=pl.CostEstimate(flops=1400000000, bytes_accessed=7000000, transcendentals=0),
         name="weight_grad",
     )(kv_own, kv_other, xt)
@@ -468,7 +468,7 @@
     kv_grad = key_grad(dkv, cosine, sine)
     kv_grad = swap(kv_grad.reshape(-1, N_Y * CAP, 2 * HD), ("zh", "x", "zl")).reshape(N_DP, 2, N_Y, CAP, 2 * HD)
     last_dq, last_out = along_y(back[2:], -1), along_y(ahead[2:], 1)
-    kv_grad, last_dq, last_out = barrier((kv_grad, last_dq, last_out))
+    kv_grad, last_dq, last_out, xt = barrier((kv_grad, last_dq, last_out, xt))
     kv_grad_other = lax.ppermute(kv_grad, "c", [(0, 1), (1, 0)])
     dw = weight_grad(xt, kv_grad, kv_grad_other)
     dw, back, ahead = barrier((dw, back, ahead))

time: 154 us -> 153 us (level)
  Pallas kernels: 43.2 us -> 36.3 us
  starting transfers between devices: 24.1 us -> 30.3 us
  local copies, waits for them, and re-layouts: 4.04 us -> 5.74 us
    pallas_call x1, Pallas kernels: 21.3 us -> 16.6 us  [attention(): pl.pallas_call(attention_kernel, in_specs=[vmem] * (3 + N_Y), out_specs=[...]
    all_to_all x2, starting transfers between devices: 9.62 us -> 14.3 us  [swap(): return lax.all_to_all(array, axes, split_axis=0, concat_axis=0, tiled=True)]
    pallas_call x1, Pallas kernels: 4.44 us -> 2.36 us  [weight_grad(): pl.pallas_call(weight_grad_kernel, grid=(steps,), in_specs=[pl.BlockSpec(...]
    ppermute x7, waiting for transfers between devices: 12.3 us -> 10.5 us  [along_y(): return lax.ppermute(array, 'y', [(i, (i + s) % N_Y) for i in range(N_Y)])]
    unnamed x39 -> x37, local copies, waits for them, and re-layouts: 4.02 us -> 5.71 us
    ppermute x7, starting transfers between devices: 10.3 us -> 11.9 us  [along_y(): return lax.ppermute(array, 'y', [(i, (i + s) % N_Y) for i in range(N_Y)])]
  transfers between devices with their start and end apart: 18 -> 18, of which waited for: 11 -> 11; matrix products, arithmetic and copies ran while one was open for 3% -> 3% of each run, Pallas kernels for 22% -> 19%
where the time goes in v5:
time: 153 us
  waiting for transfers between devices  37.1 us (24%)
  Pallas kernels  36.3 us (24%)
  starting transfers between devices  30.3 us (20%)
  blocking collectives  25.4 us (17%)
  between operations  14.2 us (9%)
  local copies, waits for them, and re-layouts  5.74 us (4%)
  other arithmetic  3.84 us (3%)
    all_to_all x1, blocking collectives, swap(): return lax.all_to_all(array, axes, split_axis=0, concat_axis=0, tiled=True)  25.4 us
    pallas_call x1, Pallas kernels, attention(): pl.pallas_call(attention_kernel, in_specs=[vmem] * (3 + N_Y), out_specs=[...  16.6 us
    all_to_all x2, starting transfers between devices, swap(): return lax.all_to_all(array, axes, split_axis=0, concat_axis=0, tiled=True)  14.3 us
    all_to_all x2, waiting for transfers between devices, swap(): return lax.all_to_all(array, axes, split_axis=0, concat_axis=0, tiled=True)  13.6 us
    ppermute x7, starting transfers between devices, along_y(): return lax.ppermute(array, 'y', [(i, (i + s) % N_Y) for i in range(N_Y)])  11.9 us
    ppermute x7, waiting for transfers between devices, along_y(): return lax.ppermute(array, 'y', [(i, (i + s) % N_Y) for i in range(N_Y)])  10.5 us
    ppermute x6, waiting for transfers between devices, flip(): return lax.ppermute(array, Q, [(i, i ^ m) for i in range(N_Q)])  8.83 us
    pallas_call x1, Pallas kernels, project(): pl.pallas_call(project_kernel, grid=(D // COLS,), in_specs=[whole(N_DP, N...  7.01 us
  transfers between devices with their start and end apart: 18, of which 11 were waited for; matrix products, arithmetic and copies ran while one was open for 3% of the time, Pallas kernels for 19%

profile of v5, /device:TPU:0, one launch (start us, length us, event | category | flops | bytes accessed | tf_op | source)
XLA Modules:
  0.0 152.8 jit_solution(16640907201585177784)
XLA Ops:
  7.2 3.6 %cut.1 = (bf16[2,128,640]{2,1,0:T(8,128)(2,1)}, bf16[2,128,640]{2,1,0:T(8,128)(2,1)}, bf16[2,128,640]{2,1,0:T(8,128)(2,1)}, bf16[2,128,640]{2,1,0:T(8,128)(2,1)}...) custom-call(s32[1,128]{1,0:T(1,128)} %bitcast.24, ...), custom_call_target="tpu_custom_call" | custom-call | flops 2000000000 | bytes 5200000 | tf_op jit(solution)/shard_map/cut/pallas_call | solution.py:97
  10.9 2.1 %collective-permute-start.1 = (bf16[1280,128]{1,0:T(8,128)(2,1)}, bf16[1280,128]{1,0:T(8,128)(2,1)S(1)}, u32[]{:S(2)}, u32[]{:S(2)}) collective-permute-start(bf16[1280,128]{1,0:T(8,128)(2,1)} %get-tuple-element.62), channel_id=1, source_target_pairs={{0,2},{1,3},{2,0},{3,1},{4,6},{5,7},{6,4},{7,5},{8,10},{9,11},{10,... | collective-permute-start | bytes 983048 | tf_op jit(solution)/shard_map/ppermute | solution.py:436
  13.1 1.6 %collective-permute-start.3 = (bf16[2,128,640]{2,1,0:T(8,128)(2,1)}, bf16[2,128,640]{2,1,0:T(8,128)(2,1)S(1)}, u32[]{:S(2)}, u32[]{:S(2)}) collective-permute-start(bf16[2,128,640]{2,1,0:T(8,128)(2,1)} %get-tuple-element.70), channel_id=1, source_target_pairs={{0,4},{4,8},{8,12},{12,0},{1,5},{5,9},{9,13},{13,1},{2,6},{6,10},{... | collective-permute-start | bytes 983048 | tf_op jit(solution)/shard_map/ppermute | solution.py:440
  14.6 2.9 %collective-permute-start.4 = (bf16[2,128,640]{2,1,0:T(8,128)(2,1)}, bf16[2,128,640]{2,1,0:T(8,128)(2,1)S(1)}, u32[]{:S(2)}, u32[]{:S(2)}) collective-permute-start(bf16[2,128,640]{2,1,0:T(8,128)(2,1)} %get-tuple-element.71), channel_id=1, source_target_pairs={{0,8},{4,12},{8,0},{12,4},{1,9},{5,13},{9,1},{13,5},{2,10},{6,14},... | collective-permute-start | bytes 983048 | tf_op jit(solution)/shard_map/ppermute | solution.py:440
  18.2 1.3 collective-permute-start.5
  19.6 7.0 %project.1 = bf16[8,4,2,16,384]{4,3,2,1,0:T(8,128)(2,1)} custom-call(s32[8,4]{1,0:T(8,128)} %copy.15.lengths_ref, s32[1,128]{1,0:T(1,128)} %bitcast.25, s32[1,128]{1,0:T(1,128)} %bitcast.26, f32[1,128]{1,0:T(1,128)} %constant.8.clone.freq_ref, bf16[1024]{0:T(1024)(128)(2,1)} %bias_ref.1, bf16[128,5120]{1,0:T(8,128)(2,1)} %x_ref.2, bf16[5120,1024]{1,0:T(8,128)(2,1)} %w_ref.1), custom_call_target="tpu_custom_call" | custom-call | flops 1600000000 | bytes 16000000 | tf_op jit(solution)/shard_map/project/pallas_call | solution.py:196
  26.6 1.6 %collective-permute-done.2 = bf16[1280,128]{1,0:T(8,128)(2,1)S(1)} collective-permute-done((bf16[1280,128]{1,0:T(8,128)(2,1)}, bf16[1280,128]{1,0:T(8,128)(2,1)S(1)}, u32[]{:S(2)}, u32[]{:S(2)}) %collective-permute-start.2) | collective-permute-done | bytes 327712 | tf_op jit(solution)/shard_map/ppermute | solution.py:436
  28.2 1.3 pad_maximum_fusion
  29.5 3.0 %collective-permute-done.4.refs_2_ = bf16[2,128,640]{2,1,0:T(8,128)(2,1)S(1)} collective-permute-done((bf16[2,128,640]{2,1,0:T(8,128)(2,1)}, bf16[2,128,640]{2,1,0:T(8,128)(2,1)S(1)}, u32[]{:S(2)}, u32[]{:S(2)}) %collective-permute-start.4) | collective-permute-done | bytes 327712 | tf_op jit(solution)/shard_map/ppermute | solution.py:440
  32.6 25.4 %all_to_all.15 = bf16[64,16,384]{2,1,0:T(8,128)(2,1)S(1)} all-to-all(bf16[64,16,384]{2,1,0:T(8,128)(2,1)S(1)} %bitcast.15), channel_id=1, replica_groups=mesh['zh'=2,'x'=4,'y'=4,'zl'=2,'c'=2] {'zh','x','y','zl'}, dimensions={0} | all-to-all | bytes 1572864 | tf_op jit(solution)/shard_map/all_to_all | solution.py:432
  58.1 2.3 %collective-permute-done.6.kv_other_ref = bf16[8,4,2,16,384]{4,3,2,1,0:T(8,128)(2,1)S(1)} collective-permute-done((bf16[8,4,2,16,384]{4,3,2,1,0:T(8,128)(2,1)S(1)}, bf16[8,4,2,16,384]{4,3,2,1,0:T(8,128)(2,1)S(1)}, u32[]{:S(2)}, u32[]{:S(2)}) %collective-permute-start.6) | collective-permute-done | bytes 786464 | tf_op jit(solution)/shard_map/ppermute | solution.py:460
  60.3 1.0 copy-done.14
  61.3 16.6 %attention.1 = (bf16[2,128,640]{2,1,0:T(8,128)(2,1)}, bf16[3,128,640]{2,1,0:T(8,128)(2,1)}, bf16[3,128,640]{2,1,0:T(8,128)(2,1)}, bf16[4,128,256]{2,1,0:T(8,128)...) custom-call(s32[8,4]{1,0:T(8,128)} %copy.15.lengths_ref, ...), custom_call_target="tpu_custom_call" | custom-call | flops 20000000000 | bytes 8000000 | tf_op jit(solution)/shard_map/attention/pallas_call | solution.py:323
  78.9 0.9 collective-permute-start.9
  79.8 2.4 %collective-permute-start.10 = (bf16[3,128,640]{2,1,0:T(8,128)(2,1)}, bf16[3,128,640]{2,1,0:T(8,128)(2,1)S(1)}, u32[]{:S(2)}, u32[]{:S(2)}) collective-permute-start(bf16[3,128,640]{2,1,0:T(8,128)(2,1)} %get-tuple-element.83), channel_id=1, source_target_pairs={{0,12},{4,0},{8,4},{12,8},{1,13},{5,1},{9,5},{13,9},{2,14},{6,2},{... | collective-permute-start | bytes 1474568 | tf_op jit(solution)/shard_map/ppermute | solution.py:440
  82.1 2.6 %sine_multiply_fusion = (f32[4,128,128]{2,1,0:T(8,128)}, f32[4,128,128]{2,1,0:T(8,128)}) fusion(f32[4,128,128]{2,1,0:T(8,128)} %get-tuple-element.78, f32[128]{0:T(128)S(1)} %compare_select_fusion, f32[128]{0:T(128)S(1)} %copy-done.13), kind=kLoop, calls=%fused_computation.1 | loop fusion | flops 131072 | bytes 787456 | tf_op jit(solution)/shard_map/mul | solution.py:465
  84.7 2.7 %collective-permute-done.8.refs_2_ = bf16[4,128,256]{2,1,0:T(8,128)(2,1)S(1)} collective-permute-done((bf16[4,128,256]{2,1,0:T(8,128)(2,1)}, bf16[4,128,256]{2,1,0:T(8,128)(2,1)S(1)}, u32[]{:S(2)}, u32[]{:S(2)}) %collective-permute-start.8) | collective-permute-done | bytes 262176 | tf_op jit(solution)/shard_map/ppermute | solution.py:436
  87.4 4.5 %collective-permute-done.9.refs_3_ = bf16[4,128,256]{2,1,0:T(8,128)(2,1)S(1)} collective-permute-done((bf16[4,128,256]{2,1,0:T(8,128)(2,1)}, bf16[4,128,256]{2,1,0:T(8,128)(2,1)S(1)}, u32[]{:S(2)}, u32[]{:S(2)}) %collective-permute-start.9) | collective-permute-done | bytes 262176 | tf_op jit(solution)/shard_map/ppermute | solution.py:436
  92.6 2.3 %key_grad.1 = bf16[8,2,4,16,256]{4,3,2,1,0:T(8,128)(2,1)} custom-call(f32[4,128,128]{2,1,0:T(8,128)} %get-tuple-element.100.cos_ref, f32[4,128,128]{2,1,0:T(8,128)} %get-tuple-element.99.sin_ref, bf16[4,128,256]{2,1,0:T(8,128)(2,1)} %get-tuple-element.79.refs_0_, bf16[4,128,256]{2,1,0:T(8,128)(2,1)} %copy-done.7, bf16[4,128,256]{2,1,0:T(8,128)(2,1)} %copy-done.8, ...), custom_call_target="tpu_custom_call" | custom-call | tf_op jit(solution)/shard_map/key_grad/pallas_call | solution.py:368
  94.9 8.7 %all-to-all-start.1 = ((bf16[16,64,256]{2,1,0:T(8,128)(2,1)}), bf16[16,64,256]{2,1,0:T(8,128)(2,1)S(1)}, u32[]{:S(2)}, u32[]{:S(2)}) async-start(bf16[16,64,256]{2,1,0:T(8,128)(2,1)} %bitcast.17), calls=%async_computation.1 | async-start | bytes 1048576 | tf_op jit(solution)/shard_map/all_to_all | solution.py:432
  104.4 3.6 %collective-permute-start.11 = (bf16[1,128,640]{2,1,0:T(8,128)(2,1)S(1)}, bf16[1,128,640]{2,1,0:T(8,128)(2,1)S(1)}, u32[]{:S(2)}, u32[]{:S(2)}) collective-permute-start(bf16[1,128,640]{2,1,0:T(8,128)(2,1)S(1)} %slice.8), channel_id=1, source_target_pairs={{0,12},{4,0},{8,4},{12,8},{1,13},{5,1},{9,5},{13,9},{2,14},{6,2},{... | collective-permute-start | bytes 491528 | tf_op jit(solution)/shard_map/ppermute | solution.py:440
  108.2 3.2 %collective-permute-done.11.dq_ref = bf16[1,128,640]{2,1,0:T(8,128)(2,1)S(1)} collective-permute-done((bf16[1,128,640]{2,1,0:T(8,128)(2,1)S(1)}, bf16[1,128,640]{2,1,0:T(8,128)(2,1)S(1)}, u32[]{:S(2)}, u32[]{:S(2)}) %collective-permute-start.11) | collective-permute-done | bytes 163872 | tf_op jit(solution)/shard_map/ppermute | solution.py:440
  111.4 3.5 %collective-permute-done.13.out_ref = bf16[1,128,640]{2,1,0:T(8,128)(2,1)S(1)} collective-permute-done((bf16[1,128,640]{2,1,0:T(8,128)(2,1)S(1)}, bf16[1,128,640]{2,1,0:T(8,128)(2,1)S(1)}, u32[]{:S(2)}, u32[]{:S(2)}) %collective-permute-start.13) | collective-permute-done | bytes 163872 | tf_op jit(solution)/shard_map/ppermute | solution.py:440
  114.9 1.5 all-to-all-done.1
  116.4 1.9 %collective-permute-done.14.kv_other_ref = bf16[8,2,4,16,256]{4,3,2,1,0:T(8,128)(2,1)S(1)} collective-permute-done((bf16[8,2,4,16,256]{4,3,2,1,0:T(8,128)(2,1)S(1)}, bf16[8,2,4,16,256]{4,3,2,1,0:T(8,128)(2,1)S(1)}, u32[]{:S(2)}, u32[]{:S(2)}) %collective-permute-start.14) | collective-permute-done | bytes 524320 | tf_op jit(solution)/shard_map/ppermute | solution.py:472
  118.3 2.5 %copy-done = bf16[16,1280,128]{2,1,0:T(8,128)(2,1)S(1)} copy-done((bf16[16,1280,128]{2,1,0:T(8,128)(2,1)S(1)}, bf16[16,1280,128]{2,1,0:T(8,128)(2,1)}, u32[]{:S(2)}) %copy-start) | copy-done | bytes 5242904
  120.8 2.4 %weight_grad.1 = bf16[32,80,128]{2,1,0:T(8,128)(2,1)} custom-call(bf16[8,2,4,16,256]{4,3,2,1,0:T(8,128)(2,1)S(1)} %bitcast.14, bf16[8,2,4,16,256]{4,3,2,1,0:T(8,128)(2,1)S(1)} %collective-permute-done.14.kv_other_ref, bf16[4,4,1280,128]{3,2,1,0:T(8,128)(2,1)S(1)} %bitcast.12), custom_call_target="tpu_custom_call" | custom-call | flops 1400000000 | bytes 7000000 | tf_op jit(solution)/shard_map/weight_grad/pallas_call | solution.py:394
  123.2 5.5 %all-to-all-start.2 = ((bf16[32,80,128]{2,1,0:T(8,128)(2,1)}), bf16[32,80,128]{2,1,0:T(8,128)(2,1)S(1)}, u32[]{:S(2)}, u32[]{:S(2)}) async-start(bf16[32,80,128]{2,1,0:T(8,128)(2,1)} %weight_grad.1), calls=%async_computation.2 | async-start | bytes 1310720 | tf_op jit(solution)/shard_map/all_to_all | solution.py:432
  128.7 2.6 %merge_heads.1 = (bf16[128,2560]{1,0:T(8,128)(2,1)}, bf16[128,2560]{1,0:T(8,128)(2,1)}) custom-call(bf16[2,128,640]{2,1,0:T(8,128)(2,1)} %get-tuple-element.89.stay_ref, bf16[3,128,640]{2,1,0:T(8,128)(2,1)} %copy-done.3, bf16[3,128,640]{2,1,0:T(8,128)(2,1)} %copy-done.4, bf16[1,128,640]{2,1,0:T(8,128)(2,1)} %copy-done.10, bf16[1,128,640]{2,1,0:T(8,128)(2,1)} %copy-done.11), custom_call_target="tpu_custom_call" | custom-call | tf_op jit(solution)/shard_map/merge_heads/pallas_call | solution.py:133
  131.3 12.1 %all-to-all-done.2 = bf16[32,80,128]{2,1,0:T(8,128)(2,1)S(1)} async-done(((bf16[32,80,128]{2,1,0:T(8,128)(2,1)}), bf16[32,80,128]{2,1,0:T(8,128)(2,1)S(1)}, u32[]{:S(2)}, u32[]{:S(2)}) %all-to-all-start.2) | async-done | bytes 655392 | tf_op jit(solution)/shard_map/all_to_all | solution.py:432
  143.3 0.8 copy-done.2
  144.2 1.8 %final_sum.1 = f32[40,1024]{1,0:T(8,128)} custom-call(bf16[8,4,80,128]{3,2,1,0:T(8,128)(2,1)} %bitcast.16), custom_call_target="tpu_custom_call" | custom-call | tf_op jit(solution)/shard_map/final_sum/pallas_call | solution.py:422
  (55 shorter events, 3.5 us)
Async XLA Ops:
  7.2 109.2 %all-gather.3.cloned.1.call-start = ((), (), s32[]{:S(2)}) async-start(), calls=%async_computation.3 | async-start | bytes 6553600 | tf_op jit(solution)/shard_map/all_gather | solution.py:458
  7.2 10.3 %copy-start.12 = (s32[8,4]{0,1:T(4,128)S(1)}, s32[8,4]{0,1:T(4,128)}, u32[]{:S(2)}) copy-start(s32[8,4]{0,1:T(4,128)} %param.16) | copy-start | bytes 388
  10.9 7.4 %collective-permute-start = (bf16[1280,128]{1,0:T(8,128)(2,1)}, bf16[1280,128]{1,0:T(8,128)(2,1)S(1)}, u32[]{:S(2)}, u32[]{:S(2)}) collective-permute-start(bf16[1280,128]{1,0:T(8,128)(2,1)} %get-tuple-element.61), channel_id=1, source_target_pairs={{0,1},{1,0},{2,3},{3,2},{4,5},{5,4},{6,7},{7,6},{8,9},{9,8},{10,11... | collective-permute-start | bytes 983048 | tf_op jit(solution)/shard_map/ppermute | solution.py:436
  10.9 15.7 %collective-permute-start.1 = (bf16[1280,128]{1,0:T(8,128)(2,1)}, bf16[1280,128]{1,0:T(8,128)(2,1)S(1)}, u32[]{:S(2)}, u32[]{:S(2)}) collective-permute-start(bf16[1280,128]{1,0:T(8,128)(2,1)} %get-tuple-element.62), channel_id=1, source_target_pairs={{0,2},{1,3},{2,0},{3,1},{4,6},{5,7},{6,4},{7,5},{8,10},{9,11},{10,... | collective-permute-start | bytes 983048 | tf_op jit(solution)/shard_map/ppermute | solution.py:436
  13.0 15.2 %collective-permute-start.2 = (bf16[1280,128]{1,0:T(8,128)(2,1)}, bf16[1280,128]{1,0:T(8,128)(2,1)S(1)}, u32[]{:S(2)}, u32[]{:S(2)}) collective-permute-start(bf16[1280,128]{1,0:T(8,128)(2,1)} %get-tuple-element.63), channel_id=1, source_target_pairs={{0,3},{1,2},{2,1},{3,0},{4,7},{5,6},{6,5},{7,4},{8,11},{9,10},{10,... | collective-permute-start | bytes 983048 | tf_op jit(solution)/shard_map/ppermute | solution.py:436
  13.1 16.4 %collective-permute-start.3 = (bf16[2,128,640]{2,1,0:T(8,128)(2,1)}, bf16[2,128,640]{2,1,0:T(8,128)(2,1)S(1)}, u32[]{:S(2)}, u32[]{:S(2)}) collective-permute-start(bf16[2,128,640]{2,1,0:T(8,128)(2,1)} %get-tuple-element.70), channel_id=1, source_target_pairs={{0,4},{4,8},{8,12},{12,0},{1,5},{5,9},{9,13},{13,1},{2,6},{6,10},{... | collective-permute-start | bytes 983048 | tf_op jit(solution)/shard_map/ppermute | solution.py:440
  14.6 17.9 %collective-permute-start.4 = (bf16[2,128,640]{2,1,0:T(8,128)(2,1)}, bf16[2,128,640]{2,1,0:T(8,128)(2,1)S(1)}, u32[]{:S(2)}, u32[]{:S(2)}) collective-permute-start(bf16[2,128,640]{2,1,0:T(8,128)(2,1)} %get-tuple-element.71), channel_id=1, source_target_pairs={{0,8},{4,12},{8,0},{12,4},{1,9},{5,13},{9,1},{13,5},{2,10},{6,14},... | collective-permute-start | bytes 983048 | tf_op jit(solution)/shard_map/ppermute | solution.py:440
  18.2 14.3 %collective-permute-start.5 = (bf16[2,128,640]{2,1,0:T(8,128)(2,1)}, bf16[2,128,640]{2,1,0:T(8,128)(2,1)S(1)}, u32[]{:S(2)}, u32[]{:S(2)}) collective-permute-start(bf16[2,128,640]{2,1,0:T(8,128)(2,1)} %get-tuple-element.72), channel_id=1, source_target_pairs={{0,12},{4,0},{8,4},{12,8},{1,13},{5,1},{9,5},{13,9},{2,14},{6,2},{... | collective-permute-start | bytes 983048 | tf_op jit(solution)/shard_map/ppermute | solution.py:440
  19.6 8.7 %copy-start.6 = (bf16[1280,128]{1,0:T(8,128)(2,1)S(1)}, bf16[1280,128]{1,0:T(8,128)(2,1)}, u32[]{:S(2)}) copy-start(bf16[1280,128]{1,0:T(8,128)(2,1)} %get-tuple-element.65) | copy-start | bytes 983044
  29.5 3.1 %copy-start.1 = (bf16[8,4,2,16,384]{4,3,2,1,0:T(8,128)(2,1)S(1)}, bf16[8,4,2,16,384]{4,3,2,1,0:T(8,128)(2,1)}, u32[]{:S(2)}) copy-start(bf16[8,4,2,16,384]{4,3,2,1,0:T(8,128)(2,1)} %project.1) | copy-start | bytes 2359300
  29.5 28.4 %copy-start.15 = (bf16[2,128,640]{2,1,0:T(8,128)(2,1)}, bf16[2,128,640]{2,1,0:T(8,128)(2,1)S(1)}, u32[]{:S(2)}) copy-start(bf16[2,128,640]{2,1,0:T(8,128)(2,1)S(1)} %collective-permute-done.3.refs_1_) | copy-start | bytes 983044
  32.5 25.4 %copy-start.16 = (bf16[2,128,640]{2,1,0:T(8,128)(2,1)}, bf16[2,128,640]{2,1,0:T(8,128)(2,1)S(1)}, u32[]{:S(2)}) copy-start(bf16[2,128,640]{2,1,0:T(8,128)(2,1)S(1)} %collective-permute-done.4.refs_2_) | copy-start | bytes 983044
  32.6 25.4 %copy-start.17 = (bf16[2,128,640]{2,1,0:T(8,128)(2,1)}, bf16[2,128,640]{2,1,0:T(8,128)(2,1)S(1)}, u32[]{:S(2)}) copy-start(bf16[2,128,640]{2,1,0:T(8,128)(2,1)S(1)} %collective-permute-done.5.refs_3_) | copy-start | bytes 983044
  58.0 24.2 %copy-start.13 = (f32[128]{0:T(128)S(1)}, f32[128]{0:T(128)}, u32[]{:S(2)}) copy-start(f32[128]{0:T(128)} %constant.9) | copy-start | bytes 1540
  58.0 2.4 %collective-permute-start.6 = (bf16[8,4,2,16,384]{4,3,2,1,0:T(8,128)(2,1)S(1)}, bf16[8,4,2,16,384]{4,3,2,1,0:T(8,128)(2,1)S(1)}, u32[]{:S(2)}, u32[]{:S(2)}) collective-permute-start(bf16[8,4,2,16,384]{4,3,2,1,0:T(8,128)(2,1)S(1)} %bitcast.18), channel_id=1, source_target_pairs={{0,1},{1,0},{2,3},{3,2},{4,5},{5,4},{6,7},{7,6},{8,9},{9,8},{10,11... | collective-permute-start | bytes 2359304 | tf_op jit(solution)/shard_map/ppermute | solution.py:460
  77.9 6.8 %collective-permute-start.7 = (bf16[4,128,256]{2,1,0:T(8,128)(2,1)}, bf16[4,128,256]{2,1,0:T(8,128)(2,1)S(1)}, u32[]{:S(2)}, u32[]{:S(2)}) collective-permute-start(bf16[4,128,256]{2,1,0:T(8,128)(2,1)} %get-tuple-element.80), channel_id=1, source_target_pairs={{0,1},{1,0},{2,3},{3,2},{4,5},{5,4},{6,7},{7,6},{8,9},{9,8},{10,11... | collective-permute-start | bytes 786440 | tf_op jit(solution)/shard_map/ppermute | solution.py:436
  78.0 9.3 %collective-permute-start.8 = (bf16[4,128,256]{2,1,0:T(8,128)(2,1)}, bf16[4,128,256]{2,1,0:T(8,128)(2,1)S(1)}, u32[]{:S(2)}, u32[]{:S(2)}) collective-permute-start(bf16[4,128,256]{2,1,0:T(8,128)(2,1)} %get-tuple-element.81), channel_id=1, source_target_pairs={{0,2},{1,3},{2,0},{3,1},{4,6},{5,7},{6,4},{7,5},{8,10},{9,11},{10,... | collective-permute-start | bytes 786440 | tf_op jit(solution)/shard_map/ppermute | solution.py:436
  78.9 13.0 %collective-permute-start.9 = (bf16[4,128,256]{2,1,0:T(8,128)(2,1)}, bf16[4,128,256]{2,1,0:T(8,128)(2,1)S(1)}, u32[]{:S(2)}, u32[]{:S(2)}) collective-permute-start(bf16[4,128,256]{2,1,0:T(8,128)(2,1)} %get-tuple-element.82), channel_id=1, source_target_pairs={{0,3},{1,2},{2,1},{3,0},{4,7},{5,6},{6,5},{7,4},{8,11},{9,10},{10,... | collective-permute-start | bytes 786440 | tf_op jit(solution)/shard_map/ppermute | solution.py:436
  79.8 24.6 %collective-permute-start.10 = (bf16[3,128,640]{2,1,0:T(8,128)(2,1)}, bf16[3,128,640]{2,1,0:T(8,128)(2,1)S(1)}, u32[]{:S(2)}, u32[]{:S(2)}) collective-permute-start(bf16[3,128,640]{2,1,0:T(8,128)(2,1)} %get-tuple-element.83), channel_id=1, source_target_pairs={{0,12},{4,0},{8,4},{12,8},{1,13},{5,1},{9,5},{13,9},{2,14},{6,2},{... | collective-permute-start | bytes 1474568 | tf_op jit(solution)/shard_map/ppermute | solution.py:440
  82.1 25.9 %collective-permute-start.12 = (bf16[3,128,640]{2,1,0:T(8,128)(2,1)}, bf16[3,128,640]{2,1,0:T(8,128)(2,1)S(1)}, u32[]{:S(2)}, u32[]{:S(2)}) collective-permute-start(bf16[3,128,640]{2,1,0:T(8,128)(2,1)} %get-tuple-element.84), channel_id=1, source_target_pairs={{0,4},{4,8},{8,12},{12,0},{1,5},{5,9},{9,13},{13,1},{2,6},{6,10},{... | collective-permute-start | bytes 1474568 | tf_op jit(solution)/shard_map/ppermute | solution.py:440
  84.7 7.2 %copy-start.7 = (bf16[4,128,256]{2,1,0:T(8,128)(2,1)}, bf16[4,128,256]{2,1,0:T(8,128)(2,1)S(1)}, u32[]{:S(2)}) copy-start(bf16[4,128,256]{2,1,0:T(8,128)(2,1)S(1)} %collective-permute-done.7.refs_1_) | copy-start | bytes 786436
  87.4 4.5 %copy-start.8 = (bf16[4,128,256]{2,1,0:T(8,128)(2,1)}, bf16[4,128,256]{2,1,0:T(8,128)(2,1)S(1)}, u32[]{:S(2)}) copy-start(bf16[4,128,256]{2,1,0:T(8,128)(2,1)S(1)} %collective-permute-done.8.refs_2_) | copy-start | bytes 786436
  94.9 21.5 %all-to-all-start.1 = ((bf16[16,64,256]{2,1,0:T(8,128)(2,1)}), bf16[16,64,256]{2,1,0:T(8,128)(2,1)S(1)}, u32[]{:S(2)}, u32[]{:S(2)}) async-start(bf16[16,64,256]{2,1,0:T(8,128)(2,1)} %bitcast.17), calls=%async_computation.1 | async-start | bytes 1048576 | tf_op jit(solution)/shard_map/all_to_all | solution.py:432
  104.4 18.8 %copy-start.3 = (bf16[3,128,640]{2,1,0:T(8,128)(2,1)}, bf16[3,128,640]{2,1,0:T(8,128)(2,1)S(1)}, u32[]{:S(2)}) copy-start(bf16[3,128,640]{2,1,0:T(8,128)(2,1)S(1)} %collective-permute-done.10.back_ref) | copy-start | bytes 1474564
  104.4 7.0 %collective-permute-start.11 = (bf16[1,128,640]{2,1,0:T(8,128)(2,1)S(1)}, bf16[1,128,640]{2,1,0:T(8,128)(2,1)S(1)}, u32[]{:S(2)}, u32[]{:S(2)}) collective-permute-start(bf16[1,128,640]{2,1,0:T(8,128)(2,1)S(1)} %slice.8), channel_id=1, source_target_pairs={{0,12},{4,0},{8,4},{12,8},{1,13},{5,1},{9,5},{13,9},{2,14},{6,2},{... | collective-permute-start | bytes 491528 | tf_op jit(solution)/shard_map/ppermute | solution.py:440
  108.0 15.1 %copy-start.4 = (bf16[3,128,640]{2,1,0:T(8,128)(2,1)}, bf16[3,128,640]{2,1,0:T(8,128)(2,1)S(1)}, u32[]{:S(2)}) copy-start(bf16[3,128,640]{2,1,0:T(8,128)(2,1)S(1)} %collective-permute-done.12.ahead_ref) | copy-start | bytes 1474564
  108.1 6.8 %collective-permute-start.13 = (bf16[1,128,640]{2,1,0:T(8,128)(2,1)S(1)}, bf16[1,128,640]{2,1,0:T(8,128)(2,1)S(1)}, u32[]{:S(2)}, u32[]{:S(2)}) collective-permute-start(bf16[1,128,640]{2,1,0:T(8,128)(2,1)S(1)} %slice.9), channel_id=1, source_target_pairs={{0,4},{4,8},{8,12},{12,0},{1,5},{5,9},{9,13},{13,1},{2,6},{6,10},{... | collective-permute-start | bytes 491528 | tf_op jit(solution)/shard_map/ppermute | solution.py:440
  111.4 11.8 %copy-start.10 = (bf16[1,128,640]{2,1,0:T(8,128)(2,1)}, bf16[1,128,640]{2,1,0:T(8,128)(2,1)S(1)}, u32[]{:S(2)}) copy-start(bf16[1,128,640]{2,1,0:T(8,128)(2,1)S(1)} %collective-permute-done.11.dq_ref) | copy-start | bytes 491524
  114.9 8.3 %copy-start.11 = (bf16[1,128,640]{2,1,0:T(8,128)(2,1)}, bf16[1,128,640]{2,1,0:T(8,128)(2,1)S(1)}, u32[]{:S(2)}) copy-start(bf16[1,128,640]{2,1,0:T(8,128)(2,1)S(1)} %collective-permute-done.13.out_ref) | copy-start | bytes 491524
  116.4 1.9 %collective-permute-start.14 = (bf16[8,2,4,16,256]{4,3,2,1,0:T(8,128)(2,1)S(1)}, bf16[8,2,4,16,256]{4,3,2,1,0:T(8,128)(2,1)S(1)}, u32[]{:S(2)}, u32[]{:S(2)}) collective-permute-start(bf16[8,2,4,16,256]{4,3,2,1,0:T(8,128)(2,1)S(1)} %bitcast.13), channel_id=1, source_target_pairs={{0,1},{1,0},{2,3},{3,2},{4,5},{5,4},{6,7},{7,6},{8,9},{9,8},{10,11... | collective-permute-start | bytes 1572872 | tf_op jit(solution)/shard_map/ppermute | solution.py:472
  118.3 2.5 %copy-start = (bf16[16,1280,128]{2,1,0:T(8,128)(2,1)S(1)}, bf16[16,1280,128]{2,1,0:T(8,128)(2,1)}, u32[]{:S(2)}) copy-start(bf16[16,1280,128]{2,1,0:T(8,128)(2,1)} %all-gather.3.cloned.1.call-done) | copy-start | bytes 15728644
  123.2 20.2 %all-to-all-start.2 = ((bf16[32,80,128]{2,1,0:T(8,128)(2,1)}), bf16[32,80,128]{2,1,0:T(8,128)(2,1)S(1)}, u32[]{:S(2)}, u32[]{:S(2)}) async-start(bf16[32,80,128]{2,1,0:T(8,128)(2,1)} %weight_grad.1), calls=%async_computation.2 | async-start | bytes 1310720 | tf_op jit(solution)/shard_map/all_to_all | solution.py:432
  (4 other events, 4.9 us)
Sparse Core Ops, SparseCore 0:
  32.7 74.4 all-gather.2
